TPU v7x, 32 devices: a whole 2x2x4 slice. The times are simulated.
32 devices in a mesh: seq: 8 (over z, core), head: 4 (over y, x).
Axes of the slice: x: 2, y: 2, z: 4, core: 2. Of those that a mesh axis runs over, the one named last changes fastest.
Arguments:
- queries: bfloat16 [1024, 4096], P(('seq', 'head')), as said below
- keys: bfloat16 [1024, 4096], P('seq', 'head'), as said below
- values: bfloat16 [1024, 4096], P('seq', 'head'), may hold values from -6 to 6
- block_order: int32 [8], replicated, may hold values from 0 to 7, each once
Outputs:
- attended: bfloat16 [1024, 4096], P('seq', 'head')
Inputs may be any that keep to these rules, and one draw needn't show every extreme that they name: `block_order`: each storage block holds a different sequence block. `queries`: entries lie within -8 to 8. `keys`: entries lie within -8 to 8.
All inputs are finite; a program needn't handle non-finite values.
Results may differ from a plain program's by a relative error of at most 0.006.
Values may be sent and summed in bfloat16 or wider, within the bound.
No kernel may reach another device: no remote copies, remote signals or barrier semaphores. Data moves between devices by JAX's collectives and lax.ppermute only.
A program may use at most 64 MiB of HBM per device.

v0:
```python
import jax
import jax.numpy as jnp
from jax import lax
from jax.sharding import PartitionSpec as P

HEAD_DIM = 128


def shortened(shard):

    def short(part):
        return part.astype(jnp.bfloat16) if part.dtype == jnp.float32 else part

    return jax.tree.map(short, shard)


def shifted(block, axis, distance):
    devices = range(lax.axis_size(axis))
    route = [((i - distance) % len(devices), i) for i in devices]
    return lax.ppermute(block, axis, route)


def body(queries, keys, values, block_order):
    seq_count = lax.axis_size("seq")
    me_index = lax.axis_index("seq")
    local_q = lax.all_to_all(queries, "head", split_axis=1, concat_axis=0, tiled=True)
    rows = local_q.shape[0]
    head_count = local_q.shape[1] // HEAD_DIM
    q_three = local_q.reshape(rows, head_count, HEAD_DIM)
    mine = block_order[me_index]
    scale = 1.0 / HEAD_DIM**0.5

    def tile(state, kv_pair, allowed):
        rowmax, total, accum = state
        key_count = kv_pair[0].shape[0]
        k_three = kv_pair[0].reshape(key_count, head_count, HEAD_DIM)
        v_three = kv_pair[1].reshape(key_count, head_count, HEAD_DIM)
        scores = (
            jnp.einsum("qhd,khd->hqk", q_three, k_three, preferred_element_type=jnp.float32) * scale
        )
        scores = jnp.where(allowed[None], scores, jnp.float32(-1e30))
        new_max = jnp.maximum(rowmax, jnp.max(scores, axis=2))
        factor = jnp.exp(rowmax - new_max)
        weight = jnp.where(allowed[None], jnp.exp(scores - new_max[:, :, None]), jnp.float32(0.0))
        total = total * factor + jnp.sum(weight, axis=2)
        mixed = jnp.einsum(
            "hqk,khd->qhd", weight.astype(jnp.bfloat16), v_three, preferred_element_type=jnp.float32
        )
        accum = accum * jnp.transpose(factor)[:, :, None] + mixed
        return (new_max, total, accum)

    def absorb(state, kv_pair, source):
        visible = block_order[source % seq_count] < mine
        allowed = jnp.broadcast_to(visible, (rows, rows))
        return tile(state, kv_pair, allowed)

    start_state = (
        jnp.full((head_count, rows), -1e30, jnp.float32),
        jnp.zeros((head_count, rows), jnp.float32),
        jnp.zeros((rows, head_count, HEAD_DIM), jnp.float32),
    )
    query_idx = lax.broadcasted_iota(jnp.int32, (rows, rows), 0)
    key_idx = lax.broadcasted_iota(jnp.int32, (rows, rows), 1)
    state = tile(start_state, (keys, values), key_idx <= query_idx)

    def forward(kv_pair):
        return jax.tree.map(
            lambda part, own: part.astype(own.dtype), shifted(shortened(kv_pair), "seq", 1), kv_pair
        )

    def backward(kv_pair):
        return jax.tree.map(
            lambda part, own: part.astype(own.dtype),
            shifted(shortened(kv_pair), "seq", -1),
            kv_pair,
        )

    def both_turn(step, carry):
        ahead, behind, st = carry
        ahead = forward(ahead)
        st = absorb(st, ahead, me_index - step + seq_count)
        behind = backward(behind)
        st = absorb(st, behind, me_index + step)
        return (ahead, behind, st)

    ahead, behind, state = lax.fori_loop(
        1, (seq_count - 1) // 2 + 1, both_turn, ((keys, values), (keys, values), state)
    )
    ahead = forward(ahead)
    state = absorb(state, ahead, me_index - seq_count // 2 + seq_count)
    rowmax, total, accum = state
    result = accum / jnp.transpose(total)[:, :, None]
    return result.reshape(rows, head_count * HEAD_DIM).astype(jnp.bfloat16)


def solution(mesh):
    in_specs = (P(("seq", "head"), None), P("seq", "head"), P("seq", "head"), P())
    out_specs = P("seq", "head")
    return jax.shard_map(body, mesh=mesh, in_specs=in_specs, out_specs=out_specs, check_vma=False)
```

profile of v0, /device:TPU:0, one launch (start us, length us, event | category | flops | bytes accessed | tf_op | source)
XLA Modules:
  0.0 71.1 jit_solution(11742582745219514329)
XLA Ops:
  0.0 1.7 %copy.73 = bf16[4,4,8,1024]{3,2,0,1:T(8,128)(2,1)} copy(bf16[4,4,8,1024]{3,2,1,0:T(8,128)(2,1)} %bitcast.117) | data formatting | bytes 524288 | tf_op jit(solution)/shard_map/all_to_all | solution.py:26
  1.7 5.3 %all-to-all-start = ((bf16[32,4,1024]{2,0,1:T(8,128)(2,1)}), bf16[32,4,1024]{2,0,1:T(8,128)(2,1)S(1)}, u32[]{:S(2)}, u32[]{:S(2)}) async-start(bf16[32,4,1024]{2,0,1:T(8,128)(2,1)} %bitcast.76), calls=%async_computation | async-start | bytes 524288 | tf_op jit(solution)/shard_map/all_to_all | solution.py:26
  7.2 0.9 %copy-done = bf16[128,1024]{1,0:T(8,128)(2,1)S(1)} copy-done((bf16[128,1024]{1,0:T(8,128)(2,1)S(1)}, bf16[128,1024]{1,0:T(8,128)(2,1)}, u32[]{:S(2)}) %copy-start) | copy-done | bytes 262168
  8.3 0.6 copy-done.2
  9.0 0.7 fusion.54
  9.6 2.7 %all-to-all-done = bf16[32,4,1024]{2,0,1:T(8,128)(2,1)S(1)} async-done(((bf16[32,4,1024]{2,0,1:T(8,128)(2,1)}), bf16[32,4,1024]{2,0,1:T(8,128)(2,1)S(1)}, u32[]{:S(2)}, u32[]{:S(2)}) %all-to-all-start) | async-done | bytes 262176 | tf_op jit(solution)/shard_map/all_to_all | solution.py:26
  13.2 46.3 %while.27 = (s32[]{:T(128)}, bf16[128,1024]{0,1:T(8,128)(2,1)S(1)}, bf16[128,1024]{0,1:T(8,128)(2,1)S(1)}, bf16[128,1024]{0,1:T(8,128)(2,1)S(1)}, bf16[128,1024]...) while((s32[]{:T(128)}, bf16[128,1024]{0,1:T(8,128)(2,1)S(1)}, ...), condition=%wide.region_7.8_spmd, body=%wide.region_2.7_spmd.sunk | while | flops 137107488 | bytes 13218471 | solution.py:86
  13.3 3.5 %collective-permute-start.2 = (bf16[128,1024]{0,1:T(8,128)(2,1)S(1)}, bf16[128,1024]{0,1:T(8,128)(2,1)S(1)}, u32[]{:S(2)}, u32[]{:S(2)}) collective-permute-start(bf16[128,1024]{0,1:T(8,128)(2,1)S(1)} %get-tuple-element.469), channel_id=1, source_target_pairs={{4,0},{8,4},{12,8},{16,12},{20,16},{24,20},{28,24},{0,28},{5,1},{9... | collective-permute-start | bytes 786440 | tf_op jit(solution)/shard_map/while/body/eval_jaxpr/ppermute | solution.py:20
  17.3 0.6 fusion.91
  20.3 1.2 %collective-permute-done = bf16[128,1024]{0,1:T(8,128)(2,1)S(1)} collective-permute-done((bf16[128,1024]{0,1:T(8,128)(2,1)S(1)}, bf16[128,1024]{0,1:T(8,128)(2,1)S(1)}, u32[]{:S(2)}, u32[]{:S(2)}) %collective-permute-start) | collective-permute-done | bytes 262176 | tf_op jit(solution)/shard_map/while/body/eval_jaxpr/ppermute | solution.py:20
  21.9 1.7 %collective-permute-done.2 = bf16[128,1024]{0,1:T(8,128)(2,1)S(1)} collective-permute-done((bf16[128,1024]{0,1:T(8,128)(2,1)S(1)}, bf16[128,1024]{0,1:T(8,128)(2,1)S(1)}, u32[]{:S(2)}, u32[]{:S(2)}) %collective-permute-start.2) | collective-permute-done | bytes 262176 | tf_op jit(solution)/shard_map/while/body/eval_jaxpr/ppermute | solution.py:20
  24.2 2.5 %collective-permute-done.3 = bf16[128,1024]{0,1:T(8,128)(2,1)S(1)} collective-permute-done((bf16[128,1024]{0,1:T(8,128)(2,1)S(1)}, bf16[128,1024]{0,1:T(8,128)(2,1)S(1)}, u32[]{:S(2)}, u32[]{:S(2)}) %collective-permute-start.3) | collective-permute-done | bytes 262176 | tf_op jit(solution)/shard_map/while/body/eval_jaxpr/ppermute | solution.py:20
  27.0 0.6 collective-permute-done.1
  27.5 0.6 fusion.98
  28.2 2.0 %collective-permute-start = (bf16[128,1024]{0,1:T(8,128)(2,1)S(1)}, bf16[128,1024]{0,1:T(8,128)(2,1)S(1)}, u32[]{:S(2)}, u32[]{:S(2)}) collective-permute-start(bf16[128,1024]{0,1:T(8,128)(2,1)S(1)} %get-tuple-element.467), channel_id=1, source_target_pairs={{28,0},{0,4},{4,8},{8,12},{12,16},{16,20},{20,24},{24,28},{29,1},{... | collective-permute-start | bytes 786440 | tf_op jit(solution)/shard_map/while/body/eval_jaxpr/ppermute | solution.py:20
  30.2 1.6 %collective-permute-start.2 = (bf16[128,1024]{0,1:T(8,128)(2,1)S(1)}, bf16[128,1024]{0,1:T(8,128)(2,1)S(1)}, u32[]{:S(2)}, u32[]{:S(2)}) collective-permute-start(bf16[128,1024]{0,1:T(8,128)(2,1)S(1)} %get-tuple-element.469), channel_id=1, source_target_pairs={{4,0},{8,4},{12,8},{16,12},{20,16},{24,20},{28,24},{0,28},{5,1},{9... | collective-permute-start | bytes 786440 | tf_op jit(solution)/shard_map/while/body/eval_jaxpr/ppermute | solution.py:20
  32.4 0.6 fusion.91
  35.4 1.2 %collective-permute-done = bf16[128,1024]{0,1:T(8,128)(2,1)S(1)} collective-permute-done((bf16[128,1024]{0,1:T(8,128)(2,1)S(1)}, bf16[128,1024]{0,1:T(8,128)(2,1)S(1)}, u32[]{:S(2)}, u32[]{:S(2)}) %collective-permute-start) | collective-permute-done | bytes 262176 | tf_op jit(solution)/shard_map/while/body/eval_jaxpr/ppermute | solution.py:20
  36.9 1.7 %collective-permute-done.2 = bf16[128,1024]{0,1:T(8,128)(2,1)S(1)} collective-permute-done((bf16[128,1024]{0,1:T(8,128)(2,1)S(1)}, bf16[128,1024]{0,1:T(8,128)(2,1)S(1)}, u32[]{:S(2)}, u32[]{:S(2)}) %collective-permute-start.2) | collective-permute-done | bytes 262176 | tf_op jit(solution)/shard_map/while/body/eval_jaxpr/ppermute | solution.py:20
  39.2 2.7 %collective-permute-done.3 = bf16[128,1024]{0,1:T(8,128)(2,1)S(1)} collective-permute-done((bf16[128,1024]{0,1:T(8,128)(2,1)S(1)}, bf16[128,1024]{0,1:T(8,128)(2,1)S(1)}, u32[]{:S(2)}, u32[]{:S(2)}) %collective-permute-start.3) | collective-permute-done | bytes 262176 | tf_op jit(solution)/shard_map/while/body/eval_jaxpr/ppermute | solution.py:20
  42.6 0.6 fusion.98
  43.3 2.0 %collective-permute-start = (bf16[128,1024]{0,1:T(8,128)(2,1)S(1)}, bf16[128,1024]{0,1:T(8,128)(2,1)S(1)}, u32[]{:S(2)}, u32[]{:S(2)}) collective-permute-start(bf16[128,1024]{0,1:T(8,128)(2,1)S(1)} %get-tuple-element.467), channel_id=1, source_target_pairs={{28,0},{0,4},{4,8},{8,12},{12,16},{16,20},{20,24},{24,28},{29,1},{... | collective-permute-start | bytes 786440 | tf_op jit(solution)/shard_map/while/body/eval_jaxpr/ppermute | solution.py:20
  45.3 1.6 %collective-permute-start.2 = (bf16[128,1024]{0,1:T(8,128)(2,1)S(1)}, bf16[128,1024]{0,1:T(8,128)(2,1)S(1)}, u32[]{:S(2)}, u32[]{:S(2)}) collective-permute-start(bf16[128,1024]{0,1:T(8,128)(2,1)S(1)} %get-tuple-element.469), channel_id=1, source_target_pairs={{4,0},{8,4},{12,8},{16,12},{20,16},{24,20},{28,24},{0,28},{5,1},{9... | collective-permute-start | bytes 786440 | tf_op jit(solution)/shard_map/while/body/eval_jaxpr/ppermute | solution.py:20
  47.4 0.6 fusion.91
  50.4 2.9 %collective-permute-done = bf16[128,1024]{0,1:T(8,128)(2,1)S(1)} collective-permute-done((bf16[128,1024]{0,1:T(8,128)(2,1)S(1)}, bf16[128,1024]{0,1:T(8,128)(2,1)S(1)}, u32[]{:S(2)}, u32[]{:S(2)}) %collective-permute-start) | collective-permute-done | bytes 262176 | tf_op jit(solution)/shard_map/while/body/eval_jaxpr/ppermute | solution.py:20
  54.2 2.7 %collective-permute-done.3 = bf16[128,1024]{0,1:T(8,128)(2,1)S(1)} collective-permute-done((bf16[128,1024]{0,1:T(8,128)(2,1)S(1)}, bf16[128,1024]{0,1:T(8,128)(2,1)S(1)}, u32[]{:S(2)}, u32[]{:S(2)}) %collective-permute-start.3) | collective-permute-done | bytes 262176 | tf_op jit(solution)/shard_map/while/body/eval_jaxpr/ppermute | solution.py:20
  57.2 1.6 %collective-permute-done.1 = bf16[128,1024]{0,1:T(8,128)(2,1)S(1)} collective-permute-done((bf16[128,1024]{0,1:T(8,128)(2,1)S(1)}, bf16[128,1024]{0,1:T(8,128)(2,1)S(1)}, u32[]{:S(2)}, u32[]{:S(2)}) %collective-permute-start.1) | collective-permute-done | bytes 262176 | tf_op jit(solution)/shard_map/while/body/eval_jaxpr/ppermute | solution.py:20
  58.9 0.6 fusion.98
  59.6 0.7 collective-permute-start.4
  61.8 5.4 %collective-permute-done.4 = bf16[128,1024]{0,1:T(8,128)(2,1)S(1)} collective-permute-done((bf16[128,1024]{0,1:T(8,128)(2,1)S(1)}, bf16[128,1024]{0,1:T(8,128)(2,1)S(1)}, u32[]{:S(2)}, u32[]{:S(2)}) %collective-permute-start.4) | collective-permute-done | bytes 262176 | tf_op jit(solution)/shard_map/ppermute | solution.py:20
  67.7 2.3 %collective-permute-done.5 = bf16[128,1024]{0,1:T(8,128)(2,1)S(1)} collective-permute-done((bf16[128,1024]{0,1:T(8,128)(2,1)S(1)}, bf16[128,1024]{0,1:T(8,128)(2,1)S(1)}, u32[]{:S(2)}, u32[]{:S(2)}) %collective-permute-start.5) | collective-permute-done | bytes 262176 | tf_op jit(solution)/shard_map/ppermute | solution.py:20
  70.3 0.9 %copy.40 = bf16[128,1024]{1,0:T(8,128)(2,1)} copy(bf16[128,1024]{0,1:T(8,128)(2,1)S(1)} %bitcast.118) | data formatting | bytes 524288 | tf_op jit(solution)/shard_map/convert_element_type | solution.py:93
  (71 shorter events, 8.2 us)
Async XLA Ops:
  1.7 5.3 %copy-start.1 = (bf16[128,1024]{1,0:T(8,128)(2,1)S(1)}, bf16[128,1024]{1,0:T(8,128)(2,1)}, u32[]{:S(2)}) copy-start(bf16[128,1024]{1,0:T(8,128)(2,1)} %param.7) | copy-start | bytes 786436
  1.7 10.7 %all-to-all-start = ((bf16[32,4,1024]{2,0,1:T(8,128)(2,1)}), bf16[32,4,1024]{2,0,1:T(8,128)(2,1)S(1)}, u32[]{:S(2)}, u32[]{:S(2)}) async-start(bf16[32,4,1024]{2,0,1:T(8,128)(2,1)} %bitcast.76), calls=%async_computation | async-start | bytes 524288 | tf_op jit(solution)/shard_map/all_to_all | solution.py:26
  7.1 1.0 %copy-start = (bf16[128,1024]{1,0:T(8,128)(2,1)S(1)}, bf16[128,1024]{1,0:T(8,128)(2,1)}, u32[]{:S(2)}) copy-start(bf16[128,1024]{1,0:T(8,128)(2,1)} %param.8) | copy-start | bytes 786436
  8.3 0.7 copy-start.2
  13.2 8.3 %collective-permute-start = (bf16[128,1024]{0,1:T(8,128)(2,1)S(1)}, bf16[128,1024]{0,1:T(8,128)(2,1)S(1)}, u32[]{:S(2)}, u32[]{:S(2)}) collective-permute-start(bf16[128,1024]{0,1:T(8,128)(2,1)S(1)} %get-tuple-element.467), channel_id=1, source_target_pairs={{28,0},{0,4},{4,8},{8,12},{12,16},{16,20},{20,24},{24,28},{29,1},{... | collective-permute-start | bytes 786440 | tf_op jit(solution)/shard_map/while/body/eval_jaxpr/ppermute | solution.py:20
  13.3 10.3 %collective-permute-start.2 = (bf16[128,1024]{0,1:T(8,128)(2,1)S(1)}, bf16[128,1024]{0,1:T(8,128)(2,1)S(1)}, u32[]{:S(2)}, u32[]{:S(2)}) collective-permute-start(bf16[128,1024]{0,1:T(8,128)(2,1)S(1)} %get-tuple-element.469), channel_id=1, source_target_pairs={{4,0},{8,4},{12,8},{16,12},{20,16},{24,20},{28,24},{0,28},{5,1},{9... | collective-permute-start | bytes 786440 | tf_op jit(solution)/shard_map/while/body/eval_jaxpr/ppermute | solution.py:20
  16.8 9.8 %collective-permute-start.3 = (bf16[128,1024]{0,1:T(8,128)(2,1)S(1)}, bf16[128,1024]{0,1:T(8,128)(2,1)S(1)}, u32[]{:S(2)}, u32[]{:S(2)}) collective-permute-start(bf16[128,1024]{0,1:T(8,128)(2,1)S(1)} %get-tuple-element.470), channel_id=1, source_target_pairs={{4,0},{8,4},{12,8},{16,12},{20,16},{24,20},{28,24},{0,28},{5,1},{9... | collective-permute-start | bytes 786440 | tf_op jit(solution)/shard_map/while/body/eval_jaxpr/ppermute | solution.py:20
  17.1 10.5 %collective-permute-start.1 = (bf16[128,1024]{0,1:T(8,128)(2,1)S(1)}, bf16[128,1024]{0,1:T(8,128)(2,1)S(1)}, u32[]{:S(2)}, u32[]{:S(2)}) collective-permute-start(bf16[128,1024]{0,1:T(8,128)(2,1)S(1)} %get-tuple-element.468), channel_id=1, source_target_pairs={{28,0},{0,4},{4,8},{8,12},{12,16},{16,20},{20,24},{24,28},{29,1},{... | collective-permute-start | bytes 786440 | tf_op jit(solution)/shard_map/while/body/eval_jaxpr/ppermute | solution.py:20
  28.2 8.3 %collective-permute-start = (bf16[128,1024]{0,1:T(8,128)(2,1)S(1)}, bf16[128,1024]{0,1:T(8,128)(2,1)S(1)}, u32[]{:S(2)}, u32[]{:S(2)}) collective-permute-start(bf16[128,1024]{0,1:T(8,128)(2,1)S(1)} %get-tuple-element.467), channel_id=1, source_target_pairs={{28,0},{0,4},{4,8},{8,12},{12,16},{16,20},{20,24},{24,28},{29,1},{... | collective-permute-start | bytes 786440 | tf_op jit(solution)/shard_map/while/body/eval_jaxpr/ppermute | solution.py:20
  30.2 8.4 %collective-permute-start.2 = (bf16[128,1024]{0,1:T(8,128)(2,1)S(1)}, bf16[128,1024]{0,1:T(8,128)(2,1)S(1)}, u32[]{:S(2)}, u32[]{:S(2)}) collective-permute-start(bf16[128,1024]{0,1:T(8,128)(2,1)S(1)} %get-tuple-element.469), channel_id=1, source_target_pairs={{4,0},{8,4},{12,8},{16,12},{20,16},{24,20},{28,24},{0,28},{5,1},{9... | collective-permute-start | bytes 786440 | tf_op jit(solution)/shard_map/while/body/eval_jaxpr/ppermute | solution.py:20
  31.8 10.0 %collective-permute-start.3 = (bf16[128,1024]{0,1:T(8,128)(2,1)S(1)}, bf16[128,1024]{0,1:T(8,128)(2,1)S(1)}, u32[]{:S(2)}, u32[]{:S(2)}) collective-permute-start(bf16[128,1024]{0,1:T(8,128)(2,1)S(1)} %get-tuple-element.470), channel_id=1, source_target_pairs={{4,0},{8,4},{12,8},{16,12},{20,16},{24,20},{28,24},{0,28},{5,1},{9... | collective-permute-start | bytes 786440 | tf_op jit(solution)/shard_map/while/body/eval_jaxpr/ppermute | solution.py:20
  32.1 10.5 %collective-permute-start.1 = (bf16[128,1024]{0,1:T(8,128)(2,1)S(1)}, bf16[128,1024]{0,1:T(8,128)(2,1)S(1)}, u32[]{:S(2)}, u32[]{:S(2)}) collective-permute-start(bf16[128,1024]{0,1:T(8,128)(2,1)S(1)} %get-tuple-element.468), channel_id=1, source_target_pairs={{28,0},{0,4},{4,8},{8,12},{12,16},{16,20},{20,24},{24,28},{29,1},{... | collective-permute-start | bytes 786440 | tf_op jit(solution)/shard_map/while/body/eval_jaxpr/ppermute | solution.py:20
  43.3 10.0 %collective-permute-start = (bf16[128,1024]{0,1:T(8,128)(2,1)S(1)}, bf16[128,1024]{0,1:T(8,128)(2,1)S(1)}, u32[]{:S(2)}, u32[]{:S(2)}) collective-permute-start(bf16[128,1024]{0,1:T(8,128)(2,1)S(1)} %get-tuple-element.467), channel_id=1, source_target_pairs={{28,0},{0,4},{4,8},{8,12},{12,16},{16,20},{20,24},{24,28},{29,1},{... | collective-permute-start | bytes 786440 | tf_op jit(solution)/shard_map/while/body/eval_jaxpr/ppermute | solution.py:20
  45.3 8.4 %collective-permute-start.2 = (bf16[128,1024]{0,1:T(8,128)(2,1)S(1)}, bf16[128,1024]{0,1:T(8,128)(2,1)S(1)}, u32[]{:S(2)}, u32[]{:S(2)}) collective-permute-start(bf16[128,1024]{0,1:T(8,128)(2,1)S(1)} %get-tuple-element.469), channel_id=1, source_target_pairs={{4,0},{8,4},{12,8},{16,12},{20,16},{24,20},{28,24},{0,28},{5,1},{9... | collective-permute-start | bytes 786440 | tf_op jit(solution)/shard_map/while/body/eval_jaxpr/ppermute | solution.py:20
  46.9 10.0 %collective-permute-start.3 = (bf16[128,1024]{0,1:T(8,128)(2,1)S(1)}, bf16[128,1024]{0,1:T(8,128)(2,1)S(1)}, u32[]{:S(2)}, u32[]{:S(2)}) collective-permute-start(bf16[128,1024]{0,1:T(8,128)(2,1)S(1)} %get-tuple-element.470), channel_id=1, source_target_pairs={{4,0},{8,4},{12,8},{16,12},{20,16},{24,20},{28,24},{0,28},{5,1},{9... | collective-permute-start | bytes 786440 | tf_op jit(solution)/shard_map/while/body/eval_jaxpr/ppermute | solution.py:20
  47.2 11.7 %collective-permute-start.1 = (bf16[128,1024]{0,1:T(8,128)(2,1)S(1)}, bf16[128,1024]{0,1:T(8,128)(2,1)S(1)}, u32[]{:S(2)}, u32[]{:S(2)}) collective-permute-start(bf16[128,1024]{0,1:T(8,128)(2,1)S(1)} %get-tuple-element.468), channel_id=1, source_target_pairs={{28,0},{0,4},{4,8},{8,12},{12,16},{16,20},{20,24},{24,28},{29,1},{... | collective-permute-start | bytes 786440 | tf_op jit(solution)/shard_map/while/body/eval_jaxpr/ppermute | solution.py:20
  59.6 7.6 %collective-permute-start.4 = (bf16[128,1024]{0,1:T(8,128)(2,1)S(1)}, bf16[128,1024]{0,1:T(8,128)(2,1)S(1)}, u32[]{:S(2)}, u32[]{:S(2)}) collective-permute-start(bf16[128,1024]{0,1:T(8,128)(2,1)S(1)} %get-tuple-element.298), channel_id=1, source_target_pairs={{28,0},{0,4},{4,8},{8,12},{12,16},{16,20},{20,24},{24,28},{29,1},{... | collective-permute-start | bytes 786440 | tf_op jit(solution)/shard_map/ppermute | solution.py:20
  61.7 8.3 %collective-permute-start.5 = (bf16[128,1024]{0,1:T(8,128)(2,1)S(1)}, bf16[128,1024]{0,1:T(8,128)(2,1)S(1)}, u32[]{:S(2)}, u32[]{:S(2)}) collective-permute-start(bf16[128,1024]{0,1:T(8,128)(2,1)S(1)} %get-tuple-element.299), channel_id=1, source_target_pairs={{28,0},{0,4},{4,8},{8,12},{12,16},{16,20},{20,24},{24,28},{29,1},{... | collective-permute-start | bytes 786440 | tf_op jit(solution)/shard_map/ppermute | solution.py:20
where the time goes:
time: 71.5 us; the launch traced here: 71.1 us
  waiting for transfers between devices  29.5 us (41%)
  starting transfers between devices  18.4 us (26%)
  local copies, waits for them, and re-layouts  7.49 us (10%)
  loops' own time  7.41 us (10%)
  matrix products  6 us (8%)
  between operations  1.4 us (2%)
  other arithmetic  0.98 us (1%)
    ppermute x14, waiting for transfers between devices, shifted(): return lax.ppermute(block, axis, route)  26.8 us
    ppermute x14, starting transfers between devices, shifted(): return lax.ppermute(block, axis, route)  13.1 us
    another operation x1, loops' own time, body(): lax.fori_loop(1, (seq_count - 1) // 2 + 1, both_turn, ((keys, values), (k...  7.41 us
    all_to_all x1, starting transfers between devices, body(): lax.all_to_all(queries, 'head', split_axis=1, concat_axis=0, tiled=True)  5.29 us
    dot_general x8, matrix products, tile(): jnp.einsum('hqk,khd->qhd', weight.astype(jnp.bfloat16), v_three, preferre...  3.3 us
    dot_general x8, matrix products, tile(): jnp.einsum('qhd,khd->hqk', q_three, k_three, preferred_element_type=jnp.f...  2.7 us
    all_to_all x1, waiting for transfers between devices, body(): lax.all_to_all(queries, 'head', split_axis=1, concat_axis=0, tiled=True)  2.69 us
    dynamic_slice x4, local copies, waits for them, and re-layouts, absorb(): visible = block_order[source % seq_count] < mine  2.51 us
  transfers between devices with their start and end apart: 15, of which 14 were waited for; matrix products, arithmetic and copies ran while one was open for 10% of the time, Pallas kernels for 0%

commit v1 on v0

--- a/solution.py
+++ b/solution.py
@@ -1,17 +1,20 @@
+import functools
+
 import jax
 import jax.numpy as jnp
 from jax import lax
+from jax.experimental import pallas as pl
+from jax.experimental.pallas import tpu as pltpu
 from jax.sharding import PartitionSpec as P
 
 HEAD_DIM = 128
-
-
-def shortened(shard):
-
-    def short(part):
-        return part.astype(jnp.bfloat16) if part.dtype == jnp.float32 else part
-
-    return jax.tree.map(short, shard)
+CORES = 2
+LOG2E = 1.4426950408889634
+ANY = pl.BlockSpec(memory_space=pl.ANY)
+HBM = pl.BlockSpec(memory_space=pltpu.HBM)
+VMEM = pl.BlockSpec(memory_space=pltpu.VMEM)
+SMEM = pl.BlockSpec(memory_space=pltpu.SMEM)
+PARAMS = pltpu.CompilerParams(vmem_limit_bytes=16 * 2**20)
 
 
 def shifted(block, axis, distance):
@@ -20,7 +23,182 @@
     return lax.ppermute(block, axis, route)
 
 
-def body(queries, keys, values, block_order):
+def swapped(block, axis, bits):
+    route = [(i, i ^ bits) for i in range(lax.axis_size(axis))]
+    return lax.ppermute(block, axis, route)
+
+
+def place():
+    me = lax.axis_index("seq")
+    return me // CORES, me % CORES, lax.axis_index("head")
+
+
+def cut(start, size):
+    return pl.ds(pl.multiple_of(start * size, size), size)
+
+
+def split_kernel(chips, q_ref, k_ref, v_ref, *rest):
+    kv_refs, q_refs, sem = rest[:chips], rest[chips:-1], rest[-1]
+    z, _, head = place()
+    width = k_ref.shape[1] // chips
+    copies = []
+
+    def copy(source, target):
+        copies.append(pltpu.make_async_copy(source, target, sem.at[len(copies)]))
+        copies[-1].start()
+
+    for step in list(range(1, chips)) + [0]:
+        copy(k_ref.at[:, cut(z ^ step, width)], kv_refs[step].at[:, pl.ds(0, width)])
+        copy(v_ref.at[:, cut(z ^ step, width)], kv_refs[step].at[:, pl.ds(width, width)])
+    for turn, target in enumerate(q_refs):
+        copy(q_ref.at[:, cut(head ^ turn, target.shape[1])], target)
+    for one in copies:
+        one.wait()
+
+
+def split(queries, keys, values, chips):
+    rows, width = keys.shape
+    groups = queries.shape[1] // width
+    part = width // chips
+    outs = [jax.ShapeDtypeStruct((rows, 2 * part), keys.dtype)] * chips
+    outs += [jax.ShapeDtypeStruct((queries.shape[0], width), queries.dtype)] * groups
+    outs = pl.pallas_call(
+        functools.partial(split_kernel, chips),
+        out_shape=outs,
+        in_specs=[HBM] * 3,
+        out_specs=[ANY] * len(outs),
+        scratch_shapes=[pltpu.SemaphoreType.DMA((2 * chips + groups,))],
+        compiler_params=PARAMS,
+    )(queries, keys, values)
+    return outs[:chips], outs[chips:]
+
+
+def regroup_kernel(chips, groups, order_ref, *rest):
+    parts, outs, rel_ref, sem = rest[:groups], rest[groups:-2], rest[-2], rest[-1]
+    z, core, head = place()
+    sub, width = parts[0].shape[0], outs[0].shape[1]
+    copies = []
+    for step, out in enumerate(outs):
+        for turn, part in enumerate(parts):
+            copies.append(
+                pltpu.make_async_copy(
+                    part.at[:, cut(z ^ step, width)],
+                    out.at[cut(head ^ turn, sub), :],
+                    sem.at[len(copies)],
+                )
+            )
+            copies[-1].start()
+    rows = rel_ref.shape[2] // (chips * CORES)
+    inner = lax.broadcasted_iota(jnp.int32, (8, rows), 1)
+    for step in range(chips):
+        mine = order_ref[(z ^ step) * CORES + core]
+        for slot in range(chips * CORES):
+            block = (z ^ (slot // CORES)) * CORES + (core ^ (slot % CORES))
+            rel_ref[step, :, pl.ds(slot * rows, rows)] = inner + (order_ref[block] - mine) * rows
+    for one in copies:
+        one.wait()
+
+
+def regroup(block_order, parts, rows, chips):
+    groups, width = len(parts), parts[0].shape[1] // chips
+    outs = [jax.ShapeDtypeStruct((rows, width), parts[0].dtype)] * chips
+    outs += [jax.ShapeDtypeStruct((chips, 8, rows * chips * CORES), jnp.int32)]
+    outs = pl.pallas_call(
+        functools.partial(regroup_kernel, chips, groups),
+        out_shape=outs,
+        in_specs=[SMEM] + [ANY] * groups,
+        out_specs=[ANY] * chips + [VMEM],
+        scratch_shapes=[pltpu.SemaphoreType.DMA((chips * groups,))],
+        compiler_params=PARAMS,
+    )(block_order, *parts)
+    return outs[:chips], outs[chips]
+
+
+def attend_kernel(step, rel_ref, q_ref, *rest):
+    kv_refs, out = rest[:-1], rest[-1]
+    rows, width = out.shape
+    scale = LOG2E / HEAD_DIM**0.5
+    below = lax.broadcasted_iota(jnp.int32, (rows, 2 * rows), 0)
+    for one in range(width // HEAD_DIM):
+        cols = pl.ds(one * HEAD_DIM, HEAD_DIM)
+        scores = []
+        for pair in range(0, len(kv_refs), 2):
+            k = jnp.concatenate([r[:, cols] for r in kv_refs[pair : pair + 2]], 0)
+            s = lax.dot_general(q_ref[:, cols], k, (((1,), (1,)), ((), ())), preferred_element_type=jnp.float32)
+            rel = rel_ref[step, 0:1, pl.ds(pair * rows, 2 * rows)]
+            scores.append(jnp.where(rel <= below, s, jnp.float32(-1e30)))
+        top = jnp.max(functools.reduce(jnp.maximum, scores), axis=1, keepdims=True)
+        total = jnp.zeros((rows, 1), jnp.float32)
+        mixed = jnp.zeros((rows, HEAD_DIM), jnp.float32)
+        cols = pl.ds(width + one * HEAD_DIM, HEAD_DIM)
+        for pair in range(0, len(kv_refs), 2):
+            weight = jnp.exp2((scores[pair // 2] - top) * scale)
+            total += jnp.sum(weight, axis=1, keepdims=True)
+            v = jnp.concatenate([r[:, cols] for r in kv_refs[pair : pair + 2]], 0)
+            mixed += jnp.dot(weight.astype(jnp.bfloat16), v, preferred_element_type=jnp.float32)
+        out[:, pl.ds(one * HEAD_DIM, HEAD_DIM)] = (mixed / total).astype(out.dtype)
+
+
+def attend(step, rel, q, kv):
+    return pl.pallas_call(
+        functools.partial(attend_kernel, step),
+        out_shape=jax.ShapeDtypeStruct(q.shape, q.dtype),
+        in_specs=[VMEM] * (2 + len(kv)),
+        out_specs=VMEM,
+        compiler_params=PARAMS,
+    )(rel, q, *kv)
+
+
+def join_kernel(chips, *refs):
+    parts, out, sem = refs[:chips], refs[chips], refs[-1]
+    z, _, _ = place()
+    width = parts[0].shape[1]
+    copies = []
+    for step in range(chips):
+        copies.append(
+            pltpu.make_async_copy(parts[step], out.at[:, cut(z ^ step, width)], sem.at[step])
+        )
+        copies[-1].start()
+    for one in copies:
+        one.wait()
+
+
+def join(parts):
+    chips = len(parts)
+    rows, width = parts[0].shape
+    return pl.pallas_call(
+        functools.partial(join_kernel, chips),
+        out_shape=jax.ShapeDtypeStruct((rows, width * chips), parts[0].dtype),
+        in_specs=[ANY] * chips,
+        out_specs=ANY,
+        scratch_shapes=[pltpu.SemaphoreType.DMA((chips,))],
+        compiler_params=PARAMS,
+    )(*parts)
+
+
+def by_heads(queries, keys, values, block_order):
+    chips = lax.axis_size("seq") // CORES
+    groups = lax.axis_size("head")
+    rows = keys.shape[0]
+    far_first = sorted(range(1, chips), key=lambda step: step < chips // 2)
+    kv_cut, q_cut = split(queries, keys, values, chips)
+    near, far, q_got, out = {0: kv_cut[0]}, {}, {}, {}
+    for step in far_first:
+        near[step] = swapped(kv_cut[step], "seq", CORES * step)
+    q_parts = [q_cut[0]] + [swapped(q_cut[turn], "head", turn) for turn in range(1, groups)]
+    q_chips, rel = regroup(block_order, q_parts, rows, chips)
+    for step in far_first:
+        q_got[step] = swapped(q_chips[step], "seq", CORES * step)
+    kv = []
+    for step in range(chips):
+        kv += [near[step], swapped(near[step], "seq", 1)]
+    for step in far_first:
+        out[step] = swapped(attend(step, rel, q_got[step], kv), "seq", CORES * step)
+    out[0] = attend(0, rel, q_chips[0], kv)
+    return join([out[step] for step in range(chips)])
+
+
+def around_ring(queries, keys, values, block_order):
     seq_count = lax.axis_size("seq")
     me_index = lax.axis_index("seq")
     local_q = lax.all_to_all(queries, "head", split_axis=1, concat_axis=0, tiled=True)
@@ -63,34 +241,33 @@
     key_idx = lax.broadcasted_iota(jnp.int32, (rows, rows), 1)
     state = tile(start_state, (keys, values), key_idx <= query_idx)
 
-    def forward(kv_pair):
-        return jax.tree.map(
-            lambda part, own: part.astype(own.dtype), shifted(shortened(kv_pair), "seq", 1), kv_pair
-        )
-
-    def backward(kv_pair):
-        return jax.tree.map(
-            lambda part, own: part.astype(own.dtype),
-            shifted(shortened(kv_pair), "seq", -1),
-            kv_pair,
-        )
-
     def both_turn(step, carry):
         ahead, behind, st = carry
-        ahead = forward(ahead)
+        ahead = tuple(shifted(part, "seq", 1) for part in ahead)
         st = absorb(st, ahead, me_index - step + seq_count)
-        behind = backward(behind)
+        behind = tuple(shifted(part, "seq", -1) for part in behind)
         st = absorb(st, behind, me_index + step)
         return (ahead, behind, st)
 
     ahead, behind, state = lax.fori_loop(
         1, (seq_count - 1) // 2 + 1, both_turn, ((keys, values), (keys, values), state)
     )
-    ahead = forward(ahead)
-    state = absorb(state, ahead, me_index - seq_count // 2 + seq_count)
+    if seq_count % 2 == 0:
+        ahead = tuple(shifted(part, "seq", 1) for part in ahead)
+        state = absorb(state, ahead, me_index - seq_count // 2 + seq_count)
     rowmax, total, accum = state
     result = accum / jnp.transpose(total)[:, :, None]
     return result.reshape(rows, head_count * HEAD_DIM).astype(jnp.bfloat16)
+
+
+def body(queries, keys, values, block_order):
+    seq_count, groups = lax.axis_size("seq"), lax.axis_size("head")
+    chips = seq_count // CORES
+    heads = keys.shape[1] // HEAD_DIM
+    powers = all(n > 1 and n & (n - 1) == 0 for n in (chips, groups))
+    if seq_count % CORES == 0 and powers and heads % chips == 0:
+        return by_heads(queries, keys, values, block_order)
+    return around_ring(queries, keys, values, block_order)
 
 
 def solution(mesh):

time: 71.5 us -> 42.8 us (0.60)
  waiting for transfers between devices: 29.5 us -> 16.4 us
  loops' own time: 7.41 us -> 0 us
  matrix products: 6 us -> 0 us
  Pallas kernels: 0 us -> 5.44 us
  local copies, waits for them, and re-layouts: 7.49 us -> 2.85 us
  between operations: 1.4 us -> 0.09 us
  other arithmetic: 0.98 us -> 0 us
    ppermute x14 -> x16, waiting for transfers between devices: 26.8 us -> 16.4 us  [swapped(): return lax.ppermute(block, axis, route)]
    another operation x1 -> x0, loops' own time: 7.41 us -> none  [body(): lax.fori_loop(1, (seq_count - 1) // 2 + 1, both_turn, ((keys, values), (k...]
    dot_general x16 -> x0, matrix products: 6 us -> none  [the longest x8 3.3 us: tile(): jnp.einsum('hqk,khd->qhd', weight.astype(jnp.bfloat16), v_three, preferre...]
    pallas_call x0 -> x7, Pallas kernels: none -> 5.44 us  [the longest x4 3.56 us: attend(): pl.pallas_call(functools.partial(attend_kernel, step), out_shape=jax.Shap...]
    all_to_all x1 -> x0, starting transfers between devices: 5.29 us -> none  [body(): lax.all_to_all(queries, 'head', split_axis=1, concat_axis=0, tiled=True)]
    ppermute x14 -> x16, starting transfers between devices: 13.1 us -> 17.8 us  [swapped(): return lax.ppermute(block, axis, route)]
    all_to_all x1 -> x0, waiting for transfers between devices: 2.69 us -> none  [body(): lax.all_to_all(queries, 'head', split_axis=1, concat_axis=0, tiled=True)]
    dynamic_slice x4 -> x0, local copies, waits for them, and re-layouts: 2.51 us -> none  [absorb(): visible = block_order[source % seq_count] < mine]
  transfers between devices with their start and end apart: 15 -> 16, of which waited for: 14 -> 7; matrix products, arithmetic and copies ran while one was open for 10% -> 0% of each run, Pallas kernels for 0% -> 10%
where the time goes in v1:
time: 42.8 us; the launch traced here: 42.6 us
  starting transfers between devices  17.8 us (42%)
  waiting for transfers between devices  16.4 us (38%)
  Pallas kernels  5.44 us (13%)
  local copies, waits for them, and re-layouts  2.85 us (7%)
    ppermute x16, starting transfers between devices, swapped(): return lax.ppermute(block, axis, route)  17.8 us
    ppermute x16, waiting for transfers between devices, swapped(): return lax.ppermute(block, axis, route)  16.4 us
    pallas_call x4, Pallas kernels, attend(): pl.pallas_call(functools.partial(attend_kernel, step), out_shape=jax.Shap...  3.56 us
    unnamed x8, local copies, waits for them, and re-layouts  2.85 us
  transfers between devices with their start and end apart: 16, of which 7 were waited for; matrix products, arithmetic and copies ran while one was open for 0% of the time, Pallas kernels for 10%

profile of v1, /device:TPU:0, one launch (start us, length us, event | category | flops | bytes accessed | tf_op | source)
XLA Modules:
  0.0 42.6 jit_solution(3069763910533973668)
XLA Ops:
  0.0 0.9 %copy-done = bf16[32,4096]{1,0:T(8,128)(2,1)S(1)} copy-done((bf16[32,4096]{1,0:T(8,128)(2,1)S(1)}, bf16[32,4096]{1,0:T(8,128)(2,1)}, u32[]{:S(2)}) %copy-start) | copy-done | bytes 262168
  1.0 0.9 %copy-done.1 = bf16[128,1024]{1,0:T(8,128)(2,1)S(1)} copy-done((bf16[128,1024]{1,0:T(8,128)(2,1)S(1)}, bf16[128,1024]{1,0:T(8,128)(2,1)}, u32[]{:S(2)}) %copy-start.1) | copy-done | bytes 262168
  1.9 0.9 %copy-done.2 = bf16[128,1024]{1,0:T(8,128)(2,1)S(1)} copy-done((bf16[128,1024]{1,0:T(8,128)(2,1)S(1)}, bf16[128,1024]{1,0:T(8,128)(2,1)}, u32[]{:S(2)}) %copy-start.2) | copy-done | bytes 262168
  2.9 0.3 shard_map.46
  3.2 3.0 %collective-permute-start = (bf16[32,1024]{1,0:T(8,128)(2,1)S(1)}, bf16[32,1024]{1,0:T(8,128)(2,1)S(1)}, u32[]{:S(2)}, u32[]{:S(2)}) collective-permute-start(bf16[32,1024]{1,0:T(8,128)(2,1)S(1)} %get-tuple-element.19), channel_id=1, source_target_pairs={{0,1},{1,0},{2,3},{3,2},{4,5},{5,4},{6,7},{7,6},{8,9},{9,8},{10,11... | collective-permute-start | bytes 196616 | tf_op jit(solution)/shard_map/ppermute | solution.py:28
  6.2 1.6 %collective-permute-start.4 = (bf16[128,512]{1,0:T(8,128)(2,1)S(1)}, bf16[128,512]{1,0:T(8,128)(2,1)S(1)}, u32[]{:S(2)}, u32[]{:S(2)}) collective-permute-start(bf16[128,512]{1,0:T(8,128)(2,1)S(1)} %get-tuple-element.25), channel_id=1, source_target_pairs={{0,8},{4,12},{8,0},{12,4},{16,24},{20,28},{24,16},{28,20},{1,9},{5... | collective-permute-start | bytes 393224 | tf_op jit(solution)/shard_map/ppermute | solution.py:28
  7.7 2.6 %collective-permute-start.6 = (bf16[128,512]{1,0:T(8,128)(2,1)S(1)}, bf16[128,512]{1,0:T(8,128)(2,1)S(1)}, u32[]{:S(2)}, u32[]{:S(2)}) collective-permute-start(bf16[128,512]{1,0:T(8,128)(2,1)S(1)} %get-tuple-element.26), channel_id=1, source_target_pairs={{0,16},{4,20},{8,24},{12,28},{16,0},{20,4},{24,8},{28,12},{1,17},{... | collective-permute-start | bytes 393224 | tf_op jit(solution)/shard_map/ppermute | solution.py:28
  10.3 0.2 collective-permute-start.8
  10.6 1.5 %collective-permute-start.1 = (bf16[32,1024]{1,0:T(8,128)(2,1)S(1)}, bf16[32,1024]{1,0:T(8,128)(2,1)S(1)}, u32[]{:S(2)}, u32[]{:S(2)}) collective-permute-start(bf16[32,1024]{1,0:T(8,128)(2,1)S(1)} %get-tuple-element.20), channel_id=1, source_target_pairs={{0,2},{1,3},{2,0},{3,1},{4,6},{5,7},{6,4},{7,5},{8,10},{9,11},{10,... | collective-permute-start | bytes 196616 | tf_op jit(solution)/shard_map/ppermute | solution.py:28
  12.1 0.0 collective-permute-done.rest_1_
  12.1 0.3 collective-permute-start.2
  12.3 3.1 %collective-permute-done.1.rest_2_ = bf16[32,1024]{1,0:T(8,128)(2,1)S(1)} collective-permute-done((bf16[32,1024]{1,0:T(8,128)(2,1)S(1)}, bf16[32,1024]{1,0:T(8,128)(2,1)S(1)}, u32[]{:S(2)}, u32[]{:S(2)}) %collective-permute-start.1) | collective-permute-done | bytes 65568 | tf_op jit(solution)/shard_map/ppermute | solution.py:28
  15.5 1.8 %collective-permute-done.2.rest_3_ = bf16[32,1024]{1,0:T(8,128)(2,1)S(1)} collective-permute-done((bf16[32,1024]{1,0:T(8,128)(2,1)S(1)}, bf16[32,1024]{1,0:T(8,128)(2,1)S(1)}, u32[]{:S(2)}, u32[]{:S(2)}) %collective-permute-start.2) | collective-permute-done | bytes 65568 | tf_op jit(solution)/shard_map/ppermute | solution.py:28
  17.2 0.9 %shard_map.47 = (bf16[128,256]{1,0:T(8,128)(2,1)S(1)}, bf16[128,256]{1,0:T(8,128)(2,1)S(1)}, bf16[128,256]{1,0:T(8,128)(2,1)S(1)}, bf16[128,256]{1,0:T(8,128)(2,1)S(1)}, s32[4,8,1024]{2,1,0:T(8,128)S(1)}) custom-call(s32[8]{0:T(128)S(1)} %copy-done.3, bf16[32,1024]{1,0:T(8,128)(2,1)S(1)} %get-tuple-element.18.rest_0_, ...), custom_call_target="tpu_custom_call" | custom-call | tf_op jit(solution)/shard_map/pallas_call | solution.py:106
  18.1 0.1 collective-permute-start.5
  18.2 2.2 %collective-permute-done.6.rest_4_ = bf16[128,512]{1,0:T(8,128)(2,1)S(1)} collective-permute-done((bf16[128,512]{1,0:T(8,128)(2,1)S(1)}, bf16[128,512]{1,0:T(8,128)(2,1)S(1)}, u32[]{:S(2)}, u32[]{:S(2)}) %collective-permute-start.6) | collective-permute-done | bytes 131104 | tf_op jit(solution)/shard_map/ppermute | solution.py:28
  20.4 0.5 %collective-permute-start.9 = (bf16[128,512]{1,0:T(8,128)(2,1)S(1)}, bf16[128,512]{1,0:T(8,128)(2,1)S(1)}, u32[]{:S(2)}, u32[]{:S(2)}) collective-permute-start(bf16[128,512]{1,0:T(8,128)(2,1)S(1)} %collective-permute-done.8.rest_6_), channel_id=1, source_target_pairs={{0,4},{4,0},{8,12},{12,8},{16,20},{20,16},{24,28},{28,24},{1,5},{5... | collective-permute-start | bytes 393224 | tf_op jit(solution)/shard_map/ppermute | solution.py:28
  20.9 1.5 %collective-permute-start.10 = (bf16[128,256]{1,0:T(8,128)(2,1)S(1)}, bf16[128,256]{1,0:T(8,128)(2,1)S(1)}, u32[]{:S(2)}, u32[]{:S(2)}) collective-permute-start(bf16[128,256]{1,0:T(8,128)(2,1)S(1)} %get-tuple-element.28), channel_id=1, source_target_pairs={{0,8},{4,12},{8,0},{12,4},{16,24},{20,28},{24,16},{28,20},{1,9},{5... | collective-permute-start | bytes 196616 | tf_op jit(solution)/shard_map/ppermute | solution.py:28
  22.4 2.8 %collective-permute-done.10.q_ref = bf16[128,256]{1,0:T(8,128)(2,1)S(1)} collective-permute-done((bf16[128,256]{1,0:T(8,128)(2,1)S(1)}, bf16[128,256]{1,0:T(8,128)(2,1)S(1)}, u32[]{:S(2)}, u32[]{:S(2)}) %collective-permute-start.10) | collective-permute-done | bytes 65568 | tf_op jit(solution)/shard_map/ppermute | solution.py:28
  25.2 2.7 %collective-permute-start.12 = (bf16[128,256]{1,0:T(8,128)(2,1)S(1)}, bf16[128,256]{1,0:T(8,128)(2,1)S(1)}, u32[]{:S(2)}, u32[]{:S(2)}) collective-permute-start(bf16[128,256]{1,0:T(8,128)(2,1)S(1)} %get-tuple-element.29), channel_id=1, source_target_pairs={{0,16},{4,20},{8,24},{12,28},{16,0},{20,4},{24,8},{28,12},{1,17},{... | collective-permute-start | bytes 196616 | tf_op jit(solution)/shard_map/ppermute | solution.py:28
  27.9 1.4 %collective-permute-start.14 = (bf16[128,256]{1,0:T(8,128)(2,1)S(1)}, bf16[128,256]{1,0:T(8,128)(2,1)S(1)}, u32[]{:S(2)}, u32[]{:S(2)}) collective-permute-start(bf16[128,256]{1,0:T(8,128)(2,1)S(1)} %get-tuple-element.30), channel_id=1, source_target_pairs={{0,24},{4,28},{8,16},{12,20},{16,8},{20,12},{24,0},{28,4},{1,25},{... | collective-permute-start | bytes 196616 | tf_op jit(solution)/shard_map/ppermute | solution.py:28
  29.2 0.9 %shard_map.49 = bf16[128,256]{1,0:T(8,128)(2,1)S(1)} custom-call(s32[4,8,1024]{2,1,0:T(8,128)S(1)} %get-tuple-element.22.rel_ref, bf16[128,256]{1,0:T(8,128)(2,1)S(1)} %collective-permute-done.10.q_ref, bf16[128,512]{1,0:T(8,128)(2,1)S(1)} %get-tuple-element.24.rest_0_, bf16[128,512]{1,0:T(8,128)(2,1)S(1)} %collective-permute-done.3.rest_1_, ...), custom_call_target="tpu_custom_call" | custom-call | tf_op jit(solution)/shard_map/pallas_call | solution.py:143
  30.1 0.1 collective-permute-start.11
  30.2 2.5 %collective-permute-done.12.q_ref = bf16[128,256]{1,0:T(8,128)(2,1)S(1)} collective-permute-done((bf16[128,256]{1,0:T(8,128)(2,1)S(1)}, bf16[128,256]{1,0:T(8,128)(2,1)S(1)}, u32[]{:S(2)}, u32[]{:S(2)}) %collective-permute-start.12) | collective-permute-done | bytes 65568 | tf_op jit(solution)/shard_map/ppermute | solution.py:28
  32.7 0.9 %shard_map.50 = bf16[128,256]{1,0:T(8,128)(2,1)S(1)} custom-call(s32[4,8,1024]{2,1,0:T(8,128)S(1)} %get-tuple-element.22.rel_ref, bf16[128,256]{1,0:T(8,128)(2,1)S(1)} %collective-permute-done.12.q_ref, bf16[128,512]{1,0:T(8,128)(2,1)S(1)} %get-tuple-element.24.rest_0_, bf16[128,512]{1,0:T(8,128)(2,1)S(1)} %collective-permute-done.3.rest_1_, ...), custom_call_target="tpu_custom_call" | custom-call | tf_op jit(solution)/shard_map/pallas_call | solution.py:143
  33.6 1.1 %collective-permute-start.13 = (bf16[128,256]{1,0:T(8,128)(2,1)S(1)}, bf16[128,256]{1,0:T(8,128)(2,1)S(1)}, u32[]{:S(2)}, u32[]{:S(2)}) collective-permute-start(bf16[128,256]{1,0:T(8,128)(2,1)S(1)} %shard_map.50), channel_id=1, source_target_pairs={{0,16},{4,20},{8,24},{12,28},{16,0},{20,4},{24,8},{28,12},{1,17},{... | collective-permute-start | bytes 196616 | tf_op jit(solution)/shard_map/ppermute | solution.py:28
  34.7 0.9 %shard_map.51 = bf16[128,256]{1,0:T(8,128)(2,1)S(1)} custom-call(s32[4,8,1024]{2,1,0:T(8,128)S(1)} %get-tuple-element.22.rel_ref, bf16[128,256]{1,0:T(8,128)(2,1)S(1)} %collective-permute-done.14.q_ref, bf16[128,512]{1,0:T(8,128)(2,1)S(1)} %get-tuple-element.24.rest_0_, bf16[128,512]{1,0:T(8,128)(2,1)S(1)} %collective-permute-done.3.rest_1_, ...), custom_call_target="tpu_custom_call" | custom-call | tf_op jit(solution)/shard_map/pallas_call | solution.py:143
  35.6 1.4 %collective-permute-start.15 = (bf16[128,256]{1,0:T(8,128)(2,1)S(1)}, bf16[128,256]{1,0:T(8,128)(2,1)S(1)}, u32[]{:S(2)}, u32[]{:S(2)}) collective-permute-start(bf16[128,256]{1,0:T(8,128)(2,1)S(1)} %shard_map.51), channel_id=1, source_target_pairs={{0,24},{4,28},{8,16},{12,20},{16,8},{20,12},{24,0},{28,4},{1,25},{... | collective-permute-start | bytes 196616 | tf_op jit(solution)/shard_map/ppermute | solution.py:28
  37.0 0.9 %shard_map.48.refs_0_ = bf16[128,256]{1,0:T(8,128)(2,1)S(1)} custom-call(s32[4,8,1024]{2,1,0:T(8,128)S(1)} %get-tuple-element.22.rel_ref, bf16[128,256]{1,0:T(8,128)(2,1)S(1)} %get-tuple-element.23.q_ref, bf16[128,512]{1,0:T(8,128)(2,1)S(1)} %get-tuple-element.24.rest_0_, bf16[128,512]{1,0:T(8,128)(2,1)S(1)} %collective-permute-done.3.rest_1_, ...), custom_call_target="tpu_custom_call" | custom-call | tf_op jit(solution)/shard_map/pallas_call | solution.py:143
  37.9 1.8 %collective-permute-done.13.refs_2_ = bf16[128,256]{1,0:T(8,128)(2,1)S(1)} collective-permute-done((bf16[128,256]{1,0:T(8,128)(2,1)S(1)}, bf16[128,256]{1,0:T(8,128)(2,1)S(1)}, u32[]{:S(2)}, u32[]{:S(2)}) %collective-permute-start.13) | collective-permute-done | bytes 65568 | tf_op jit(solution)/shard_map/ppermute | solution.py:28
  39.7 2.2 %collective-permute-done.15.refs_3_ = bf16[128,256]{1,0:T(8,128)(2,1)S(1)} collective-permute-done((bf16[128,256]{1,0:T(8,128)(2,1)S(1)}, bf16[128,256]{1,0:T(8,128)(2,1)S(1)}, u32[]{:S(2)}, u32[]{:S(2)}) %collective-permute-start.15) | collective-permute-done | bytes 65568 | tf_op jit(solution)/shard_map/ppermute | solution.py:28
  41.8 0.7 %shard_map.52 = bf16[128,1024]{1,0:T(8,128)(2,1)} custom-call(bf16[128,256]{1,0:T(8,128)(2,1)S(1)} %shard_map.48.refs_0_, bf16[128,256]{1,0:T(8,128)(2,1)S(1)} %collective-permute-done.11.refs_1_, bf16[128,256]{1,0:T(8,128)(2,1)S(1)} %collective-permute-done.13.refs_2_, bf16[128,256]{1,0:T(8,128)(2,1)S(1)} %collective-permute-done.15.refs_3_), custom_call_target="tpu_custom_call" | custom-call | tf_op jit(solution)/shard_map/pallas_call | solution.py:169
  (15 shorter events, 0.0 us)
Async XLA Ops:
  0.0 0.9 %copy-start = (bf16[32,4096]{1,0:T(8,128)(2,1)S(1)}, bf16[32,4096]{1,0:T(8,128)(2,1)}, u32[]{:S(2)}) copy-start(bf16[32,4096]{1,0:T(8,128)(2,1)} %q_ref.1) | copy-start | bytes 786436
  1.0 0.9 %copy-start.1 = (bf16[128,1024]{1,0:T(8,128)(2,1)S(1)}, bf16[128,1024]{1,0:T(8,128)(2,1)}, u32[]{:S(2)}) copy-start(bf16[128,1024]{1,0:T(8,128)(2,1)} %k_ref.1) | copy-start | bytes 786436
  1.9 0.9 %copy-start.2 = (bf16[128,1024]{1,0:T(8,128)(2,1)S(1)}, bf16[128,1024]{1,0:T(8,128)(2,1)}, u32[]{:S(2)}) copy-start(bf16[128,1024]{1,0:T(8,128)(2,1)} %v_ref.1) | copy-start | bytes 786436
  3.2 8.9 %collective-permute-start = (bf16[32,1024]{1,0:T(8,128)(2,1)S(1)}, bf16[32,1024]{1,0:T(8,128)(2,1)S(1)}, u32[]{:S(2)}, u32[]{:S(2)}) collective-permute-start(bf16[32,1024]{1,0:T(8,128)(2,1)S(1)} %get-tuple-element.19), channel_id=1, source_target_pairs={{0,1},{1,0},{2,3},{3,2},{4,5},{5,4},{6,7},{7,6},{8,9},{9,8},{10,11... | collective-permute-start | bytes 196616 | tf_op jit(solution)/shard_map/ppermute | solution.py:28
  6.2 11.9 %collective-permute-start.4 = (bf16[128,512]{1,0:T(8,128)(2,1)S(1)}, bf16[128,512]{1,0:T(8,128)(2,1)S(1)}, u32[]{:S(2)}, u32[]{:S(2)}) collective-permute-start(bf16[128,512]{1,0:T(8,128)(2,1)S(1)} %get-tuple-element.25), channel_id=1, source_target_pairs={{0,8},{4,12},{8,0},{12,4},{16,24},{20,28},{24,16},{28,20},{1,9},{5... | collective-permute-start | bytes 393224 | tf_op jit(solution)/shard_map/ppermute | solution.py:28
  7.7 12.6 %collective-permute-start.6 = (bf16[128,512]{1,0:T(8,128)(2,1)S(1)}, bf16[128,512]{1,0:T(8,128)(2,1)S(1)}, u32[]{:S(2)}, u32[]{:S(2)}) collective-permute-start(bf16[128,512]{1,0:T(8,128)(2,1)S(1)} %get-tuple-element.26), channel_id=1, source_target_pairs={{0,16},{4,20},{8,24},{12,28},{16,0},{20,4},{24,8},{28,12},{1,17},{... | collective-permute-start | bytes 393224 | tf_op jit(solution)/shard_map/ppermute | solution.py:28
  10.3 10.1 %collective-permute-start.8 = (bf16[128,512]{1,0:T(8,128)(2,1)S(1)}, bf16[128,512]{1,0:T(8,128)(2,1)S(1)}, u32[]{:S(2)}, u32[]{:S(2)}) collective-permute-start(bf16[128,512]{1,0:T(8,128)(2,1)S(1)} %get-tuple-element.27), channel_id=1, source_target_pairs={{0,24},{4,28},{8,16},{12,20},{16,8},{20,12},{24,0},{28,4},{1,25},{... | collective-permute-start | bytes 393224 | tf_op jit(solution)/shard_map/ppermute | solution.py:28
  10.6 4.9 %collective-permute-start.1 = (bf16[32,1024]{1,0:T(8,128)(2,1)S(1)}, bf16[32,1024]{1,0:T(8,128)(2,1)S(1)}, u32[]{:S(2)}, u32[]{:S(2)}) collective-permute-start(bf16[32,1024]{1,0:T(8,128)(2,1)S(1)} %get-tuple-element.20), channel_id=1, source_target_pairs={{0,2},{1,3},{2,0},{3,1},{4,6},{5,7},{6,4},{7,5},{8,10},{9,11},{10,... | collective-permute-start | bytes 196616 | tf_op jit(solution)/shard_map/ppermute | solution.py:28
  12.1 5.2 %collective-permute-start.2 = (bf16[32,1024]{1,0:T(8,128)(2,1)S(1)}, bf16[32,1024]{1,0:T(8,128)(2,1)S(1)}, u32[]{:S(2)}, u32[]{:S(2)}) collective-permute-start(bf16[32,1024]{1,0:T(8,128)(2,1)S(1)} %get-tuple-element.21), channel_id=1, source_target_pairs={{0,3},{1,2},{2,1},{3,0},{4,7},{5,6},{6,5},{7,4},{8,11},{9,10},{10,... | collective-permute-start | bytes 196616 | tf_op jit(solution)/shard_map/ppermute | solution.py:28
  15.5 1.8 %copy-start.3 = (s32[8]{0:T(128)S(1)}, s32[8]{0:T(128)}, u32[]{:S(2)}) copy-start(s32[8]{0:T(128)} %order_ref.1) | copy-start | bytes 100
  15.5 12.4 %collective-permute-start.3 = (bf16[128,512]{1,0:T(8,128)(2,1)S(1)}, bf16[128,512]{1,0:T(8,128)(2,1)S(1)}, u32[]{:S(2)}, u32[]{:S(2)}) collective-permute-start(bf16[128,512]{1,0:T(8,128)(2,1)S(1)} %get-tuple-element.24.rest_0_), channel_id=1, source_target_pairs={{0,4},{4,0},{8,12},{12,8},{16,20},{20,16},{24,28},{28,24},{1,5},{5... | collective-permute-start | bytes 393224 | tf_op jit(solution)/shard_map/ppermute | solution.py:28
  18.1 11.1 %collective-permute-start.5 = (bf16[128,512]{1,0:T(8,128)(2,1)S(1)}, bf16[128,512]{1,0:T(8,128)(2,1)S(1)}, u32[]{:S(2)}, u32[]{:S(2)}) collective-permute-start(bf16[128,512]{1,0:T(8,128)(2,1)S(1)} %collective-permute-done.4.rest_2_), channel_id=1, source_target_pairs={{0,4},{4,0},{8,12},{12,8},{16,20},{20,16},{24,28},{28,24},{1,5},{5... | collective-permute-start | bytes 393224 | tf_op jit(solution)/shard_map/ppermute | solution.py:28
  20.4 8.8 %collective-permute-start.7 = (bf16[128,512]{1,0:T(8,128)(2,1)S(1)}, bf16[128,512]{1,0:T(8,128)(2,1)S(1)}, u32[]{:S(2)}, u32[]{:S(2)}) collective-permute-start(bf16[128,512]{1,0:T(8,128)(2,1)S(1)} %collective-permute-done.6.rest_4_), channel_id=1, source_target_pairs={{0,4},{4,0},{8,12},{12,8},{16,20},{20,16},{24,28},{28,24},{1,5},{5... | collective-permute-start | bytes 393224 | tf_op jit(solution)/shard_map/ppermute | solution.py:28
  20.4 8.8 %collective-permute-start.9 = (bf16[128,512]{1,0:T(8,128)(2,1)S(1)}, bf16[128,512]{1,0:T(8,128)(2,1)S(1)}, u32[]{:S(2)}, u32[]{:S(2)}) collective-permute-start(bf16[128,512]{1,0:T(8,128)(2,1)S(1)} %collective-permute-done.8.rest_6_), channel_id=1, source_target_pairs={{0,4},{4,0},{8,12},{12,8},{16,20},{20,16},{24,28},{28,24},{1,5},{5... | collective-permute-start | bytes 393224 | tf_op jit(solution)/shard_map/ppermute | solution.py:28
  20.9 4.3 %collective-permute-start.10 = (bf16[128,256]{1,0:T(8,128)(2,1)S(1)}, bf16[128,256]{1,0:T(8,128)(2,1)S(1)}, u32[]{:S(2)}, u32[]{:S(2)}) collective-permute-start(bf16[128,256]{1,0:T(8,128)(2,1)S(1)} %get-tuple-element.28), channel_id=1, source_target_pairs={{0,8},{4,12},{8,0},{12,4},{16,24},{20,28},{24,16},{28,20},{1,9},{5... | collective-permute-start | bytes 196616 | tf_op jit(solution)/shard_map/ppermute | solution.py:28
  25.2 7.6 %collective-permute-start.12 = (bf16[128,256]{1,0:T(8,128)(2,1)S(1)}, bf16[128,256]{1,0:T(8,128)(2,1)S(1)}, u32[]{:S(2)}, u32[]{:S(2)}) collective-permute-start(bf16[128,256]{1,0:T(8,128)(2,1)S(1)} %get-tuple-element.29), channel_id=1, source_target_pairs={{0,16},{4,20},{8,24},{12,28},{16,0},{20,4},{24,8},{28,12},{1,17},{... | collective-permute-start | bytes 196616 | tf_op jit(solution)/shard_map/ppermute | solution.py:28
  27.9 6.8 %collective-permute-start.14 = (bf16[128,256]{1,0:T(8,128)(2,1)S(1)}, bf16[128,256]{1,0:T(8,128)(2,1)S(1)}, u32[]{:S(2)}, u32[]{:S(2)}) collective-permute-start(bf16[128,256]{1,0:T(8,128)(2,1)S(1)} %get-tuple-element.30), channel_id=1, source_target_pairs={{0,24},{4,28},{8,16},{12,20},{16,8},{20,12},{24,0},{28,4},{1,25},{... | collective-permute-start | bytes 196616 | tf_op jit(solution)/shard_map/ppermute | solution.py:28
  30.1 7.8 %collective-permute-start.11 = (bf16[128,256]{1,0:T(8,128)(2,1)S(1)}, bf16[128,256]{1,0:T(8,128)(2,1)S(1)}, u32[]{:S(2)}, u32[]{:S(2)}) collective-permute-start(bf16[128,256]{1,0:T(8,128)(2,1)S(1)} %shard_map.49), channel_id=1, source_target_pairs={{0,8},{4,12},{8,0},{12,4},{16,24},{20,28},{24,16},{28,20},{1,9},{5... | collective-permute-start | bytes 196616 | tf_op jit(solution)/shard_map/ppermute | solution.py:28
  33.6 6.0 %collective-permute-start.13 = (bf16[128,256]{1,0:T(8,128)(2,1)S(1)}, bf16[128,256]{1,0:T(8,128)(2,1)S(1)}, u32[]{:S(2)}, u32[]{:S(2)}) collective-permute-start(bf16[128,256]{1,0:T(8,128)(2,1)S(1)} %shard_map.50), channel_id=1, source_target_pairs={{0,16},{4,20},{8,24},{12,28},{16,0},{20,4},{24,8},{28,12},{1,17},{... | collective-permute-start | bytes 196616 | tf_op jit(solution)/shard_map/ppermute | solution.py:28
  35.6 6.2 %collective-permute-start.15 = (bf16[128,256]{1,0:T(8,128)(2,1)S(1)}, bf16[128,256]{1,0:T(8,128)(2,1)S(1)}, u32[]{:S(2)}, u32[]{:S(2)}) collective-permute-start(bf16[128,256]{1,0:T(8,128)(2,1)S(1)} %shard_map.51), channel_id=1, source_target_pairs={{0,24},{4,28},{8,16},{12,20},{16,8},{20,12},{24,0},{28,4},{1,25},{... | collective-permute-start | bytes 196616 | tf_op jit(solution)/shard_map/ppermute | solution.py:28

commit v2 on v0

--- a/solution.py
+++ b/solution.py
@@ -1,17 +1,22 @@
+import functools
+
 import jax
 import jax.numpy as jnp
 from jax import lax
+from jax.experimental import pallas as pl
+from jax.experimental.pallas import tpu as pltpu
 from jax.sharding import PartitionSpec as P
 
 HEAD_DIM = 128
-
-
-def shortened(shard):
-
-    def short(part):
-        return part.astype(jnp.bfloat16) if part.dtype == jnp.float32 else part
-
-    return jax.tree.map(short, shard)
+CORES = 2
+LOG2E = 1.4426950408889634
+ANY = pl.BlockSpec(memory_space=pl.ANY)
+HBM = pl.BlockSpec(memory_space=pltpu.HBM)
+VMEM = pl.BlockSpec(memory_space=pltpu.VMEM)
+SMEM = pl.BlockSpec(memory_space=pltpu.SMEM)
+PARAMS = pltpu.CompilerParams(vmem_limit_bytes=16 * 2**20)
+STACK_COST = pl.CostEstimate(flops=20 * 10**9, bytes_accessed=0, transcendentals=0)
+NEAR_COST = pl.CostEstimate(flops=60 * 10**9, bytes_accessed=0, transcendentals=0)
 
 
 def shifted(block, axis, distance):
@@ -20,7 +25,223 @@
     return lax.ppermute(block, axis, route)
 
 
-def body(queries, keys, values, block_order):
+def swapped(block, axis, bits):
+    route = [(i, i ^ bits) for i in range(lax.axis_size(axis))]
+    return lax.ppermute(block, axis, route)
+
+
+def place():
+    me = lax.axis_index("seq")
+    return me // CORES, me % CORES, lax.axis_index("head")
+
+
+def over(block, turn):
+    return swapped(block, "seq", CORES * turn)
+
+
+def cut(start, size):
+    return pl.ds(pl.multiple_of(start * size, size), size)
+
+
+def copy_all(pairs, sem):
+    copies = [pltpu.make_async_copy(one, other, sem.at[i]) for i, (one, other) in enumerate(pairs)]
+    for one in copies:
+        one.start()
+    return copies
+
+
+def cut_pairs(k_ref, v_ref, chip, out):
+    width = out.shape[1] // 2
+    return [
+        (k_ref.at[:, cut(chip, width)], out.at[:, pl.ds(0, width)]),
+        (v_ref.at[:, cut(chip, width)], out.at[:, pl.ds(width, width)]),
+    ]
+
+
+def split_kernel(chips, q_ref, k_ref, v_ref, *rest):
+    kv_refs, q_refs, sem = rest[:chips], rest[chips:-1], rest[-1]
+    z, _, head = place()
+    pairs = []
+    for turn in [*range(1, chips), 0]:
+        pairs += cut_pairs(k_ref, v_ref, z ^ turn, kv_refs[turn])
+    for step, out in enumerate(q_refs):
+        pairs.append((q_ref.at[:, cut(head ^ step, out.shape[1])], out))
+    for one in copy_all(pairs, sem):
+        one.wait()
+
+
+def split(queries, keys, values, chips):
+    rows, width = keys.shape
+    groups = queries.shape[1] // width
+    outs = [jax.ShapeDtypeStruct((rows, 2 * width // chips), keys.dtype)] * chips
+    outs += [jax.ShapeDtypeStruct((queries.shape[0], width), queries.dtype)] * groups
+    outs = pl.pallas_call(
+        functools.partial(split_kernel, chips),
+        out_shape=outs,
+        in_specs=[HBM] * 3,
+        out_specs=[ANY] * len(outs),
+        scratch_shapes=[pltpu.SemaphoreType.DMA((2 * chips + groups,))],
+        compiler_params=PARAMS,
+    )(*(pltpu.with_memory_space_constraint(x, pltpu.HBM) for x in (queries, keys, values)))
+    return outs[:chips], outs[chips:]
+
+
+def regroup_kernel(chips, groups, order_ref, *rest):
+    q_parts, q_refs, rel_ref = rest[:groups], rest[groups:-1], rest[-1]
+    z, core, head = place()
+    sub, (rows, width) = q_parts[0].shape[0], q_refs[0].shape
+    for turn, out in enumerate(q_refs):
+        for step, part in enumerate(q_parts):
+            out[cut(head ^ step, sub), :] = part[:, cut(z ^ turn, width)]
+    inner = lax.broadcasted_iota(jnp.int32, (8, rows), 1)
+    starts = [
+        order_ref[(z ^ (slot % chips)) * CORES + (core ^ (slot // chips))] * rows for slot in range(chips * CORES)
+    ]
+    for turn in range(chips):
+        for slot, start in enumerate(starts):
+            rel_ref[turn, :, pl.ds(slot * rows, rows)] = inner + (start - starts[turn])
+
+
+def regroup(block_order, q_parts, rows, chips):
+    outs = [jax.ShapeDtypeStruct((rows, q_parts[0].shape[1] // chips), q_parts[0].dtype)] * chips
+    outs += [jax.ShapeDtypeStruct((chips, 8, rows * chips * CORES), jnp.int32)]
+    outs = pl.pallas_call(
+        functools.partial(regroup_kernel, chips, len(q_parts)),
+        out_shape=outs,
+        in_specs=[SMEM] + [VMEM] * len(q_parts),
+        out_specs=[VMEM] * len(outs),
+        compiler_params=PARAMS,
+    )(block_order, *q_parts)
+    return outs[:-1], outs[-1]
+
+
+def stack_kernel(*refs):
+    for at, ref in enumerate(refs[:-1]):
+        refs[-1][at] = ref[...]
+
+
+def stack(parts):
+    return pl.pallas_call(
+        stack_kernel,
+        out_shape=jax.ShapeDtypeStruct((len(parts),) + parts[0].shape, parts[0].dtype),
+        in_specs=[VMEM] * len(parts),
+        out_specs=VMEM,
+        compiler_params=PARAMS,
+        cost_estimate=STACK_COST,
+    )(*parts)
+
+
+def attend_kernel(turns, count, first, stacked, alone, rel_ref, *rest):
+    q_refs, rest = rest[: len(turns)], rest[len(turns) :]
+    if first:
+        blocks, states = rest[:count], rest[count:]
+    else:
+        blocks = {turn: rest[0].at[at] for at, turn in enumerate(stacked)} | dict(zip(alone, rest[1:]))
+        blocks, rest = [blocks[turn] for turn in range(count)], rest[1 + len(alone) :]
+        states, outs = rest[: 2 * len(turns)], rest[2 * len(turns) :]
+    rows, width = q_refs[0].shape
+    scale = LOG2E / HEAD_DIM**0.5
+    below = lax.broadcasted_iota(jnp.int32, (rows, CORES * rows), 0)
+    ones = jnp.ones((CORES * rows, HEAD_DIM), jnp.bfloat16)
+    start = 0 if first else count * rows
+
+    def both(at, column):
+        return jnp.concatenate([ref[:, pl.ds(column, HEAD_DIM)] for ref in blocks[at : at + CORES]], 0)
+
+    for index, (turn, q_ref) in enumerate(zip(turns, q_refs)):
+        top_ref, sums_ref = states[2 * index : 2 * index + 2]
+        for column in range(0, width, HEAD_DIM):
+            tops, wide = pl.ds(column, HEAD_DIM), pl.ds(2 * column, 2 * HEAD_DIM)
+            top = None if first else top_ref[:, tops]
+            sums = None if first else sums_ref[:, wide]
+            for at in range(0, count, CORES):
+                s = lax.dot_general(
+                    q_ref[:, tops], both(at, column), (((1,), (1,)), ((), ())), preferred_element_type=jnp.float32
+                )
+                rel = rel_ref[turn, 0:1, pl.ds(start + at * rows, CORES * rows)]
+                s = jnp.where(rel <= below, s, jnp.float32(-1e30))
+                high = jnp.broadcast_to(jnp.max(s, axis=1, keepdims=True), (rows, HEAD_DIM))
+                high = high if top is None else jnp.maximum(top, high)
+                weight = jnp.exp2((s - jnp.concatenate([high] * CORES, 1)) * scale).astype(jnp.bfloat16)
+                values = jnp.concatenate([both(at, width + column), ones], 1)
+                mixed = jnp.dot(weight, values, preferred_element_type=jnp.float32)
+                if top is not None:
+                    shrink = jnp.exp2((top - high) * scale)
+                    mixed += sums * jnp.concatenate([shrink, shrink], 1)
+                top, sums = high, mixed
+            if first:
+                top_ref[:, tops], sums_ref[:, wide] = top, sums
+            else:
+                outs[index][:, tops] = (sums[:, :HEAD_DIM] / sums[:, HEAD_DIM:]).astype(outs[index].dtype)
+
+
+def attend_near(turns, rel, q, near):
+    rows, width = q[0].shape
+    state = [jax.ShapeDtypeStruct((rows, wide), jnp.float32) for wide in (width, 2 * width)]
+    outs = pl.pallas_call(
+        functools.partial(attend_kernel, turns, len(near), True, (), ()),
+        out_shape=state * len(turns),
+        in_specs=[VMEM] * (1 + len(turns) + len(near)),
+        out_specs=[VMEM] * (2 * len(turns)),
+        compiler_params=PARAMS,
+        cost_estimate=NEAR_COST,
+    )(rel, *(q[turn] for turn in turns), *near)
+    return {turn: outs[2 * index : 2 * index + 2] for index, turn in enumerate(turns)}
+
+
+def attend_far(turns, rel, q, far, stacked, alone, states):
+    return pl.pallas_call(
+        functools.partial(attend_kernel, turns, len(q), False, stacked, tuple(alone)),
+        out_shape=[jax.ShapeDtypeStruct(q[0].shape, q[0].dtype)] * len(turns),
+        in_specs=[VMEM] * (2 + len(alone) + 3 * len(turns)),
+        out_specs=[VMEM] * len(turns),
+        compiler_params=PARAMS,
+    )(rel, *(q[turn] for turn in turns), far, *alone.values(), *(part for turn in turns for part in states[turn]))
+
+
+def join_kernel(chips, *refs):
+    parts, out, sem = refs[:chips], refs[-2], refs[-1]
+    z, _, _ = place()
+    width = parts[0].shape[1]
+    pairs = [(part, out.at[:, cut(z ^ turn, width)]) for turn, part in enumerate(parts)]
+    for one in copy_all(pairs, sem):
+        one.wait()
+
+
+def join(parts):
+    chips, (rows, width) = len(parts), parts[0].shape
+    return pl.pallas_call(
+        functools.partial(join_kernel, chips),
+        out_shape=jax.ShapeDtypeStruct((rows, width * chips), parts[0].dtype),
+        in_specs=[ANY] * chips,
+        out_specs=ANY,
+        scratch_shapes=[pltpu.SemaphoreType.DMA((chips,))],
+        compiler_params=PARAMS,
+    )(*parts)
+
+
+def by_heads(queries, keys, values, block_order):
+    chips = lax.axis_size("seq") // CORES
+    groups = lax.axis_size("head")
+    half = chips // 2
+    across, within = list(range(half, chips)), list(range(1, half))
+    kv, q_cut = split(queries, keys, values, chips)
+    near = [kv[0]] + [over(kv[turn], turn) for turn in range(1, chips)]
+    q_parts = [q_cut[0]] + [swapped(q_cut[step], "head", step) for step in range(1, groups)]
+    q, rel = regroup(block_order, q_parts, keys.shape[0], chips)
+    q = [q[0]] + [over(q[turn], turn) for turn in range(1, chips)]
+    stacked = [*across[::-1], 0]
+    far = swapped(stack([near[turn] for turn in stacked]), "seq", 1)
+    alone = {turn: swapped(near[turn], "seq", 1) for turn in within}
+    states = attend_near([*across, *within, 0], rel, q, near)
+    out = {}
+    for turns in (across, [*within, 0]):
+        for turn, part in zip(turns, attend_far(turns, rel, q, far, stacked, alone, states)):
+            out[turn] = over(part, turn) if turn else part
+    return join([out[turn] for turn in range(chips)])
+
+
+def around_ring(queries, keys, values, block_order):
     seq_count = lax.axis_size("seq")
     me_index = lax.axis_index("seq")
     local_q = lax.all_to_all(queries, "head", split_axis=1, concat_axis=0, tiled=True)
@@ -63,34 +284,33 @@
     key_idx = lax.broadcasted_iota(jnp.int32, (rows, rows), 1)
     state = tile(start_state, (keys, values), key_idx <= query_idx)
 
-    def forward(kv_pair):
-        return jax.tree.map(
-            lambda part, own: part.astype(own.dtype), shifted(shortened(kv_pair), "seq", 1), kv_pair
-        )
-
-    def backward(kv_pair):
-        return jax.tree.map(
-            lambda part, own: part.astype(own.dtype),
-            shifted(shortened(kv_pair), "seq", -1),
-            kv_pair,
-        )
-
     def both_turn(step, carry):
         ahead, behind, st = carry
-        ahead = forward(ahead)
+        ahead = tuple(shifted(part, "seq", 1) for part in ahead)
         st = absorb(st, ahead, me_index - step + seq_count)
-        behind = backward(behind)
+        behind = tuple(shifted(part, "seq", -1) for part in behind)
         st = absorb(st, behind, me_index + step)
         return (ahead, behind, st)
 
     ahead, behind, state = lax.fori_loop(
         1, (seq_count - 1) // 2 + 1, both_turn, ((keys, values), (keys, values), state)
     )
-    ahead = forward(ahead)
-    state = absorb(state, ahead, me_index - seq_count // 2 + seq_count)
+    if seq_count % 2 == 0:
+        ahead = tuple(shifted(part, "seq", 1) for part in ahead)
+        state = absorb(state, ahead, me_index - seq_count // 2 + seq_count)
     rowmax, total, accum = state
     result = accum / jnp.transpose(total)[:, :, None]
     return result.reshape(rows, head_count * HEAD_DIM).astype(jnp.bfloat16)
+
+
+def body(queries, keys, values, block_order):
+    seq_count, groups = lax.axis_size("seq"), lax.axis_size("head")
+    chips = seq_count // CORES
+    heads = keys.shape[1] // HEAD_DIM
+    powers = all(n > 1 and n & (n - 1) == 0 for n in (chips, groups))
+    if seq_count % CORES == 0 and powers and heads % chips == 0:
+        return by_heads(queries, keys, values, block_order)
+    return around_ring(queries, keys, values, block_order)
 
 
 def solution(mesh):

time: 71.5 us -> 34.4 us (0.48)
  waiting for transfers between devices: 29.5 us -> 11.4 us
  local copies, waits for them, and re-layouts: 7.49 us -> 0.01 us
  loops' own time: 7.41 us -> 0 us
  matrix products: 6 us -> 0 us
  Pallas kernels: 0 us -> 4.94 us
  between operations: 1.4 us -> 0.08 us
  other arithmetic: 0.98 us -> 0 us
    ppermute x14, waiting for transfers between devices: 26.8 us -> 11.4 us  [swapped(): return lax.ppermute(block, axis, route)]
    another operation x1 -> x0, loops' own time: 7.41 us -> none  [body(): lax.fori_loop(1, (seq_count - 1) // 2 + 1, both_turn, ((keys, values), (k...]
    dot_general x16 -> x0, matrix products: 6 us -> none  [the longest x8 3.3 us: tile(): jnp.einsum('hqk,khd->qhd', weight.astype(jnp.bfloat16), v_three, preferre...]
    all_to_all x1 -> x0, starting transfers between devices: 5.29 us -> none  [body(): lax.all_to_all(queries, 'head', split_axis=1, concat_axis=0, tiled=True)]
    pallas_call x0 -> x7, Pallas kernels: none -> 4.94 us  [the longest x2 1.35 us: attend_far(): pl.pallas_call(functools.partial(attend_kernel, turns, len(q), False, sta...]
    ppermute x14, starting transfers between devices: 13.1 us -> 17.9 us  [swapped(): return lax.ppermute(block, axis, route)]
    all_to_all x1 -> x0, waiting for transfers between devices: 2.69 us -> none  [body(): lax.all_to_all(queries, 'head', split_axis=1, concat_axis=0, tiled=True)]
    dynamic_slice x4 -> x0, local copies, waits for them, and re-layouts: 2.51 us -> none  [absorb(): visible = block_order[source % seq_count] < mine]
  transfers between devices with their start and end apart: 15 -> 14, of which waited for: 14 -> 9; matrix products, arithmetic and copies ran while one was open for 10% -> 0% of each run, Pallas kernels for 0% -> 7%
where the time goes in v2:
time: 34.4 us; the launch traced here: 34.3 us
  starting transfers between devices  17.9 us (52%)
  waiting for transfers between devices  11.4 us (33%)
  Pallas kernels  4.94 us (14%)
    ppermute x14, starting transfers between devices, swapped(): return lax.ppermute(block, axis, route)  17.9 us
    ppermute x14, waiting for transfers between devices, swapped(): return lax.ppermute(block, axis, route)  11.4 us
    pallas_call x2, Pallas kernels, attend_far(): pl.pallas_call(functools.partial(attend_kernel, turns, len(q), False, sta...  1.35 us
    pallas_call x1, Pallas kernels, split(): pl.pallas_call(functools.partial(split_kernel, chips), out_shape=outs, in...  1.27 us
    pallas_call x1, Pallas kernels, attend_near(): pl.pallas_call(functools.partial(attend_kernel, turns, len(near), True, (...  0.96 us
    pallas_call x1, Pallas kernels, join(): pl.pallas_call(functools.partial(join_kernel, chips), out_shape=jax.Shape...  0.73 us
  transfers between devices with their start and end apart: 14, of which 9 were waited for; matrix products, arithmetic and copies ran while one was open for 0% of the time, Pallas kernels for 7%

profile of v2, /device:TPU:0, one launch (start us, length us, event | category | flops | bytes accessed | tf_op | source)
XLA Modules:
  0.0 34.3 jit_solution(15273259079583611544)
XLA Ops:
  0.0 1.3 %shard_map.46 = (bf16[128,512]{1,0:T(8,128)(2,1)S(1)}, bf16[128,512]{1,0:T(8,128)(2,1)S(1)}, bf16[128,512]{1,0:T(8,128)(2,1)S(1)}, bf16[128,512]{1,0:T(8,128)(2,...) custom-call(bf16[32,4096]{1,0:T(8,128)(2,1)} %q_ref.1, ...), custom_call_target="tpu_custom_call" | custom-call | tf_op jit(solution)/shard_map/pallas_call | solution.py:78
  1.3 5.1 %collective-permute-start.4 = (bf16[128,512]{1,0:T(8,128)(2,1)S(1)}, bf16[128,512]{1,0:T(8,128)(2,1)S(1)}, u32[]{:S(2)}, u32[]{:S(2)}) collective-permute-start(bf16[128,512]{1,0:T(8,128)(2,1)S(1)} %get-tuple-element.37), channel_id=1, source_target_pairs={{0,24},{4,28},{8,16},{12,20},{16,8},{20,12},{24,0},{28,4},{1,25},{... | collective-permute-start | bytes 393224 | tf_op jit(solution)/shard_map/ppermute | solution.py:30
  6.4 0.0 collective-permute-start.5
  6.4 1.5 %collective-permute-start = (bf16[32,1024]{1,0:T(8,128)(2,1)S(1)}, bf16[32,1024]{1,0:T(8,128)(2,1)S(1)}, u32[]{:S(2)}, u32[]{:S(2)}) collective-permute-start(bf16[32,1024]{1,0:T(8,128)(2,1)S(1)} %get-tuple-element.31), channel_id=1, source_target_pairs={{0,1},{1,0},{2,3},{3,2},{4,5},{5,4},{6,7},{7,6},{8,9},{9,8},{10,11... | collective-permute-start | bytes 196616 | tf_op jit(solution)/shard_map/ppermute | solution.py:30
  7.9 1.5 %collective-permute-start.1 = (bf16[32,1024]{1,0:T(8,128)(2,1)S(1)}, bf16[32,1024]{1,0:T(8,128)(2,1)S(1)}, u32[]{:S(2)}, u32[]{:S(2)}) collective-permute-start(bf16[32,1024]{1,0:T(8,128)(2,1)S(1)} %get-tuple-element.32), channel_id=1, source_target_pairs={{0,2},{1,3},{2,0},{3,1},{4,6},{5,7},{6,4},{7,5},{8,10},{9,11},{10,... | collective-permute-start | bytes 196616 | tf_op jit(solution)/shard_map/ppermute | solution.py:30
  9.4 0.5 %collective-permute-start.2 = (bf16[32,1024]{1,0:T(8,128)(2,1)S(1)}, bf16[32,1024]{1,0:T(8,128)(2,1)S(1)}, u32[]{:S(2)}, u32[]{:S(2)}) collective-permute-start(bf16[32,1024]{1,0:T(8,128)(2,1)S(1)} %get-tuple-element.33), channel_id=1, source_target_pairs={{0,3},{1,2},{2,1},{3,0},{4,7},{5,6},{6,5},{7,4},{8,11},{9,10},{10,... | collective-permute-start | bytes 196616 | tf_op jit(solution)/shard_map/ppermute | solution.py:30
  9.9 0.8 %collective-permute-done.rest_1_ = bf16[32,1024]{1,0:T(8,128)(2,1)S(1)} collective-permute-done((bf16[32,1024]{1,0:T(8,128)(2,1)S(1)}, bf16[32,1024]{1,0:T(8,128)(2,1)S(1)}, u32[]{:S(2)}, u32[]{:S(2)}) %collective-permute-start) | collective-permute-done | bytes 65568 | tf_op jit(solution)/shard_map/ppermute | solution.py:30
  10.7 0.6 %collective-permute-start.7 = (bf16[128,512]{1,0:T(8,128)(2,1)S(1)}, bf16[128,512]{1,0:T(8,128)(2,1)S(1)}, u32[]{:S(2)}, u32[]{:S(2)}) collective-permute-start(bf16[128,512]{1,0:T(8,128)(2,1)S(1)} %get-tuple-element.40), channel_id=1, source_target_pairs={{0,8},{4,12},{8,0},{12,4},{16,24},{20,28},{24,16},{28,20},{1,9},{5... | collective-permute-start | bytes 393224 | tf_op jit(solution)/shard_map/ppermute | solution.py:30
  11.3 1.6 %collective-permute-done.1.rest_2_ = bf16[32,1024]{1,0:T(8,128)(2,1)S(1)} collective-permute-done((bf16[32,1024]{1,0:T(8,128)(2,1)S(1)}, bf16[32,1024]{1,0:T(8,128)(2,1)S(1)}, u32[]{:S(2)}, u32[]{:S(2)}) %collective-permute-start.1) | collective-permute-done | bytes 65568 | tf_op jit(solution)/shard_map/ppermute | solution.py:30
  12.9 1.7 %collective-permute-done.2.rest_3_ = bf16[32,1024]{1,0:T(8,128)(2,1)S(1)} collective-permute-done((bf16[32,1024]{1,0:T(8,128)(2,1)S(1)}, bf16[32,1024]{1,0:T(8,128)(2,1)S(1)}, u32[]{:S(2)}, u32[]{:S(2)}) %collective-permute-start.2) | collective-permute-done | bytes 65568 | tf_op jit(solution)/shard_map/ppermute | solution.py:30
  14.6 0.6 %shard_map.47 = (bf16[128,256]{1,0:T(8,128)(2,1)S(1)}, bf16[128,256]{1,0:T(8,128)(2,1)S(1)}, bf16[128,256]{1,0:T(8,128)(2,1)S(1)}, bf16[128,256]{1,0:T(8,128)(2,1)S(1)}, s32[4,8,1024]{2,1,0:T(8,128)S(1)}) custom-call(s32[8]{0:T(128)S(1)} %copy-done, bf16[32,1024]{1,0:T(8,128)(2,1)S(1)} %get-tuple-element.30.rest_0_, ...), custom_call_target="tpu_custom_call" | custom-call | tf_op jit(solution)/shard_map/pallas_call | solution.py:108
  15.2 2.0 %collective-permute-start.10 = (bf16[128,256]{1,0:T(8,128)(2,1)S(1)}, bf16[128,256]{1,0:T(8,128)(2,1)S(1)}, u32[]{:S(2)}, u32[]{:S(2)}) collective-permute-start(bf16[128,256]{1,0:T(8,128)(2,1)S(1)} %get-tuple-element.42), channel_id=1, source_target_pairs={{0,24},{4,28},{8,16},{12,20},{16,8},{20,12},{24,0},{28,4},{1,25},{... | collective-permute-start | bytes 196616 | tf_op jit(solution)/shard_map/ppermute | solution.py:30
  17.2 1.6 %collective-permute-start.3 = (bf16[128,256]{1,0:T(8,128)(2,1)S(1)}, bf16[128,256]{1,0:T(8,128)(2,1)S(1)}, u32[]{:S(2)}, u32[]{:S(2)}) collective-permute-start(bf16[128,256]{1,0:T(8,128)(2,1)S(1)} %get-tuple-element.35), channel_id=1, source_target_pairs={{0,8},{4,12},{8,0},{12,4},{16,24},{20,28},{24,16},{28,20},{1,9},{5... | collective-permute-start | bytes 196616 | tf_op jit(solution)/shard_map/ppermute | solution.py:30
  18.7 0.0 collective-permute-done.4.refs_0_.rest_7_
  18.7 0.9 %collective-permute-start.9 = (bf16[128,256]{1,0:T(8,128)(2,1)S(1)}, bf16[128,256]{1,0:T(8,128)(2,1)S(1)}, u32[]{:S(2)}, u32[]{:S(2)}) collective-permute-start(bf16[128,256]{1,0:T(8,128)(2,1)S(1)} %get-tuple-element.41), channel_id=1, source_target_pairs={{0,16},{4,20},{8,24},{12,28},{16,0},{20,4},{24,8},{28,12},{1,17},{... | collective-permute-start | bytes 196616 | tf_op jit(solution)/shard_map/ppermute | solution.py:30
  19.7 0.1 collective-permute-start.6
  19.8 0.0 collective-permute-done.7.rest_5_
  19.8 0.5 %collective-permute-start.8 = (bf16[128,512]{1,0:T(8,128)(2,1)S(1)}, bf16[128,512]{1,0:T(8,128)(2,1)S(1)}, u32[]{:S(2)}, u32[]{:S(2)}) collective-permute-start(bf16[128,512]{1,0:T(8,128)(2,1)S(1)} %collective-permute-done.7.rest_5_), channel_id=1, source_target_pairs={{0,4},{4,0},{8,12},{12,8},{16,20},{20,16},{24,28},{28,24},{1,5},{5... | collective-permute-start | bytes 393224 | tf_op jit(solution)/shard_map/ppermute | solution.py:30
  20.3 1.1 %collective-permute-done.10.rest_1_ = bf16[128,256]{1,0:T(8,128)(2,1)S(1)} collective-permute-done((bf16[128,256]{1,0:T(8,128)(2,1)S(1)}, bf16[128,256]{1,0:T(8,128)(2,1)S(1)}, u32[]{:S(2)}, u32[]{:S(2)}) %collective-permute-start.10) | collective-permute-done | bytes 65568 | tf_op jit(solution)/shard_map/ppermute | solution.py:30
  21.4 1.1 %collective-permute-done.3.rest_2_.rest_0_ = bf16[128,256]{1,0:T(8,128)(2,1)S(1)} collective-permute-done((bf16[128,256]{1,0:T(8,128)(2,1)S(1)}, bf16[128,256]{1,0:T(8,128)(2,1)S(1)}, u32[]{:S(2)}, u32[]{:S(2)}) %collective-permute-start.3) | collective-permute-done | bytes 65568 | tf_op jit(solution)/shard_map/ppermute | solution.py:30
  22.5 2.0 %collective-permute-done.9.rest_0_ = bf16[128,256]{1,0:T(8,128)(2,1)S(1)} collective-permute-done((bf16[128,256]{1,0:T(8,128)(2,1)S(1)}, bf16[128,256]{1,0:T(8,128)(2,1)S(1)}, u32[]{:S(2)}, u32[]{:S(2)}) %collective-permute-start.9) | collective-permute-done | bytes 65568 | tf_op jit(solution)/shard_map/ppermute | solution.py:30
  24.5 1.0 %shard_map.49 = (f32[128,256]{1,0:T(8,128)S(1)}, f32[128,512]{1,0:T(8,128)S(1)}, f32[128,256]{1,0:T(8,128)S(1)}, f32[128,512]{1,0:T(8,128)S(1)}, f32[128,256]{1,...) custom-call(s32[4,8,1024]{2,1,0:T(8,128)S(1)} %get-tuple-element.34.rel_ref, ...), custom_call_target="tpu_custom_call" | custom-call | flops 60000002048 | tf_op jit(solution)/shard_map/pallas_call | solution.py:181
  25.5 0.0 collective-permute-done.6.rest_2_
  25.5 0.7 %shard_map.51 = (bf16[128,256]{1,0:T(8,128)(2,1)S(1)}, bf16[128,256]{1,0:T(8,128)(2,1)S(1)}) custom-call(s32[4,8,1024]{2,1,0:T(8,128)S(1)} %get-tuple-element.34.rel_ref, bf16[128,256]{1,0:T(8,128)(2,1)S(1)} %collective-permute-done.9.rest_0_, bf16[128,256]{1,0:T(8,128)(2,1)S(1)} %collective-permute-done.10.rest_1_, ...), custom_call_target="tpu_custom_call" | custom-call | tf_op jit(solution)/shard_map/pallas_call | solution.py:193
  26.2 0.4 %collective-permute-start.12 = (bf16[128,256]{1,0:T(8,128)(2,1)S(1)}, bf16[128,256]{1,0:T(8,128)(2,1)S(1)}, u32[]{:S(2)}, u32[]{:S(2)}) collective-permute-start(bf16[128,256]{1,0:T(8,128)(2,1)S(1)} %get-tuple-element.53), channel_id=1, source_target_pairs={{0,16},{4,20},{8,24},{12,28},{16,0},{20,4},{24,8},{28,12},{1,17},{... | collective-permute-start | bytes 196616 | tf_op jit(solution)/shard_map/ppermute | solution.py:30
  26.6 2.0 %collective-permute-start.13 = (bf16[128,256]{1,0:T(8,128)(2,1)S(1)}, bf16[128,256]{1,0:T(8,128)(2,1)S(1)}, u32[]{:S(2)}, u32[]{:S(2)}) collective-permute-start(bf16[128,256]{1,0:T(8,128)(2,1)S(1)} %get-tuple-element.54), channel_id=1, source_target_pairs={{0,24},{4,28},{8,16},{12,20},{16,8},{20,12},{24,0},{28,4},{1,25},{... | collective-permute-start | bytes 196616 | tf_op jit(solution)/shard_map/ppermute | solution.py:30
  28.5 0.7 %shard_map.50 = (bf16[128,256]{1,0:T(8,128)(2,1)S(1)}, bf16[128,256]{1,0:T(8,128)(2,1)S(1)}) custom-call(s32[4,8,1024]{2,1,0:T(8,128)S(1)} %get-tuple-element.34.rel_ref, bf16[128,256]{1,0:T(8,128)(2,1)S(1)} %collective-permute-done.3.rest_2_.rest_0_, bf16[128,256]{1,0:T(8,128)(2,1)S(1)} %get-tuple-element.36.rest_3_.rest_1_, ...), custom_call_target="tpu_custom_call" | custom-call | tf_op jit(solution)/shard_map/pallas_call | solution.py:193
  29.2 1.3 %collective-permute-start.11 = (bf16[128,256]{1,0:T(8,128)(2,1)S(1)}, bf16[128,256]{1,0:T(8,128)(2,1)S(1)}, u32[]{:S(2)}, u32[]{:S(2)}) collective-permute-start(bf16[128,256]{1,0:T(8,128)(2,1)S(1)} %get-tuple-element.48), channel_id=1, source_target_pairs={{0,8},{4,12},{8,0},{12,4},{16,24},{20,28},{24,16},{28,20},{1,9},{5... | collective-permute-start | bytes 196616 | tf_op jit(solution)/shard_map/ppermute | solution.py:30
  30.5 1.1 %collective-permute-done.12.refs_2_ = bf16[128,256]{1,0:T(8,128)(2,1)S(1)} collective-permute-done((bf16[128,256]{1,0:T(8,128)(2,1)S(1)}, bf16[128,256]{1,0:T(8,128)(2,1)S(1)}, u32[]{:S(2)}, u32[]{:S(2)}) %collective-permute-start.12) | collective-permute-done | bytes 65568 | tf_op jit(solution)/shard_map/ppermute | solution.py:30
  31.6 1.1 %collective-permute-done.13.refs_3_ = bf16[128,256]{1,0:T(8,128)(2,1)S(1)} collective-permute-done((bf16[128,256]{1,0:T(8,128)(2,1)S(1)}, bf16[128,256]{1,0:T(8,128)(2,1)S(1)}, u32[]{:S(2)}, u32[]{:S(2)}) %collective-permute-start.13) | collective-permute-done | bytes 65568 | tf_op jit(solution)/shard_map/ppermute | solution.py:30
  32.7 0.8 %collective-permute-done.11.refs_1_ = bf16[128,256]{1,0:T(8,128)(2,1)S(1)} collective-permute-done((bf16[128,256]{1,0:T(8,128)(2,1)S(1)}, bf16[128,256]{1,0:T(8,128)(2,1)S(1)}, u32[]{:S(2)}, u32[]{:S(2)}) %collective-permute-start.11) | collective-permute-done | bytes 65568 | tf_op jit(solution)/shard_map/ppermute | solution.py:30
  33.5 0.7 %shard_map.52 = bf16[128,1024]{1,0:T(8,128)(2,1)} custom-call(bf16[128,256]{1,0:T(8,128)(2,1)S(1)} %get-tuple-element.47.refs_0_, bf16[128,256]{1,0:T(8,128)(2,1)S(1)} %collective-permute-done.11.refs_1_, bf16[128,256]{1,0:T(8,128)(2,1)S(1)} %collective-permute-done.12.refs_2_, bf16[128,256]{1,0:T(8,128)(2,1)S(1)} %collective-permute-done.13.refs_3_), custom_call_target="tpu_custom_call" | custom-call | tf_op jit(solution)/shard_map/pallas_call | solution.py:213
  (5 shorter events, 0.0 us)
Async XLA Ops:
  1.3 17.5 %collective-permute-start.4 = (bf16[128,512]{1,0:T(8,128)(2,1)S(1)}, bf16[128,512]{1,0:T(8,128)(2,1)S(1)}, u32[]{:S(2)}, u32[]{:S(2)}) collective-permute-start(bf16[128,512]{1,0:T(8,128)(2,1)S(1)} %get-tuple-element.37), channel_id=1, source_target_pairs={{0,24},{4,28},{8,16},{12,20},{16,8},{20,12},{24,0},{28,4},{1,25},{... | collective-permute-start | bytes 393224 | tf_op jit(solution)/shard_map/ppermute | solution.py:30
  6.4 13.3 %collective-permute-start.5 = (bf16[128,512]{1,0:T(8,128)(2,1)S(1)}, bf16[128,512]{1,0:T(8,128)(2,1)S(1)}, u32[]{:S(2)}, u32[]{:S(2)}) collective-permute-start(bf16[128,512]{1,0:T(8,128)(2,1)S(1)} %get-tuple-element.38), channel_id=1, source_target_pairs={{0,16},{4,20},{8,24},{12,28},{16,0},{20,4},{24,8},{28,12},{1,17},{... | collective-permute-start | bytes 393224 | tf_op jit(solution)/shard_map/ppermute | solution.py:30
  6.4 4.3 %collective-permute-start = (bf16[32,1024]{1,0:T(8,128)(2,1)S(1)}, bf16[32,1024]{1,0:T(8,128)(2,1)S(1)}, u32[]{:S(2)}, u32[]{:S(2)}) collective-permute-start(bf16[32,1024]{1,0:T(8,128)(2,1)S(1)} %get-tuple-element.31), channel_id=1, source_target_pairs={{0,1},{1,0},{2,3},{3,2},{4,5},{5,4},{6,7},{7,6},{8,9},{9,8},{10,11... | collective-permute-start | bytes 196616 | tf_op jit(solution)/shard_map/ppermute | solution.py:30
  7.9 5.0 %collective-permute-start.1 = (bf16[32,1024]{1,0:T(8,128)(2,1)S(1)}, bf16[32,1024]{1,0:T(8,128)(2,1)S(1)}, u32[]{:S(2)}, u32[]{:S(2)}) collective-permute-start(bf16[32,1024]{1,0:T(8,128)(2,1)S(1)} %get-tuple-element.32), channel_id=1, source_target_pairs={{0,2},{1,3},{2,0},{3,1},{4,6},{5,7},{6,4},{7,5},{8,10},{9,11},{10,... | collective-permute-start | bytes 196616 | tf_op jit(solution)/shard_map/ppermute | solution.py:30
  9.4 5.2 %collective-permute-start.2 = (bf16[32,1024]{1,0:T(8,128)(2,1)S(1)}, bf16[32,1024]{1,0:T(8,128)(2,1)S(1)}, u32[]{:S(2)}, u32[]{:S(2)}) collective-permute-start(bf16[32,1024]{1,0:T(8,128)(2,1)S(1)} %get-tuple-element.33), channel_id=1, source_target_pairs={{0,3},{1,2},{2,1},{3,0},{4,7},{5,6},{6,5},{7,4},{8,11},{9,10},{10,... | collective-permute-start | bytes 196616 | tf_op jit(solution)/shard_map/ppermute | solution.py:30
  10.7 3.9 %copy-start = (s32[8]{0:T(128)S(1)}, s32[8]{0:T(128)}, u32[]{:S(2)}) copy-start(s32[8]{0:T(128)} %order_ref.1) | copy-start | bytes 100
  10.7 9.1 %collective-permute-start.7 = (bf16[128,512]{1,0:T(8,128)(2,1)S(1)}, bf16[128,512]{1,0:T(8,128)(2,1)S(1)}, u32[]{:S(2)}, u32[]{:S(2)}) collective-permute-start(bf16[128,512]{1,0:T(8,128)(2,1)S(1)} %get-tuple-element.40), channel_id=1, source_target_pairs={{0,8},{4,12},{8,0},{12,4},{16,24},{20,28},{24,16},{28,20},{1,9},{5... | collective-permute-start | bytes 393224 | tf_op jit(solution)/shard_map/ppermute | solution.py:30
  15.2 6.2 %collective-permute-start.10 = (bf16[128,256]{1,0:T(8,128)(2,1)S(1)}, bf16[128,256]{1,0:T(8,128)(2,1)S(1)}, u32[]{:S(2)}, u32[]{:S(2)}) collective-permute-start(bf16[128,256]{1,0:T(8,128)(2,1)S(1)} %get-tuple-element.42), channel_id=1, source_target_pairs={{0,24},{4,28},{8,16},{12,20},{16,8},{20,12},{24,0},{28,4},{1,25},{... | collective-permute-start | bytes 196616 | tf_op jit(solution)/shard_map/ppermute | solution.py:30
  17.2 5.3 %collective-permute-start.3 = (bf16[128,256]{1,0:T(8,128)(2,1)S(1)}, bf16[128,256]{1,0:T(8,128)(2,1)S(1)}, u32[]{:S(2)}, u32[]{:S(2)}) collective-permute-start(bf16[128,256]{1,0:T(8,128)(2,1)S(1)} %get-tuple-element.35), channel_id=1, source_target_pairs={{0,8},{4,12},{8,0},{12,4},{16,24},{20,28},{24,16},{28,20},{1,9},{5... | collective-permute-start | bytes 196616 | tf_op jit(solution)/shard_map/ppermute | solution.py:30
  18.7 5.8 %collective-permute-start.9 = (bf16[128,256]{1,0:T(8,128)(2,1)S(1)}, bf16[128,256]{1,0:T(8,128)(2,1)S(1)}, u32[]{:S(2)}, u32[]{:S(2)}) collective-permute-start(bf16[128,256]{1,0:T(8,128)(2,1)S(1)} %get-tuple-element.41), channel_id=1, source_target_pairs={{0,16},{4,20},{8,24},{12,28},{16,0},{20,4},{24,8},{28,12},{1,17},{... | collective-permute-start | bytes 196616 | tf_op jit(solution)/shard_map/ppermute | solution.py:30
  19.7 5.8 %collective-permute-start.6 = (bf16[3,128,512]{2,1,0:T(8,128)(2,1)S(1)}, bf16[3,128,512]{2,1,0:T(8,128)(2,1)S(1)}, u32[]{:S(2)}, u32[]{:S(2)}) collective-permute-start(bf16[3,128,512]{2,1,0:T(8,128)(2,1)S(1)} %shard_map.48), channel_id=1, source_target_pairs={{0,4},{4,0},{8,12},{12,8},{16,20},{20,16},{24,28},{28,24},{1,5},{5... | collective-permute-start | bytes 1179656 | tf_op jit(solution)/shard_map/ppermute | solution.py:30
  19.8 5.7 %collective-permute-start.8 = (bf16[128,512]{1,0:T(8,128)(2,1)S(1)}, bf16[128,512]{1,0:T(8,128)(2,1)S(1)}, u32[]{:S(2)}, u32[]{:S(2)}) collective-permute-start(bf16[128,512]{1,0:T(8,128)(2,1)S(1)} %collective-permute-done.7.rest_5_), channel_id=1, source_target_pairs={{0,4},{4,0},{8,12},{12,8},{16,20},{20,16},{24,28},{28,24},{1,5},{5... | collective-permute-start | bytes 393224 | tf_op jit(solution)/shard_map/ppermute | solution.py:30
  26.2 5.4 %collective-permute-start.12 = (bf16[128,256]{1,0:T(8,128)(2,1)S(1)}, bf16[128,256]{1,0:T(8,128)(2,1)S(1)}, u32[]{:S(2)}, u32[]{:S(2)}) collective-permute-start(bf16[128,256]{1,0:T(8,128)(2,1)S(1)} %get-tuple-element.53), channel_id=1, source_target_pairs={{0,16},{4,20},{8,24},{12,28},{16,0},{20,4},{24,8},{28,12},{1,17},{... | collective-permute-start | bytes 196616 | tf_op jit(solution)/shard_map/ppermute | solution.py:30
  26.6 6.2 %collective-permute-start.13 = (bf16[128,256]{1,0:T(8,128)(2,1)S(1)}, bf16[128,256]{1,0:T(8,128)(2,1)S(1)}, u32[]{:S(2)}, u32[]{:S(2)}) collective-permute-start(bf16[128,256]{1,0:T(8,128)(2,1)S(1)} %get-tuple-element.54), channel_id=1, source_target_pairs={{0,24},{4,28},{8,16},{12,20},{16,8},{20,12},{24,0},{28,4},{1,25},{... | collective-permute-start | bytes 196616 | tf_op jit(solution)/shard_map/ppermute | solution.py:30
  29.2 4.3 %collective-permute-start.11 = (bf16[128,256]{1,0:T(8,128)(2,1)S(1)}, bf16[128,256]{1,0:T(8,128)(2,1)S(1)}, u32[]{:S(2)}, u32[]{:S(2)}) collective-permute-start(bf16[128,256]{1,0:T(8,128)(2,1)S(1)} %get-tuple-element.48), channel_id=1, source_target_pairs={{0,8},{4,12},{8,0},{12,4},{16,24},{20,28},{24,16},{28,20},{1,9},{5... | collective-permute-start | bytes 196616 | tf_op jit(solution)/shard_map/ppermute | solution.py:30

commit v3 on v2

--- a/solution.py
+++ b/solution.py
@@ -131,14 +131,17 @@
     )(*parts)
 
 
-def attend_kernel(turns, count, first, stacked, alone, rel_ref, *rest):
+def attend_kernel(turns, count, first, last, stacked, alone, rel_ref, *rest):
     q_refs, rest = rest[: len(turns)], rest[len(turns) :]
+    blocks, states, outs = [], (), ()
     if first:
-        blocks, states = rest[:count], rest[count:]
-    else:
-        blocks = {turn: rest[0].at[at] for at, turn in enumerate(stacked)} | dict(zip(alone, rest[1:]))
-        blocks, rest = [blocks[turn] for turn in range(count)], rest[1 + len(alone) :]
-        states, outs = rest[: 2 * len(turns)], rest[2 * len(turns) :]
+        blocks, rest = list(rest[:count]), rest[count:]
+    if last:
+        others = {turn: rest[0].at[at] for at, turn in enumerate(stacked)} | dict(zip(alone, rest[1:]))
+        blocks, rest = blocks + [others[turn] for turn in range(count)], rest[1 + len(alone) :]
+        outs, rest = rest[len(rest) - len(turns) :], rest[: len(rest) - len(turns)]
+    if not (first and last):
+        states = rest[: 2 * len(turns)]
     rows, width = q_refs[0].shape
     scale = LOG2E / HEAD_DIM**0.5
     below = lax.broadcasted_iota(jnp.int32, (rows, CORES * rows), 0)
@@ -149,12 +152,12 @@
         return jnp.concatenate([ref[:, pl.ds(column, HEAD_DIM)] for ref in blocks[at : at + CORES]], 0)
 
     for index, (turn, q_ref) in enumerate(zip(turns, q_refs)):
-        top_ref, sums_ref = states[2 * index : 2 * index + 2]
+        top_ref, sums_ref = states[2 * index : 2 * index + 2] or (None, None)
         for column in range(0, width, HEAD_DIM):
             tops, wide = pl.ds(column, HEAD_DIM), pl.ds(2 * column, 2 * HEAD_DIM)
             top = None if first else top_ref[:, tops]
             sums = None if first else sums_ref[:, wide]
-            for at in range(0, count, CORES):
+            for at in range(0, len(blocks), CORES):
                 s = lax.dot_general(
                     q_ref[:, tops], both(at, column), (((1,), (1,)), ((), ())), preferred_element_type=jnp.float32
                 )
@@ -169,17 +172,17 @@
                     shrink = jnp.exp2((top - high) * scale)
                     mixed += sums * jnp.concatenate([shrink, shrink], 1)
                 top, sums = high, mixed
-            if first:
+            if last:
+                outs[index][:, tops] = (sums[:, :HEAD_DIM] / sums[:, HEAD_DIM:]).astype(outs[index].dtype)
+            else:
                 top_ref[:, tops], sums_ref[:, wide] = top, sums
-            else:
-                outs[index][:, tops] = (sums[:, :HEAD_DIM] / sums[:, HEAD_DIM:]).astype(outs[index].dtype)
 
 
 def attend_near(turns, rel, q, near):
     rows, width = q[0].shape
     state = [jax.ShapeDtypeStruct((rows, wide), jnp.float32) for wide in (width, 2 * width)]
     outs = pl.pallas_call(
-        functools.partial(attend_kernel, turns, len(near), True, (), ()),
+        functools.partial(attend_kernel, turns, len(near), True, False, (), ()),
         out_shape=state * len(turns),
         in_specs=[VMEM] * (1 + len(turns) + len(near)),
         out_specs=[VMEM] * (2 * len(turns)),
@@ -189,14 +192,17 @@
     return {turn: outs[2 * index : 2 * index + 2] for index, turn in enumerate(turns)}
 
 
-def attend_far(turns, rel, q, far, stacked, alone, states):
-    return pl.pallas_call(
-        functools.partial(attend_kernel, turns, len(q), False, stacked, tuple(alone)),
+def attend(turns, rel, q, near, far, states, *after):
+    stacked, swap, alone = far
+    given = [*near, swap, *alone.values(), *(part for turn in turns for part in states.get(turn, ()))]
+    outs = pl.pallas_call(
+        functools.partial(attend_kernel, turns, len(q), bool(near), True, stacked, tuple(alone)),
         out_shape=[jax.ShapeDtypeStruct(q[0].shape, q[0].dtype)] * len(turns),
-        in_specs=[VMEM] * (2 + len(alone) + 3 * len(turns)),
+        in_specs=[VMEM] * (1 + len(turns) + len(given)) + [ANY] * len(after),
         out_specs=[VMEM] * len(turns),
         compiler_params=PARAMS,
-    )(rel, *(q[turn] for turn in turns), far, *alone.values(), *(part for turn in turns for part in states[turn]))
+    )(rel, *(q[turn] for turn in turns), *given, *after)
+    return dict(zip(turns, outs))
 
 
 def join_kernel(chips, *refs):
@@ -231,13 +237,14 @@
     q, rel = regroup(block_order, q_parts, keys.shape[0], chips)
     q = [q[0]] + [over(q[turn], turn) for turn in range(1, chips)]
     stacked = [*across[::-1], 0]
-    far = swapped(stack([near[turn] for turn in stacked]), "seq", 1)
-    alone = {turn: swapped(near[turn], "seq", 1) for turn in within}
-    states = attend_near([*across, *within, 0], rel, q, near)
-    out = {}
-    for turns in (across, [*within, 0]):
-        for turn, part in zip(turns, attend_far(turns, rel, q, far, stacked, alone, states)):
-            out[turn] = over(part, turn) if turn else part
+    swap = swapped(stack([near[turn] for turn in stacked]), "seq", 1)
+    far = (stacked, swap, {turn: swapped(near[turn], "seq", 1) for turn in within})
+    states = attend_near([*within, 0], rel, q, near)
+    done = attend(within, rel, q, (), far, states) if within else {}
+    out = {turn: over(part, turn) for turn, part in done.items()}
+    for turn in across[::-1]:
+        out[turn] = over(attend([turn], rel, q, near, far, {}, *done.values())[turn], turn)
+    out |= attend([0], rel, q, (), far, states)
     return join([out[turn] for turn in range(chips)])
 
 

time: 34.4 us -> 33 us (0.959)
  waiting for transfers between devices: 11.4 us -> 9.34 us
  Pallas kernels: 4.94 us -> 5.55 us
    ppermute x14, waiting for transfers between devices: 11.4 us -> 9.34 us  [swapped(): return lax.ppermute(block, axis, route)]
    pallas_call x3 -> x5, Pallas kernels: 2.32 us -> 2.93 us  [the longest x4 2.29 us: attend(): pl.pallas_call(functools.partial(attend_kernel, turns, len(q), bool(near)...]
  transfers between devices with their start and end apart: 14 -> 14, of which waited for: 9 -> 7; matrix products, arithmetic and copies ran while one was open for 0% -> 0% of each run, Pallas kernels for 7% -> 11%
where the time goes in v3:
time: 33 us; the launch traced here: 32.9 us
  starting transfers between devices  17.9 us (54%)
  waiting for transfers between devices  9.34 us (28%)
  Pallas kernels  5.55 us (17%)
    ppermute x14, starting transfers between devices, swapped(): return lax.ppermute(block, axis, route)  17.9 us
    ppermute x14, waiting for transfers between devices, swapped(): return lax.ppermute(block, axis, route)  9.34 us
    pallas_call x4, Pallas kernels, attend(): pl.pallas_call(functools.partial(attend_kernel, turns, len(q), bool(near)...  2.29 us
    pallas_call x1, Pallas kernels, split(): pl.pallas_call(functools.partial(split_kernel, chips), out_shape=outs, in...  1.27 us
    pallas_call x1, Pallas kernels, join(): pl.pallas_call(functools.partial(join_kernel, chips), out_shape=jax.Shape...  0.73 us
  transfers between devices with their start and end apart: 14, of which 7 were waited for; matrix products, arithmetic and copies ran while one was open for 0% of the time, Pallas kernels for 11%

profile of v3, /device:TPU:0, one launch (start us, length us, event | category | flops | bytes accessed | tf_op | source)
XLA Modules:
  0.0 32.9 jit_solution(4216609895122289889)
XLA Ops:
  0.0 1.3 %shard_map.46 = (bf16[128,512]{1,0:T(8,128)(2,1)S(1)}, bf16[128,512]{1,0:T(8,128)(2,1)S(1)}, bf16[128,512]{1,0:T(8,128)(2,1)S(1)}, bf16[128,512]{1,0:T(8,128)(2,...) custom-call(bf16[32,4096]{1,0:T(8,128)(2,1)} %q_ref.1, ...), custom_call_target="tpu_custom_call" | custom-call | tf_op jit(solution)/shard_map/pallas_call | solution.py:78
  1.3 5.1 %collective-permute-start.3 = (bf16[128,512]{1,0:T(8,128)(2,1)S(1)}, bf16[128,512]{1,0:T(8,128)(2,1)S(1)}, u32[]{:S(2)}, u32[]{:S(2)}) collective-permute-start(bf16[128,512]{1,0:T(8,128)(2,1)S(1)} %get-tuple-element.28), channel_id=1, source_target_pairs={{0,24},{4,28},{8,16},{12,20},{16,8},{20,12},{24,0},{28,4},{1,25},{... | collective-permute-start | bytes 393224 | tf_op jit(solution)/shard_map/ppermute | solution.py:30
  6.4 0.0 collective-permute-start.4
  6.4 1.5 %collective-permute-start = (bf16[32,1024]{1,0:T(8,128)(2,1)S(1)}, bf16[32,1024]{1,0:T(8,128)(2,1)S(1)}, u32[]{:S(2)}, u32[]{:S(2)}) collective-permute-start(bf16[32,1024]{1,0:T(8,128)(2,1)S(1)} %get-tuple-element.23), channel_id=1, source_target_pairs={{0,1},{1,0},{2,3},{3,2},{4,5},{5,4},{6,7},{7,6},{8,9},{9,8},{10,11... | collective-permute-start | bytes 196616 | tf_op jit(solution)/shard_map/ppermute | solution.py:30
  7.9 1.5 %collective-permute-start.1 = (bf16[32,1024]{1,0:T(8,128)(2,1)S(1)}, bf16[32,1024]{1,0:T(8,128)(2,1)S(1)}, u32[]{:S(2)}, u32[]{:S(2)}) collective-permute-start(bf16[32,1024]{1,0:T(8,128)(2,1)S(1)} %get-tuple-element.24), channel_id=1, source_target_pairs={{0,2},{1,3},{2,0},{3,1},{4,6},{5,7},{6,4},{7,5},{8,10},{9,11},{10,... | collective-permute-start | bytes 196616 | tf_op jit(solution)/shard_map/ppermute | solution.py:30
  9.4 0.5 %collective-permute-start.2 = (bf16[32,1024]{1,0:T(8,128)(2,1)S(1)}, bf16[32,1024]{1,0:T(8,128)(2,1)S(1)}, u32[]{:S(2)}, u32[]{:S(2)}) collective-permute-start(bf16[32,1024]{1,0:T(8,128)(2,1)S(1)} %get-tuple-element.25), channel_id=1, source_target_pairs={{0,3},{1,2},{2,1},{3,0},{4,7},{5,6},{6,5},{7,4},{8,11},{9,10},{10,... | collective-permute-start | bytes 196616 | tf_op jit(solution)/shard_map/ppermute | solution.py:30
  9.9 0.8 %collective-permute-done.rest_1_ = bf16[32,1024]{1,0:T(8,128)(2,1)S(1)} collective-permute-done((bf16[32,1024]{1,0:T(8,128)(2,1)S(1)}, bf16[32,1024]{1,0:T(8,128)(2,1)S(1)}, u32[]{:S(2)}, u32[]{:S(2)}) %collective-permute-start) | collective-permute-done | bytes 65568 | tf_op jit(solution)/shard_map/ppermute | solution.py:30
  10.7 0.6 %collective-permute-start.6 = (bf16[128,512]{1,0:T(8,128)(2,1)S(1)}, bf16[128,512]{1,0:T(8,128)(2,1)S(1)}, u32[]{:S(2)}, u32[]{:S(2)}) collective-permute-start(bf16[128,512]{1,0:T(8,128)(2,1)S(1)} %get-tuple-element.31), channel_id=1, source_target_pairs={{0,8},{4,12},{8,0},{12,4},{16,24},{20,28},{24,16},{28,20},{1,9},{5... | collective-permute-start | bytes 393224 | tf_op jit(solution)/shard_map/ppermute | solution.py:30
  11.3 1.6 %collective-permute-done.1.rest_2_ = bf16[32,1024]{1,0:T(8,128)(2,1)S(1)} collective-permute-done((bf16[32,1024]{1,0:T(8,128)(2,1)S(1)}, bf16[32,1024]{1,0:T(8,128)(2,1)S(1)}, u32[]{:S(2)}, u32[]{:S(2)}) %collective-permute-start.1) | collective-permute-done | bytes 65568 | tf_op jit(solution)/shard_map/ppermute | solution.py:30
  12.9 1.7 %collective-permute-done.2.rest_3_ = bf16[32,1024]{1,0:T(8,128)(2,1)S(1)} collective-permute-done((bf16[32,1024]{1,0:T(8,128)(2,1)S(1)}, bf16[32,1024]{1,0:T(8,128)(2,1)S(1)}, u32[]{:S(2)}, u32[]{:S(2)}) %collective-permute-start.2) | collective-permute-done | bytes 65568 | tf_op jit(solution)/shard_map/ppermute | solution.py:30
  14.6 0.6 %shard_map.47 = (bf16[128,256]{1,0:T(8,128)(2,1)S(1)}, bf16[128,256]{1,0:T(8,128)(2,1)S(1)}, bf16[128,256]{1,0:T(8,128)(2,1)S(1)}, bf16[128,256]{1,0:T(8,128)(2,1)S(1)}, s32[4,8,1024]{2,1,0:T(8,128)S(1)}) custom-call(s32[8]{0:T(128)S(1)} %copy-done, bf16[32,1024]{1,0:T(8,128)(2,1)S(1)} %get-tuple-element.22.rest_0_, ...), custom_call_target="tpu_custom_call" | custom-call | tf_op jit(solution)/shard_map/pallas_call | solution.py:108
  15.2 0.8 %collective-permute-start.8 = (bf16[128,256]{1,0:T(8,128)(2,1)S(1)}, bf16[128,256]{1,0:T(8,128)(2,1)S(1)}, u32[]{:S(2)}, u32[]{:S(2)}) collective-permute-start(bf16[128,256]{1,0:T(8,128)(2,1)S(1)} %get-tuple-element.32), channel_id=1, source_target_pairs={{0,8},{4,12},{8,0},{12,4},{16,24},{20,28},{24,16},{28,20},{1,9},{5... | collective-permute-start | bytes 196616 | tf_op jit(solution)/shard_map/ppermute | solution.py:30
  16.0 2.2 %collective-permute-start.10 = (bf16[128,256]{1,0:T(8,128)(2,1)S(1)}, bf16[128,256]{1,0:T(8,128)(2,1)S(1)}, u32[]{:S(2)}, u32[]{:S(2)}) collective-permute-start(bf16[128,256]{1,0:T(8,128)(2,1)S(1)} %get-tuple-element.37), channel_id=1, source_target_pairs={{0,16},{4,20},{8,24},{12,28},{16,0},{20,4},{24,8},{28,12},{1,17},{... | collective-permute-start | bytes 196616 | tf_op jit(solution)/shard_map/ppermute | solution.py:30
  18.3 0.0 collective-permute-done.3.refs_0_.rest_5_.rest_4_
  18.3 1.4 %collective-permute-start.12 = (bf16[128,256]{1,0:T(8,128)(2,1)S(1)}, bf16[128,256]{1,0:T(8,128)(2,1)S(1)}, u32[]{:S(2)}, u32[]{:S(2)}) collective-permute-start(bf16[128,256]{1,0:T(8,128)(2,1)S(1)} %get-tuple-element.38), channel_id=1, source_target_pairs={{0,24},{4,28},{8,16},{12,20},{16,8},{20,12},{24,0},{28,4},{1,25},{... | collective-permute-start | bytes 196616 | tf_op jit(solution)/shard_map/ppermute | solution.py:30
  19.7 0.1 collective-permute-start.5
  19.8 0.0 collective-permute-done.6.rest_3_.rest_2_
  19.8 0.5 %collective-permute-start.7 = (bf16[128,512]{1,0:T(8,128)(2,1)S(1)}, bf16[128,512]{1,0:T(8,128)(2,1)S(1)}, u32[]{:S(2)}, u32[]{:S(2)}) collective-permute-start(bf16[128,512]{1,0:T(8,128)(2,1)S(1)} %collective-permute-done.6.rest_3_.rest_2_), channel_id=1, source_target_pairs={{0,4},{4,0},{8,12},{12,8},{16,20},{20,16},{24,28},{28,24},{1,5},{5... | collective-permute-start | bytes 393224 | tf_op jit(solution)/shard_map/ppermute | solution.py:30
  20.3 0.0 collective-permute-done.8.rest_0_
  20.3 0.6 %shard_map.49 = (f32[128,256]{1,0:T(8,128)S(1)}, f32[128,512]{1,0:T(8,128)S(1)}, f32[128,256]{1,0:T(8,128)S(1)}, f32[128,512]{1,0:T(8,128)S(1)}) custom-call(s32[4,8,1024]{2,1,0:T(8,128)S(1)} %get-tuple-element.26.rel_ref, bf16[128,256]{1,0:T(8,128)(2,1)S(1)} %collective-permute-done.8.rest_0_, bf16[128,256]{1,0:T(8,128)(2,1)S(1)} %get-tuple-element.27.rest_1_.rest_0_, ...), custom_call_target="tpu_custom_call" | custom-call | flops 60000002048 | tf_op jit(solution)/shard_map/pallas_call | solution.py:184
  20.9 0.7 %collective-permute-done.7.rest_2_.rest_6_ = bf16[128,512]{1,0:T(8,128)(2,1)S(1)} collective-permute-done((bf16[128,512]{1,0:T(8,128)(2,1)S(1)}, bf16[128,512]{1,0:T(8,128)(2,1)S(1)}, u32[]{:S(2)}, u32[]{:S(2)}) %collective-permute-start.7) | collective-permute-done | bytes 131104 | tf_op jit(solution)/shard_map/ppermute | solution.py:30
  21.7 0.5 %shard_map.51.rest_7_ = bf16[128,256]{1,0:T(8,128)(2,1)S(1)} custom-call(s32[4,8,1024]{2,1,0:T(8,128)S(1)} %get-tuple-element.26.rel_ref, bf16[128,256]{1,0:T(8,128)(2,1)S(1)} %collective-permute-done.8.rest_0_, bf16[3,128,512]{2,1,0:T(8,128)(2,1)S(1)} %collective-permute-done.5.rest_1_.rest_5_, bf16[128,512]{1,0:T(8,128)(2,1)S(1)} %collective-permute-done.7.rest_2_.rest_6_, ...), custom_call_target="tpu_custom_call" | custom-call | tf_op jit(solution)/shard_map/pallas_call | solution.py:198
  22.2 0.7 %shard_map.52 = bf16[128,256]{1,0:T(8,128)(2,1)S(1)} custom-call(s32[4,8,1024]{2,1,0:T(8,128)S(1)} %get-tuple-element.26.rel_ref, bf16[128,256]{1,0:T(8,128)(2,1)S(1)} %collective-permute-done.10.rest_0_, bf16[128,512]{1,0:T(8,128)(2,1)S(1)} %get-tuple-element.30.refs_2_.rest_2_.rest_1_, bf16[128,512]{1,0:T(8,128)(2,1)S(1)} %collective-permute-done.6.rest_3_.rest_2_, ...), custom_call_target="tpu_custom_call" | custom-call | tf_op jit(solution)/shard_map/pallas_call | solution.py:198
  22.8 2.1 %collective-permute-start.11 = (bf16[128,256]{1,0:T(8,128)(2,1)S(1)}, bf16[128,256]{1,0:T(8,128)(2,1)S(1)}, u32[]{:S(2)}, u32[]{:S(2)}) collective-permute-start(bf16[128,256]{1,0:T(8,128)(2,1)S(1)} %shard_map.52), channel_id=1, source_target_pairs={{0,16},{4,20},{8,24},{12,28},{16,0},{20,4},{24,8},{28,12},{1,17},{... | collective-permute-start | bytes 196616 | tf_op jit(solution)/shard_map/ppermute | solution.py:30
  24.9 0.7 %shard_map.53 = bf16[128,256]{1,0:T(8,128)(2,1)S(1)} custom-call(s32[4,8,1024]{2,1,0:T(8,128)S(1)} %get-tuple-element.26.rel_ref, bf16[128,256]{1,0:T(8,128)(2,1)S(1)} %collective-permute-done.12.rest_0_, bf16[128,512]{1,0:T(8,128)(2,1)S(1)} %get-tuple-element.30.refs_2_.rest_2_.rest_1_, bf16[128,512]{1,0:T(8,128)(2,1)S(1)} %collective-permute-done.6.rest_3_.rest_2_, ...), custom_call_target="tpu_custom_call" | custom-call | tf_op jit(solution)/shard_map/pallas_call | solution.py:198
  25.6 1.4 %collective-permute-start.13 = (bf16[128,256]{1,0:T(8,128)(2,1)S(1)}, bf16[128,256]{1,0:T(8,128)(2,1)S(1)}, u32[]{:S(2)}, u32[]{:S(2)}) collective-permute-start(bf16[128,256]{1,0:T(8,128)(2,1)S(1)} %shard_map.53), channel_id=1, source_target_pairs={{0,24},{4,28},{8,16},{12,20},{16,8},{20,12},{24,0},{28,4},{1,25},{... | collective-permute-start | bytes 196616 | tf_op jit(solution)/shard_map/ppermute | solution.py:30
  26.9 0.2 collective-permute-start.9
  27.1 0.5 %shard_map.50.refs_0_ = bf16[128,256]{1,0:T(8,128)(2,1)S(1)} custom-call(s32[4,8,1024]{2,1,0:T(8,128)S(1)} %get-tuple-element.26.rel_ref, bf16[128,256]{1,0:T(8,128)(2,1)S(1)} %get-tuple-element.27.rest_1_.rest_0_, bf16[3,128,512]{2,1,0:T(8,128)(2,1)S(1)} %collective-permute-done.5.rest_1_.rest_5_, ...), custom_call_target="tpu_custom_call" | custom-call | tf_op jit(solution)/shard_map/pallas_call | solution.py:198
  27.6 1.8 %collective-permute-done.11.refs_2_ = bf16[128,256]{1,0:T(8,128)(2,1)S(1)} collective-permute-done((bf16[128,256]{1,0:T(8,128)(2,1)S(1)}, bf16[128,256]{1,0:T(8,128)(2,1)S(1)}, u32[]{:S(2)}, u32[]{:S(2)}) %collective-permute-start.11) | collective-permute-done | bytes 65568 | tf_op jit(solution)/shard_map/ppermute | solution.py:30
  29.5 2.6 %collective-permute-done.13.refs_3_ = bf16[128,256]{1,0:T(8,128)(2,1)S(1)} collective-permute-done((bf16[128,256]{1,0:T(8,128)(2,1)S(1)}, bf16[128,256]{1,0:T(8,128)(2,1)S(1)}, u32[]{:S(2)}, u32[]{:S(2)}) %collective-permute-start.13) | collective-permute-done | bytes 65568 | tf_op jit(solution)/shard_map/ppermute | solution.py:30
  32.0 0.1 collective-permute-done.9.refs_1_
  32.1 0.7 %shard_map.54 = bf16[128,1024]{1,0:T(8,128)(2,1)} custom-call(bf16[128,256]{1,0:T(8,128)(2,1)S(1)} %shard_map.50.refs_0_, bf16[128,256]{1,0:T(8,128)(2,1)S(1)} %collective-permute-done.9.refs_1_, bf16[128,256]{1,0:T(8,128)(2,1)S(1)} %collective-permute-done.11.refs_2_, bf16[128,256]{1,0:T(8,128)(2,1)S(1)} %collective-permute-done.13.refs_3_), custom_call_target="tpu_custom_call" | custom-call | tf_op jit(solution)/shard_map/pallas_call | solution.py:219
  (7 shorter events, 0.0 us)
Async XLA Ops:
  1.3 17.0 %collective-permute-start.3 = (bf16[128,512]{1,0:T(8,128)(2,1)S(1)}, bf16[128,512]{1,0:T(8,128)(2,1)S(1)}, u32[]{:S(2)}, u32[]{:S(2)}) collective-permute-start(bf16[128,512]{1,0:T(8,128)(2,1)S(1)} %get-tuple-element.28), channel_id=1, source_target_pairs={{0,24},{4,28},{8,16},{12,20},{16,8},{20,12},{24,0},{28,4},{1,25},{... | collective-permute-start | bytes 393224 | tf_op jit(solution)/shard_map/ppermute | solution.py:30
  6.4 13.3 %collective-permute-start.4 = (bf16[128,512]{1,0:T(8,128)(2,1)S(1)}, bf16[128,512]{1,0:T(8,128)(2,1)S(1)}, u32[]{:S(2)}, u32[]{:S(2)}) collective-permute-start(bf16[128,512]{1,0:T(8,128)(2,1)S(1)} %get-tuple-element.29), channel_id=1, source_target_pairs={{0,16},{4,20},{8,24},{12,28},{16,0},{20,4},{24,8},{28,12},{1,17},{... | collective-permute-start | bytes 393224 | tf_op jit(solution)/shard_map/ppermute | solution.py:30
  6.4 4.3 %collective-permute-start = (bf16[32,1024]{1,0:T(8,128)(2,1)S(1)}, bf16[32,1024]{1,0:T(8,128)(2,1)S(1)}, u32[]{:S(2)}, u32[]{:S(2)}) collective-permute-start(bf16[32,1024]{1,0:T(8,128)(2,1)S(1)} %get-tuple-element.23), channel_id=1, source_target_pairs={{0,1},{1,0},{2,3},{3,2},{4,5},{5,4},{6,7},{7,6},{8,9},{9,8},{10,11... | collective-permute-start | bytes 196616 | tf_op jit(solution)/shard_map/ppermute | solution.py:30
  7.9 5.0 %collective-permute-start.1 = (bf16[32,1024]{1,0:T(8,128)(2,1)S(1)}, bf16[32,1024]{1,0:T(8,128)(2,1)S(1)}, u32[]{:S(2)}, u32[]{:S(2)}) collective-permute-start(bf16[32,1024]{1,0:T(8,128)(2,1)S(1)} %get-tuple-element.24), channel_id=1, source_target_pairs={{0,2},{1,3},{2,0},{3,1},{4,6},{5,7},{6,4},{7,5},{8,10},{9,11},{10,... | collective-permute-start | bytes 196616 | tf_op jit(solution)/shard_map/ppermute | solution.py:30
  9.4 5.2 %collective-permute-start.2 = (bf16[32,1024]{1,0:T(8,128)(2,1)S(1)}, bf16[32,1024]{1,0:T(8,128)(2,1)S(1)}, u32[]{:S(2)}, u32[]{:S(2)}) collective-permute-start(bf16[32,1024]{1,0:T(8,128)(2,1)S(1)} %get-tuple-element.25), channel_id=1, source_target_pairs={{0,3},{1,2},{2,1},{3,0},{4,7},{5,6},{6,5},{7,4},{8,11},{9,10},{10,... | collective-permute-start | bytes 196616 | tf_op jit(solution)/shard_map/ppermute | solution.py:30
  10.7 3.9 %copy-start = (s32[8]{0:T(128)S(1)}, s32[8]{0:T(128)}, u32[]{:S(2)}) copy-start(s32[8]{0:T(128)} %order_ref.1) | copy-start | bytes 100
  10.7 9.1 %collective-permute-start.6 = (bf16[128,512]{1,0:T(8,128)(2,1)S(1)}, bf16[128,512]{1,0:T(8,128)(2,1)S(1)}, u32[]{:S(2)}, u32[]{:S(2)}) collective-permute-start(bf16[128,512]{1,0:T(8,128)(2,1)S(1)} %get-tuple-element.31), channel_id=1, source_target_pairs={{0,8},{4,12},{8,0},{12,4},{16,24},{20,28},{24,16},{28,20},{1,9},{5... | collective-permute-start | bytes 393224 | tf_op jit(solution)/shard_map/ppermute | solution.py:30
  15.2 5.1 %collective-permute-start.8 = (bf16[128,256]{1,0:T(8,128)(2,1)S(1)}, bf16[128,256]{1,0:T(8,128)(2,1)S(1)}, u32[]{:S(2)}, u32[]{:S(2)}) collective-permute-start(bf16[128,256]{1,0:T(8,128)(2,1)S(1)} %get-tuple-element.32), channel_id=1, source_target_pairs={{0,8},{4,12},{8,0},{12,4},{16,24},{20,28},{24,16},{28,20},{1,9},{5... | collective-permute-start | bytes 196616 | tf_op jit(solution)/shard_map/ppermute | solution.py:30
  16.0 6.1 %collective-permute-start.10 = (bf16[128,256]{1,0:T(8,128)(2,1)S(1)}, bf16[128,256]{1,0:T(8,128)(2,1)S(1)}, u32[]{:S(2)}, u32[]{:S(2)}) collective-permute-start(bf16[128,256]{1,0:T(8,128)(2,1)S(1)} %get-tuple-element.37), channel_id=1, source_target_pairs={{0,16},{4,20},{8,24},{12,28},{16,0},{20,4},{24,8},{28,12},{1,17},{... | collective-permute-start | bytes 196616 | tf_op jit(solution)/shard_map/ppermute | solution.py:30
  18.3 6.7 %collective-permute-start.12 = (bf16[128,256]{1,0:T(8,128)(2,1)S(1)}, bf16[128,256]{1,0:T(8,128)(2,1)S(1)}, u32[]{:S(2)}, u32[]{:S(2)}) collective-permute-start(bf16[128,256]{1,0:T(8,128)(2,1)S(1)} %get-tuple-element.38), channel_id=1, source_target_pairs={{0,24},{4,28},{8,16},{12,20},{16,8},{20,12},{24,0},{28,4},{1,25},{... | collective-permute-start | bytes 196616 | tf_op jit(solution)/shard_map/ppermute | solution.py:30
  19.7 2.0 %collective-permute-start.5 = (bf16[3,128,512]{2,1,0:T(8,128)(2,1)S(1)}, bf16[3,128,512]{2,1,0:T(8,128)(2,1)S(1)}, u32[]{:S(2)}, u32[]{:S(2)}) collective-permute-start(bf16[3,128,512]{2,1,0:T(8,128)(2,1)S(1)} %shard_map.48), channel_id=1, source_target_pairs={{0,4},{4,0},{8,12},{12,8},{16,20},{20,16},{24,28},{28,24},{1,5},{5... | collective-permute-start | bytes 1179656 | tf_op jit(solution)/shard_map/ppermute | solution.py:30
  19.8 1.9 %collective-permute-start.7 = (bf16[128,512]{1,0:T(8,128)(2,1)S(1)}, bf16[128,512]{1,0:T(8,128)(2,1)S(1)}, u32[]{:S(2)}, u32[]{:S(2)}) collective-permute-start(bf16[128,512]{1,0:T(8,128)(2,1)S(1)} %collective-permute-done.6.rest_3_.rest_2_), channel_id=1, source_target_pairs={{0,4},{4,0},{8,12},{12,8},{16,20},{20,16},{24,28},{28,24},{1,5},{5... | collective-permute-start | bytes 393224 | tf_op jit(solution)/shard_map/ppermute | solution.py:30
  22.8 6.6 %collective-permute-start.11 = (bf16[128,256]{1,0:T(8,128)(2,1)S(1)}, bf16[128,256]{1,0:T(8,128)(2,1)S(1)}, u32[]{:S(2)}, u32[]{:S(2)}) collective-permute-start(bf16[128,256]{1,0:T(8,128)(2,1)S(1)} %shard_map.52), channel_id=1, source_target_pairs={{0,16},{4,20},{8,24},{12,28},{16,0},{20,4},{24,8},{28,12},{1,17},{... | collective-permute-start | bytes 196616 | tf_op jit(solution)/shard_map/ppermute | solution.py:30
  25.6 6.5 %collective-permute-start.13 = (bf16[128,256]{1,0:T(8,128)(2,1)S(1)}, bf16[128,256]{1,0:T(8,128)(2,1)S(1)}, u32[]{:S(2)}, u32[]{:S(2)}) collective-permute-start(bf16[128,256]{1,0:T(8,128)(2,1)S(1)} %shard_map.53), channel_id=1, source_target_pairs={{0,24},{4,28},{8,16},{12,20},{16,8},{20,12},{24,0},{28,4},{1,25},{... | collective-permute-start | bytes 196616 | tf_op jit(solution)/shard_map/ppermute | solution.py:30
  26.9 5.2 %collective-permute-start.9 = (bf16[128,256]{1,0:T(8,128)(2,1)S(1)}, bf16[128,256]{1,0:T(8,128)(2,1)S(1)}, u32[]{:S(2)}, u32[]{:S(2)}) collective-permute-start(bf16[128,256]{1,0:T(8,128)(2,1)S(1)} %shard_map.51.rest_7_), channel_id=1, source_target_pairs={{0,8},{4,12},{8,0},{12,4},{16,24},{20,28},{24,16},{28,20},{1,9},{5... | collective-permute-start | bytes 196616 | tf_op jit(solution)/shard_map/ppermute | solution.py:30

commit v4 on v3

--- a/solution.py
+++ b/solution.py
@@ -86,13 +86,9 @@
     return outs[:chips], outs[chips:]
 
 
-def regroup_kernel(chips, groups, order_ref, *rest):
-    q_parts, q_refs, rel_ref = rest[:groups], rest[groups:-1], rest[-1]
-    z, core, head = place()
-    sub, (rows, width) = q_parts[0].shape[0], q_refs[0].shape
-    for turn, out in enumerate(q_refs):
-        for step, part in enumerate(q_parts):
-            out[cut(head ^ step, sub), :] = part[:, cut(z ^ turn, width)]
+def measure_kernel(chips, rows, order_ref, *rest):
+    rel_ref = rest[-1]
+    z, core, _ = place()
     inner = lax.broadcasted_iota(jnp.int32, (8, rows), 1)
     starts = [
         order_ref[(z ^ (slot % chips)) * CORES + (core ^ (slot // chips))] * rows for slot in range(chips * CORES)
@@ -102,17 +98,33 @@
             rel_ref[turn, :, pl.ds(slot * rows, rows)] = inner + (start - starts[turn])
 
 
-def regroup(block_order, q_parts, rows, chips):
-    outs = [jax.ShapeDtypeStruct((rows, q_parts[0].shape[1] // chips), q_parts[0].dtype)] * chips
-    outs += [jax.ShapeDtypeStruct((chips, 8, rows * chips * CORES), jnp.int32)]
-    outs = pl.pallas_call(
-        functools.partial(regroup_kernel, chips, len(q_parts)),
-        out_shape=outs,
-        in_specs=[SMEM] + [VMEM] * len(q_parts),
-        out_specs=[VMEM] * len(outs),
-        compiler_params=PARAMS,
-    )(block_order, *q_parts)
-    return outs[:-1], outs[-1]
+def measure(block_order, rows, chips, *after):
+    return pl.pallas_call(
+        functools.partial(measure_kernel, chips, rows),
+        out_shape=jax.ShapeDtypeStruct((chips, 8, rows * chips * CORES), jnp.int32),
+        in_specs=[SMEM] + [ANY] * len(after),
+        out_specs=VMEM,
+        compiler_params=PARAMS,
+    )(block_order, *after)
+
+
+def regroup_kernel(groups, *refs):
+    q_parts, q_refs = refs[:groups], refs[groups + 1 :]
+    z, _, head = place()
+    sub, (rows, width) = q_parts[0].shape[0], q_refs[0].shape
+    for turn, out in enumerate(q_refs):
+        for step, part in enumerate(q_parts):
+            out[cut(head ^ step, sub), :] = part[:, cut(z ^ turn, width)]
+
+
+def regroup(q_parts, rows, chips, after):
+    return pl.pallas_call(
+        functools.partial(regroup_kernel, len(q_parts)),
+        out_shape=[jax.ShapeDtypeStruct((rows, q_parts[0].shape[1] // chips), q_parts[0].dtype)] * chips,
+        in_specs=[VMEM] * len(q_parts) + [ANY],
+        out_specs=[VMEM] * chips,
+        compiler_params=PARAMS,
+    )(*q_parts, after)
 
 
 def stack_kernel(*refs):
@@ -234,7 +246,8 @@
     kv, q_cut = split(queries, keys, values, chips)
     near = [kv[0]] + [over(kv[turn], turn) for turn in range(1, chips)]
     q_parts = [q_cut[0]] + [swapped(q_cut[step], "head", step) for step in range(1, groups)]
-    q, rel = regroup(block_order, q_parts, keys.shape[0], chips)
+    rel = measure(block_order, keys.shape[0], chips, q_parts[1])
+    q = regroup(q_parts, keys.shape[0], chips, rel)
     q = [q[0]] + [over(q[turn], turn) for turn in range(1, chips)]
     stacked = [*across[::-1], 0]
     swap = swapped(stack([near[turn] for turn in stacked]), "seq", 1)

time: 33 us -> 32.5 us (0.985)
  starting transfers between devices: 17.9 us -> 17.5 us
    ppermute x14, starting transfers between devices: 17.9 us -> 17.5 us  [swapped(): return lax.ppermute(block, axis, route)]
  transfers between devices with their start and end apart: 14 -> 14, of which waited for: 7 -> 8; matrix products, arithmetic and copies ran while one was open for 0% -> 0% of each run, Pallas kernels for 11% -> 11%
where the time goes in v4:
time: 32.5 us; the launch traced here: 32.3 us
  starting transfers between devices  17.5 us (54%)
  waiting for transfers between devices  9.18 us (28%)
  Pallas kernels  5.56 us (17%)
    ppermute x14, starting transfers between devices, swapped(): return lax.ppermute(block, axis, route)  17.5 us
    ppermute x14, waiting for transfers between devices, swapped(): return lax.ppermute(block, axis, route)  9.18 us
    pallas_call x4, Pallas kernels, attend(): pl.pallas_call(functools.partial(attend_kernel, turns, len(q), bool(near)...  2.3 us
    pallas_call x1, Pallas kernels, split(): pl.pallas_call(functools.partial(split_kernel, chips), out_shape=outs, in...  1.27 us
    pallas_call x1, Pallas kernels, join(): pl.pallas_call(functools.partial(join_kernel, chips), out_shape=jax.Shape...  0.73 us
  transfers between devices with their start and end apart: 14, of which 8 were waited for; matrix products, arithmetic and copies ran while one was open for 0% of the time, Pallas kernels for 11%

profile of v4, /device:TPU:0, one launch (start us, length us, event | category | flops | bytes accessed | tf_op | source)
XLA Modules:
  0.0 32.3 jit_solution(5249836096886155211)
XLA Ops:
  0.0 1.3 %shard_map.46 = (bf16[128,512]{1,0:T(8,128)(2,1)S(1)}, bf16[128,512]{1,0:T(8,128)(2,1)S(1)}, bf16[128,512]{1,0:T(8,128)(2,1)S(1)}, bf16[128,512]{1,0:T(8,128)(2,...) custom-call(bf16[32,4096]{1,0:T(8,128)(2,1)} %q_ref.1, ...), custom_call_target="tpu_custom_call" | custom-call | tf_op jit(solution)/shard_map/pallas_call | solution.py:78
  1.3 5.1 %collective-permute-start.3 = (bf16[128,512]{1,0:T(8,128)(2,1)S(1)}, bf16[128,512]{1,0:T(8,128)(2,1)S(1)}, u32[]{:S(2)}, u32[]{:S(2)}) collective-permute-start(bf16[128,512]{1,0:T(8,128)(2,1)S(1)} %get-tuple-element.26), channel_id=1, source_target_pairs={{0,24},{4,28},{8,16},{12,20},{16,8},{20,12},{24,0},{28,4},{1,25},{... | collective-permute-start | bytes 393224 | tf_op jit(solution)/shard_map/ppermute | solution.py:30
  6.4 1.5 %collective-permute-start = (bf16[32,1024]{1,0:T(8,128)(2,1)S(1)}, bf16[32,1024]{1,0:T(8,128)(2,1)S(1)}, u32[]{:S(2)}, u32[]{:S(2)}) collective-permute-start(bf16[32,1024]{1,0:T(8,128)(2,1)S(1)} %get-tuple-element.21), channel_id=1, source_target_pairs={{0,1},{1,0},{2,3},{3,2},{4,5},{5,4},{6,7},{7,6},{8,9},{9,8},{10,11... | collective-permute-start | bytes 196616 | tf_op jit(solution)/shard_map/ppermute | solution.py:30
  7.9 1.5 %collective-permute-start.1 = (bf16[32,1024]{1,0:T(8,128)(2,1)S(1)}, bf16[32,1024]{1,0:T(8,128)(2,1)S(1)}, u32[]{:S(2)}, u32[]{:S(2)}) collective-permute-start(bf16[32,1024]{1,0:T(8,128)(2,1)S(1)} %get-tuple-element.23), channel_id=1, source_target_pairs={{0,2},{1,3},{2,0},{3,1},{4,6},{5,7},{6,4},{7,5},{8,10},{9,11},{10,... | collective-permute-start | bytes 196616 | tf_op jit(solution)/shard_map/ppermute | solution.py:30
  9.4 0.5 %collective-permute-start.2 = (bf16[32,1024]{1,0:T(8,128)(2,1)S(1)}, bf16[32,1024]{1,0:T(8,128)(2,1)S(1)}, u32[]{:S(2)}, u32[]{:S(2)}) collective-permute-start(bf16[32,1024]{1,0:T(8,128)(2,1)S(1)} %get-tuple-element.24), channel_id=1, source_target_pairs={{0,3},{1,2},{2,1},{3,0},{4,7},{5,6},{6,5},{7,4},{8,11},{9,10},{10,... | collective-permute-start | bytes 196616 | tf_op jit(solution)/shard_map/ppermute | solution.py:30
  9.9 0.8 %collective-permute-done.rest_0_.refs_1_ = bf16[32,1024]{1,0:T(8,128)(2,1)S(1)} collective-permute-done((bf16[32,1024]{1,0:T(8,128)(2,1)S(1)}, bf16[32,1024]{1,0:T(8,128)(2,1)S(1)}, u32[]{:S(2)}, u32[]{:S(2)}) %collective-permute-start) | collective-permute-done | bytes 65568 | tf_op jit(solution)/shard_map/ppermute | solution.py:30
  10.7 0.6 %collective-permute-start.6 = (bf16[128,512]{1,0:T(8,128)(2,1)S(1)}, bf16[128,512]{1,0:T(8,128)(2,1)S(1)}, u32[]{:S(2)}, u32[]{:S(2)}) collective-permute-start(bf16[128,512]{1,0:T(8,128)(2,1)S(1)} %get-tuple-element.29), channel_id=1, source_target_pairs={{0,8},{4,12},{8,0},{12,4},{16,24},{20,28},{24,16},{28,20},{1,9},{5... | collective-permute-start | bytes 393224 | tf_op jit(solution)/shard_map/ppermute | solution.py:30
  11.3 0.6 %shard_map.47.refs_4_.rel_ref = s32[4,8,1024]{2,1,0:T(8,128)S(1)} custom-call(s32[8]{0:T(128)S(1)} %copy-done, bf16[32,1024]{1,0:T(8,128)(2,1)S(1)} %collective-permute-done.rest_0_.refs_1_), custom_call_target="tpu_custom_call" | custom-call | tf_op jit(solution)/shard_map/pallas_call | solution.py:102
  11.9 1.0 %collective-permute-done.1.refs_2_ = bf16[32,1024]{1,0:T(8,128)(2,1)S(1)} collective-permute-done((bf16[32,1024]{1,0:T(8,128)(2,1)S(1)}, bf16[32,1024]{1,0:T(8,128)(2,1)S(1)}, u32[]{:S(2)}, u32[]{:S(2)}) %collective-permute-start.1) | collective-permute-done | bytes 65568 | tf_op jit(solution)/shard_map/ppermute | solution.py:30
  12.9 1.7 %collective-permute-done.2.refs_3_ = bf16[32,1024]{1,0:T(8,128)(2,1)S(1)} collective-permute-done((bf16[32,1024]{1,0:T(8,128)(2,1)S(1)}, bf16[32,1024]{1,0:T(8,128)(2,1)S(1)}, u32[]{:S(2)}, u32[]{:S(2)}) %collective-permute-start.2) | collective-permute-done | bytes 65568 | tf_op jit(solution)/shard_map/ppermute | solution.py:30
  14.6 0.8 %collective-permute-start.8 = (bf16[128,256]{1,0:T(8,128)(2,1)S(1)}, bf16[128,256]{1,0:T(8,128)(2,1)S(1)}, u32[]{:S(2)}, u32[]{:S(2)}) collective-permute-start(bf16[128,256]{1,0:T(8,128)(2,1)S(1)} %get-tuple-element.30), channel_id=1, source_target_pairs={{0,8},{4,12},{8,0},{12,4},{16,24},{20,28},{24,16},{28,20},{1,9},{5... | collective-permute-start | bytes 196616 | tf_op jit(solution)/shard_map/ppermute | solution.py:30
  15.5 2.2 %collective-permute-start.10 = (bf16[128,256]{1,0:T(8,128)(2,1)S(1)}, bf16[128,256]{1,0:T(8,128)(2,1)S(1)}, u32[]{:S(2)}, u32[]{:S(2)}) collective-permute-start(bf16[128,256]{1,0:T(8,128)(2,1)S(1)} %get-tuple-element.35), channel_id=1, source_target_pairs={{0,16},{4,20},{8,24},{12,28},{16,0},{20,4},{24,8},{28,12},{1,17},{... | collective-permute-start | bytes 196616 | tf_op jit(solution)/shard_map/ppermute | solution.py:30
  17.7 1.4 %collective-permute-start.12 = (bf16[128,256]{1,0:T(8,128)(2,1)S(1)}, bf16[128,256]{1,0:T(8,128)(2,1)S(1)}, u32[]{:S(2)}, u32[]{:S(2)}) collective-permute-start(bf16[128,256]{1,0:T(8,128)(2,1)S(1)} %get-tuple-element.36), channel_id=1, source_target_pairs={{0,24},{4,28},{8,16},{12,20},{16,8},{20,12},{24,0},{28,4},{1,25},{... | collective-permute-start | bytes 196616 | tf_op jit(solution)/shard_map/ppermute | solution.py:30
  19.1 0.0 collective-permute-done.4.refs_1_.rest_4_.rest_3_
  19.1 0.1 collective-permute-start.5
  19.2 0.4 %collective-permute-done.6.rest_3_.rest_2_ = bf16[128,512]{1,0:T(8,128)(2,1)S(1)} collective-permute-done((bf16[128,512]{1,0:T(8,128)(2,1)S(1)}, bf16[128,512]{1,0:T(8,128)(2,1)S(1)}, u32[]{:S(2)}, u32[]{:S(2)}) %collective-permute-start.6) | collective-permute-done | bytes 131104 | tf_op jit(solution)/shard_map/ppermute | solution.py:30
  19.6 0.1 collective-permute-start.7
  19.7 1.9 %collective-permute-done.8.rest_0_ = bf16[128,256]{1,0:T(8,128)(2,1)S(1)} collective-permute-done((bf16[128,256]{1,0:T(8,128)(2,1)S(1)}, bf16[128,256]{1,0:T(8,128)(2,1)S(1)}, u32[]{:S(2)}, u32[]{:S(2)}) %collective-permute-start.8) | collective-permute-done | bytes 65568 | tf_op jit(solution)/shard_map/ppermute | solution.py:30
  21.6 0.6 %shard_map.50 = (f32[128,256]{1,0:T(8,128)S(1)}, f32[128,512]{1,0:T(8,128)S(1)}, f32[128,256]{1,0:T(8,128)S(1)}, f32[128,512]{1,0:T(8,128)S(1)}) custom-call(s32[4,8,1024]{2,1,0:T(8,128)S(1)} %shard_map.47.refs_4_.rel_ref, bf16[128,256]{1,0:T(8,128)(2,1)S(1)} %collective-permute-done.8.rest_0_, bf16[128,256]{1,0:T(8,128)(2,1)S(1)} %get-tuple-element.25.rest_1_.rest_0_, ...), custom_call_target="tpu_custom_call" | custom-call | flops 60000002048 | tf_op jit(solution)/shard_map/pallas_call | solution.py:196
  22.2 0.0 collective-permute-done.7.rest_2_.rest_6_
  22.2 0.0 collective-permute-done.5.rest_1_.rest_5_
  22.2 0.5 %shard_map.52.rest_7_ = bf16[128,256]{1,0:T(8,128)(2,1)S(1)} custom-call(s32[4,8,1024]{2,1,0:T(8,128)S(1)} %shard_map.47.refs_4_.rel_ref, bf16[128,256]{1,0:T(8,128)(2,1)S(1)} %collective-permute-done.8.rest_0_, bf16[3,128,512]{2,1,0:T(8,128)(2,1)S(1)} %collective-permute-done.5.rest_1_.rest_5_, bf16[128,512]{1,0:T(8,128)(2,1)S(1)} %collective-permute-done.7.rest_2_.rest_6_, ...), custom_call_target="tpu_custom_call" | custom-call | tf_op jit(solution)/shard_map/pallas_call | solution.py:210
  22.8 0.7 %shard_map.53 = bf16[128,256]{1,0:T(8,128)(2,1)S(1)} custom-call(s32[4,8,1024]{2,1,0:T(8,128)S(1)} %shard_map.47.refs_4_.rel_ref, bf16[128,256]{1,0:T(8,128)(2,1)S(1)} %collective-permute-done.10.rest_0_, bf16[128,512]{1,0:T(8,128)(2,1)S(1)} %get-tuple-element.28.refs_2_.rest_2_.rest_1_, bf16[128,512]{1,0:T(8,128)(2,1)S(1)} %collective-permute-done.6.rest_3_.rest_2_, ...), custom_call_target="tpu_custom_call" | custom-call | tf_op jit(solution)/shard_map/pallas_call | solution.py:210
  23.4 0.9 %collective-permute-start.11 = (bf16[128,256]{1,0:T(8,128)(2,1)S(1)}, bf16[128,256]{1,0:T(8,128)(2,1)S(1)}, u32[]{:S(2)}, u32[]{:S(2)}) collective-permute-start(bf16[128,256]{1,0:T(8,128)(2,1)S(1)} %shard_map.53), channel_id=1, source_target_pairs={{0,16},{4,20},{8,24},{12,28},{16,0},{20,4},{24,8},{28,12},{1,17},{... | collective-permute-start | bytes 196616 | tf_op jit(solution)/shard_map/ppermute | solution.py:30
  24.3 0.7 %shard_map.54 = bf16[128,256]{1,0:T(8,128)(2,1)S(1)} custom-call(s32[4,8,1024]{2,1,0:T(8,128)S(1)} %shard_map.47.refs_4_.rel_ref, bf16[128,256]{1,0:T(8,128)(2,1)S(1)} %collective-permute-done.12.rest_0_, bf16[128,512]{1,0:T(8,128)(2,1)S(1)} %get-tuple-element.28.refs_2_.rest_2_.rest_1_, bf16[128,512]{1,0:T(8,128)(2,1)S(1)} %collective-permute-done.6.rest_3_.rest_2_, ...), custom_call_target="tpu_custom_call" | custom-call | tf_op jit(solution)/shard_map/pallas_call | solution.py:210
  25.0 1.5 %collective-permute-start.13 = (bf16[128,256]{1,0:T(8,128)(2,1)S(1)}, bf16[128,256]{1,0:T(8,128)(2,1)S(1)}, u32[]{:S(2)}, u32[]{:S(2)}) collective-permute-start(bf16[128,256]{1,0:T(8,128)(2,1)S(1)} %shard_map.54), channel_id=1, source_target_pairs={{0,24},{4,28},{8,16},{12,20},{16,8},{20,12},{24,0},{28,4},{1,25},{... | collective-permute-start | bytes 196616 | tf_op jit(solution)/shard_map/ppermute | solution.py:30
  26.5 1.2 %collective-permute-start.9 = (bf16[128,256]{1,0:T(8,128)(2,1)S(1)}, bf16[128,256]{1,0:T(8,128)(2,1)S(1)}, u32[]{:S(2)}, u32[]{:S(2)}) collective-permute-start(bf16[128,256]{1,0:T(8,128)(2,1)S(1)} %shard_map.52.rest_7_), channel_id=1, source_target_pairs={{0,8},{4,12},{8,0},{12,4},{16,24},{20,28},{24,16},{28,20},{1,9},{5... | collective-permute-start | bytes 196616 | tf_op jit(solution)/shard_map/ppermute | solution.py:30
  27.7 0.5 %shard_map.51.refs_0_ = bf16[128,256]{1,0:T(8,128)(2,1)S(1)} custom-call(s32[4,8,1024]{2,1,0:T(8,128)S(1)} %shard_map.47.refs_4_.rel_ref, bf16[128,256]{1,0:T(8,128)(2,1)S(1)} %get-tuple-element.25.rest_1_.rest_0_, bf16[3,128,512]{2,1,0:T(8,128)(2,1)S(1)} %collective-permute-done.5.rest_1_.rest_5_, ...), custom_call_target="tpu_custom_call" | custom-call | tf_op jit(solution)/shard_map/pallas_call | solution.py:210
  28.2 2.0 %collective-permute-done.11.refs_2_ = bf16[128,256]{1,0:T(8,128)(2,1)S(1)} collective-permute-done((bf16[128,256]{1,0:T(8,128)(2,1)S(1)}, bf16[128,256]{1,0:T(8,128)(2,1)S(1)}, u32[]{:S(2)}, u32[]{:S(2)}) %collective-permute-start.11) | collective-permute-done | bytes 65568 | tf_op jit(solution)/shard_map/ppermute | solution.py:30
  30.2 1.3 %collective-permute-done.13.refs_3_ = bf16[128,256]{1,0:T(8,128)(2,1)S(1)} collective-permute-done((bf16[128,256]{1,0:T(8,128)(2,1)S(1)}, bf16[128,256]{1,0:T(8,128)(2,1)S(1)}, u32[]{:S(2)}, u32[]{:S(2)}) %collective-permute-start.13) | collective-permute-done | bytes 65568 | tf_op jit(solution)/shard_map/ppermute | solution.py:30
  31.5 0.1 collective-permute-done.9.refs_1_
  31.6 0.7 %shard_map.55 = bf16[128,1024]{1,0:T(8,128)(2,1)} custom-call(bf16[128,256]{1,0:T(8,128)(2,1)S(1)} %shard_map.51.refs_0_, bf16[128,256]{1,0:T(8,128)(2,1)S(1)} %collective-permute-done.9.refs_1_, bf16[128,256]{1,0:T(8,128)(2,1)S(1)} %collective-permute-done.11.refs_2_, bf16[128,256]{1,0:T(8,128)(2,1)S(1)} %collective-permute-done.13.refs_3_), custom_call_target="tpu_custom_call" | custom-call | tf_op jit(solution)/shard_map/pallas_call | solution.py:231
  (8 shorter events, 0.1 us)
Async XLA Ops:
  1.3 16.4 %collective-permute-start.3 = (bf16[128,512]{1,0:T(8,128)(2,1)S(1)}, bf16[128,512]{1,0:T(8,128)(2,1)S(1)}, u32[]{:S(2)}, u32[]{:S(2)}) collective-permute-start(bf16[128,512]{1,0:T(8,128)(2,1)S(1)} %get-tuple-element.26), channel_id=1, source_target_pairs={{0,24},{4,28},{8,16},{12,20},{16,8},{20,12},{24,0},{28,4},{1,25},{... | collective-permute-start | bytes 393224 | tf_op jit(solution)/shard_map/ppermute | solution.py:30
  6.4 12.7 %collective-permute-start.4 = (bf16[128,512]{1,0:T(8,128)(2,1)S(1)}, bf16[128,512]{1,0:T(8,128)(2,1)S(1)}, u32[]{:S(2)}, u32[]{:S(2)}) collective-permute-start(bf16[128,512]{1,0:T(8,128)(2,1)S(1)} %get-tuple-element.27), channel_id=1, source_target_pairs={{0,16},{4,20},{8,24},{12,28},{16,0},{20,4},{24,8},{28,12},{1,17},{... | collective-permute-start | bytes 393224 | tf_op jit(solution)/shard_map/ppermute | solution.py:30
  6.4 4.3 %collective-permute-start = (bf16[32,1024]{1,0:T(8,128)(2,1)S(1)}, bf16[32,1024]{1,0:T(8,128)(2,1)S(1)}, u32[]{:S(2)}, u32[]{:S(2)}) collective-permute-start(bf16[32,1024]{1,0:T(8,128)(2,1)S(1)} %get-tuple-element.21), channel_id=1, source_target_pairs={{0,1},{1,0},{2,3},{3,2},{4,5},{5,4},{6,7},{7,6},{8,9},{9,8},{10,11... | collective-permute-start | bytes 196616 | tf_op jit(solution)/shard_map/ppermute | solution.py:30
  7.9 5.0 %collective-permute-start.1 = (bf16[32,1024]{1,0:T(8,128)(2,1)S(1)}, bf16[32,1024]{1,0:T(8,128)(2,1)S(1)}, u32[]{:S(2)}, u32[]{:S(2)}) collective-permute-start(bf16[32,1024]{1,0:T(8,128)(2,1)S(1)} %get-tuple-element.23), channel_id=1, source_target_pairs={{0,2},{1,3},{2,0},{3,1},{4,6},{5,7},{6,4},{7,5},{8,10},{9,11},{10,... | collective-permute-start | bytes 196616 | tf_op jit(solution)/shard_map/ppermute | solution.py:30
  9.4 1.9 %copy-start = (s32[8]{0:T(128)S(1)}, s32[8]{0:T(128)}, u32[]{:S(2)}) copy-start(s32[8]{0:T(128)} %order_ref.1) | copy-start | bytes 100
  9.4 5.2 %collective-permute-start.2 = (bf16[32,1024]{1,0:T(8,128)(2,1)S(1)}, bf16[32,1024]{1,0:T(8,128)(2,1)S(1)}, u32[]{:S(2)}, u32[]{:S(2)}) collective-permute-start(bf16[32,1024]{1,0:T(8,128)(2,1)S(1)} %get-tuple-element.24), channel_id=1, source_target_pairs={{0,3},{1,2},{2,1},{3,0},{4,7},{5,6},{6,5},{7,4},{8,11},{9,10},{10,... | collective-permute-start | bytes 196616 | tf_op jit(solution)/shard_map/ppermute | solution.py:30
  10.7 8.9 %collective-permute-start.6 = (bf16[128,512]{1,0:T(8,128)(2,1)S(1)}, bf16[128,512]{1,0:T(8,128)(2,1)S(1)}, u32[]{:S(2)}, u32[]{:S(2)}) collective-permute-start(bf16[128,512]{1,0:T(8,128)(2,1)S(1)} %get-tuple-element.29), channel_id=1, source_target_pairs={{0,8},{4,12},{8,0},{12,4},{16,24},{20,28},{24,16},{28,20},{1,9},{5... | collective-permute-start | bytes 393224 | tf_op jit(solution)/shard_map/ppermute | solution.py:30
  14.6 7.0 %collective-permute-start.8 = (bf16[128,256]{1,0:T(8,128)(2,1)S(1)}, bf16[128,256]{1,0:T(8,128)(2,1)S(1)}, u32[]{:S(2)}, u32[]{:S(2)}) collective-permute-start(bf16[128,256]{1,0:T(8,128)(2,1)S(1)} %get-tuple-element.30), channel_id=1, source_target_pairs={{0,8},{4,12},{8,0},{12,4},{16,24},{20,28},{24,16},{28,20},{1,9},{5... | collective-permute-start | bytes 196616 | tf_op jit(solution)/shard_map/ppermute | solution.py:30
  15.5 7.3 %collective-permute-start.10 = (bf16[128,256]{1,0:T(8,128)(2,1)S(1)}, bf16[128,256]{1,0:T(8,128)(2,1)S(1)}, u32[]{:S(2)}, u32[]{:S(2)}) collective-permute-start(bf16[128,256]{1,0:T(8,128)(2,1)S(1)} %get-tuple-element.35), channel_id=1, source_target_pairs={{0,16},{4,20},{8,24},{12,28},{16,0},{20,4},{24,8},{28,12},{1,17},{... | collective-permute-start | bytes 196616 | tf_op jit(solution)/shard_map/ppermute | solution.py:30
  17.7 6.7 %collective-permute-start.12 = (bf16[128,256]{1,0:T(8,128)(2,1)S(1)}, bf16[128,256]{1,0:T(8,128)(2,1)S(1)}, u32[]{:S(2)}, u32[]{:S(2)}) collective-permute-start(bf16[128,256]{1,0:T(8,128)(2,1)S(1)} %get-tuple-element.36), channel_id=1, source_target_pairs={{0,24},{4,28},{8,16},{12,20},{16,8},{20,12},{24,0},{28,4},{1,25},{... | collective-permute-start | bytes 196616 | tf_op jit(solution)/shard_map/ppermute | solution.py:30
  19.1 3.1 %collective-permute-start.5 = (bf16[3,128,512]{2,1,0:T(8,128)(2,1)S(1)}, bf16[3,128,512]{2,1,0:T(8,128)(2,1)S(1)}, u32[]{:S(2)}, u32[]{:S(2)}) collective-permute-start(bf16[3,128,512]{2,1,0:T(8,128)(2,1)S(1)} %shard_map.49), channel_id=1, source_target_pairs={{0,4},{4,0},{8,12},{12,8},{16,20},{20,16},{24,28},{28,24},{1,5},{5... | collective-permute-start | bytes 1179656 | tf_op jit(solution)/shard_map/ppermute | solution.py:30
  19.6 2.7 %collective-permute-start.7 = (bf16[128,512]{1,0:T(8,128)(2,1)S(1)}, bf16[128,512]{1,0:T(8,128)(2,1)S(1)}, u32[]{:S(2)}, u32[]{:S(2)}) collective-permute-start(bf16[128,512]{1,0:T(8,128)(2,1)S(1)} %collective-permute-done.6.rest_3_.rest_2_), channel_id=1, source_target_pairs={{0,4},{4,0},{8,12},{12,8},{16,20},{20,16},{24,28},{28,24},{1,5},{5... | collective-permute-start | bytes 393224 | tf_op jit(solution)/shard_map/ppermute | solution.py:30
  23.4 6.8 %collective-permute-start.11 = (bf16[128,256]{1,0:T(8,128)(2,1)S(1)}, bf16[128,256]{1,0:T(8,128)(2,1)S(1)}, u32[]{:S(2)}, u32[]{:S(2)}) collective-permute-start(bf16[128,256]{1,0:T(8,128)(2,1)S(1)} %shard_map.53), channel_id=1, source_target_pairs={{0,16},{4,20},{8,24},{12,28},{16,0},{20,4},{24,8},{28,12},{1,17},{... | collective-permute-start | bytes 196616 | tf_op jit(solution)/shard_map/ppermute | solution.py:30
  25.0 6.5 %collective-permute-start.13 = (bf16[128,256]{1,0:T(8,128)(2,1)S(1)}, bf16[128,256]{1,0:T(8,128)(2,1)S(1)}, u32[]{:S(2)}, u32[]{:S(2)}) collective-permute-start(bf16[128,256]{1,0:T(8,128)(2,1)S(1)} %shard_map.54), channel_id=1, source_target_pairs={{0,24},{4,28},{8,16},{12,20},{16,8},{20,12},{24,0},{28,4},{1,25},{... | collective-permute-start | bytes 196616 | tf_op jit(solution)/shard_map/ppermute | solution.py:30
  26.5 5.1 %collective-permute-start.9 = (bf16[128,256]{1,0:T(8,128)(2,1)S(1)}, bf16[128,256]{1,0:T(8,128)(2,1)S(1)}, u32[]{:S(2)}, u32[]{:S(2)}) collective-permute-start(bf16[128,256]{1,0:T(8,128)(2,1)S(1)} %shard_map.52.rest_7_), channel_id=1, source_target_pairs={{0,8},{4,12},{8,0},{12,4},{16,24},{20,28},{24,16},{28,20},{1,9},{5... | collective-permute-start | bytes 196616 | tf_op jit(solution)/shard_map/ppermute | solution.py:30

commit v5 on v4

--- a/solution.py
+++ b/solution.py
@@ -58,37 +58,46 @@
     ]
 
 
-def split_kernel(chips, q_ref, k_ref, v_ref, *rest):
-    kv_refs, q_refs, sem = rest[:chips], rest[chips:-1], rest[-1]
+def split_kernel(turns, q_ref, k_ref, v_ref, *rest):
+    kv_refs, q_refs, sem = rest[: len(turns)], rest[len(turns) : -1], rest[-1]
     z, _, head = place()
     pairs = []
-    for turn in [*range(1, chips), 0]:
-        pairs += cut_pairs(k_ref, v_ref, z ^ turn, kv_refs[turn])
-    for step, out in enumerate(q_refs):
+    for turn, out in zip(turns, kv_refs):
+        pairs += cut_pairs(k_ref, v_ref, z ^ turn, out)
+    for step, out in enumerate(q_refs, 1):
         pairs.append((q_ref.at[:, cut(head ^ step, out.shape[1])], out))
     for one in copy_all(pairs, sem):
         one.wait()
 
 
-def split(queries, keys, values, chips):
+def split(queries, keys, values, turns, chips):
     rows, width = keys.shape
-    groups = queries.shape[1] // width
-    outs = [jax.ShapeDtypeStruct((rows, 2 * width // chips), keys.dtype)] * chips
-    outs += [jax.ShapeDtypeStruct((queries.shape[0], width), queries.dtype)] * groups
+    others = queries.shape[1] // width - 1
+    outs = [jax.ShapeDtypeStruct((rows, 2 * width // chips), keys.dtype)] * len(turns)
+    outs += [jax.ShapeDtypeStruct((queries.shape[0], width), queries.dtype)] * others
     outs = pl.pallas_call(
-        functools.partial(split_kernel, chips),
+        functools.partial(split_kernel, turns),
         out_shape=outs,
         in_specs=[HBM] * 3,
         out_specs=[ANY] * len(outs),
-        scratch_shapes=[pltpu.SemaphoreType.DMA((2 * chips + groups,))],
-        compiler_params=PARAMS,
-    )(*(pltpu.with_memory_space_constraint(x, pltpu.HBM) for x in (queries, keys, values)))
-    return outs[:chips], outs[chips:]
-
-
-def measure_kernel(chips, rows, order_ref, *rest):
-    rel_ref = rest[-1]
-    z, core, _ = place()
+        scratch_shapes=[pltpu.SemaphoreType.DMA((2 * len(turns) + others,))],
+        compiler_params=PARAMS,
+    )(*in_hbm(queries, keys, values))
+    return dict(zip(turns, outs)), outs[len(turns) :]
+
+
+def in_hbm(*arrays):
+    return [pltpu.with_memory_space_constraint(x, pltpu.HBM) for x in arrays]
+
+
+def measure_kernel(turns, chips, order_ref, q_ref, k_ref, v_ref, _, *rest):
+    kv_refs, q_out, rel_ref, sem = rest[: len(turns)], rest[-3], rest[-2], rest[-1]
+    z, core, head = place()
+    rows = k_ref.shape[0]
+    pairs = [(q_ref.at[:, cut(head, q_out.shape[1])], q_out)]
+    for turn, out in zip(turns, kv_refs):
+        pairs += cut_pairs(k_ref, v_ref, z ^ turn, out)
+    copies = copy_all(pairs, sem)
     inner = lax.broadcasted_iota(jnp.int32, (8, rows), 1)
     starts = [
         order_ref[(z ^ (slot % chips)) * CORES + (core ^ (slot // chips))] * rows for slot in range(chips * CORES)
@@ -96,16 +105,26 @@
     for turn in range(chips):
         for slot, start in enumerate(starts):
             rel_ref[turn, :, pl.ds(slot * rows, rows)] = inner + (start - starts[turn])
-
-
-def measure(block_order, rows, chips, *after):
-    return pl.pallas_call(
-        functools.partial(measure_kernel, chips, rows),
-        out_shape=jax.ShapeDtypeStruct((chips, 8, rows * chips * CORES), jnp.int32),
-        in_specs=[SMEM] + [ANY] * len(after),
-        out_specs=VMEM,
-        compiler_params=PARAMS,
-    )(block_order, *after)
+    for one in copies:
+        one.wait()
+
+
+def measure(block_order, queries, keys, values, turns, chips, after):
+    rows, width = keys.shape
+    outs = [jax.ShapeDtypeStruct((rows, 2 * width // chips), keys.dtype)] * len(turns)
+    outs += [
+        jax.ShapeDtypeStruct((queries.shape[0], width), queries.dtype),
+        jax.ShapeDtypeStruct((chips, 8, rows * chips * CORES), jnp.int32),
+    ]
+    outs = pl.pallas_call(
+        functools.partial(measure_kernel, turns, chips),
+        out_shape=outs,
+        in_specs=[SMEM] + [HBM] * 3 + [ANY],
+        out_specs=[ANY] * (len(turns) + 1) + [VMEM],
+        scratch_shapes=[pltpu.SemaphoreType.DMA((2 * len(turns) + 1,))],
+        compiler_params=PARAMS,
+    )(block_order, *in_hbm(queries, keys, values), after)
+    return dict(zip(turns, outs)), outs[-2], outs[-1]
 
 
 def regroup_kernel(groups, *refs):
@@ -218,12 +237,11 @@
 
 
 def join_kernel(chips, *refs):
-    parts, out, sem = refs[:chips], refs[-2], refs[-1]
+    parts, out = refs[:chips], refs[-1]
     z, _, _ = place()
     width = parts[0].shape[1]
-    pairs = [(part, out.at[:, cut(z ^ turn, width)]) for turn, part in enumerate(parts)]
-    for one in copy_all(pairs, sem):
-        one.wait()
+    for turn, part in enumerate(parts):
+        out[:, cut(z ^ turn, width)] = part[...]
 
 
 def join(parts):
@@ -231,9 +249,8 @@
     return pl.pallas_call(
         functools.partial(join_kernel, chips),
         out_shape=jax.ShapeDtypeStruct((rows, width * chips), parts[0].dtype),
-        in_specs=[ANY] * chips,
-        out_specs=ANY,
-        scratch_shapes=[pltpu.SemaphoreType.DMA((chips,))],
+        in_specs=[VMEM] * chips,
+        out_specs=VMEM,
         compiler_params=PARAMS,
     )(*parts)
 
@@ -243,11 +260,12 @@
     groups = lax.axis_size("head")
     half = chips // 2
     across, within = list(range(half, chips)), list(range(1, half))
-    kv, q_cut = split(queries, keys, values, chips)
+    kv, q_cut = split(queries, keys, values, [*across[::-1], *within], chips)
+    q_parts = [swapped(part, "head", step) for step, part in enumerate(q_cut, 1)]
+    kv_late, q_own, rel = measure(block_order, queries, keys, values, [0], chips, q_parts[0])
+    kv |= kv_late
     near = [kv[0]] + [over(kv[turn], turn) for turn in range(1, chips)]
-    q_parts = [q_cut[0]] + [swapped(q_cut[step], "head", step) for step in range(1, groups)]
-    rel = measure(block_order, keys.shape[0], chips, q_parts[1])
-    q = regroup(q_parts, keys.shape[0], chips, rel)
+    q = regroup([q_own, *q_parts], keys.shape[0], chips, rel)
     q = [q[0]] + [over(q[turn], turn) for turn in range(1, chips)]
     stacked = [*across[::-1], 0]
     swap = swapped(stack([near[turn] for turn in stacked]), "seq", 1)

time: 32.5 us -> 32.5 us (level)
  waiting for transfers between devices: 9.18 us -> 8.27 us
  Pallas kernels: 5.56 us -> 6.39 us
    ppermute x14, waiting for transfers between devices: 9.18 us -> 8.27 us  [swapped(): return lax.ppermute(block, axis, route)]
    pallas_call x2, Pallas kernels: 1.84 us -> 2.66 us  [the longest x1 1.48 us: measure(): pl.pallas_call(functools.partial(measure_kernel, turns, chips), out_shape...]
  transfers between devices with their start and end apart: 14 -> 14, of which waited for: 8 -> 8; matrix products, arithmetic and copies ran while one was open for 0% -> 0% of each run, Pallas kernels for 11% -> 14%
where the time goes in v5:
time: 32.5 us; the launch traced here: 32.3 us
  starting transfers between devices  17.5 us (54%)
  waiting for transfers between devices  8.27 us (25%)
  Pallas kernels  6.39 us (20%)
    ppermute x14, starting transfers between devices, swapped(): return lax.ppermute(block, axis, route)  17.5 us
    ppermute x14, waiting for transfers between devices, swapped(): return lax.ppermute(block, axis, route)  8.27 us
    pallas_call x4, Pallas kernels, attend(): pl.pallas_call(functools.partial(attend_kernel, turns, len(q), bool(near)...  2.3 us
    pallas_call x1, Pallas kernels, measure(): pl.pallas_call(functools.partial(measure_kernel, turns, chips), out_shape...  1.48 us
    pallas_call x1, Pallas kernels, split(): pl.pallas_call(functools.partial(split_kernel, turns), out_shape=outs, in...  1.18 us
    pallas_call x1, Pallas kernels, join(): pl.pallas_call(functools.partial(join_kernel, chips), out_shape=jax.Shape...  0.74 us
  transfers between devices with their start and end apart: 14, of which 8 were waited for; matrix products, arithmetic and copies ran while one was open for 0% of the time, Pallas kernels for 14%

profile of v5, /device:TPU:0, one launch (start us, length us, event | category | flops | bytes accessed | tf_op | source)
XLA Modules:
  0.0 32.3 jit_solution(1491707303980429114)
XLA Ops:
  0.0 1.2 %shard_map.46 = (bf16[128,512]{1,0:T(8,128)(2,1)S(1)}, bf16[128,512]{1,0:T(8,128)(2,1)S(1)}, bf16[128,512]{1,0:T(8,128)(2,1)S(1)}, bf16[32,1024]{1,0:T(8,128)(2,...) custom-call(bf16[32,4096]{1,0:T(8,128)(2,1)} %q_ref.3, bf16[128,1024]{1,0:T(8,128)(2,1)} %k_ref.3, ...), custom_call_target="tpu_custom_call" | custom-call | tf_op jit(solution)/shard_map/pallas_call | solution.py:78
  1.2 5.1 %collective-permute-start.3 = (bf16[128,512]{1,0:T(8,128)(2,1)S(1)}, bf16[128,512]{1,0:T(8,128)(2,1)S(1)}, u32[]{:S(2)}, u32[]{:S(2)}) collective-permute-start(bf16[128,512]{1,0:T(8,128)(2,1)S(1)} %get-tuple-element.28), channel_id=1, source_target_pairs={{0,24},{4,28},{8,16},{12,20},{16,8},{20,12},{24,0},{28,4},{1,25},{... | collective-permute-start | bytes 393224 | tf_op jit(solution)/shard_map/ppermute | solution.py:30
  6.3 0.0 collective-permute-start.4
  6.3 1.5 %collective-permute-start = (bf16[32,1024]{1,0:T(8,128)(2,1)S(1)}, bf16[32,1024]{1,0:T(8,128)(2,1)S(1)}, u32[]{:S(2)}, u32[]{:S(2)}) collective-permute-start(bf16[32,1024]{1,0:T(8,128)(2,1)S(1)} %get-tuple-element.22), channel_id=1, source_target_pairs={{0,1},{1,0},{2,3},{3,2},{4,5},{5,4},{6,7},{7,6},{8,9},{9,8},{10,11... | collective-permute-start | bytes 196616 | tf_op jit(solution)/shard_map/ppermute | solution.py:30
  7.8 1.5 %collective-permute-start.1 = (bf16[32,1024]{1,0:T(8,128)(2,1)S(1)}, bf16[32,1024]{1,0:T(8,128)(2,1)S(1)}, u32[]{:S(2)}, u32[]{:S(2)}) collective-permute-start(bf16[32,1024]{1,0:T(8,128)(2,1)S(1)} %get-tuple-element.25), channel_id=1, source_target_pairs={{0,2},{1,3},{2,0},{3,1},{4,6},{5,7},{6,4},{7,5},{8,10},{9,11},{10,... | collective-permute-start | bytes 196616 | tf_op jit(solution)/shard_map/ppermute | solution.py:30
  9.3 0.5 %collective-permute-start.2 = (bf16[32,1024]{1,0:T(8,128)(2,1)S(1)}, bf16[32,1024]{1,0:T(8,128)(2,1)S(1)}, u32[]{:S(2)}, u32[]{:S(2)}) collective-permute-start(bf16[32,1024]{1,0:T(8,128)(2,1)S(1)} %get-tuple-element.26), channel_id=1, source_target_pairs={{0,3},{1,2},{2,1},{3,0},{4,7},{5,6},{6,5},{7,4},{8,11},{9,10},{10,... | collective-permute-start | bytes 196616 | tf_op jit(solution)/shard_map/ppermute | solution.py:30
  9.8 0.8 %collective-permute-done._.refs_1_ = bf16[32,1024]{1,0:T(8,128)(2,1)S(1)} collective-permute-done((bf16[32,1024]{1,0:T(8,128)(2,1)S(1)}, bf16[32,1024]{1,0:T(8,128)(2,1)S(1)}, u32[]{:S(2)}, u32[]{:S(2)}) %collective-permute-start) | collective-permute-done | bytes 65568 | tf_op jit(solution)/shard_map/ppermute | solution.py:30
  10.6 0.6 %collective-permute-start.6 = (bf16[128,512]{1,0:T(8,128)(2,1)S(1)}, bf16[128,512]{1,0:T(8,128)(2,1)S(1)}, u32[]{:S(2)}, u32[]{:S(2)}) collective-permute-start(bf16[128,512]{1,0:T(8,128)(2,1)S(1)} %get-tuple-element.31), channel_id=1, source_target_pairs={{0,8},{4,12},{8,0},{12,4},{16,24},{20,28},{24,16},{28,20},{1,9},{5... | collective-permute-start | bytes 393224 | tf_op jit(solution)/shard_map/ppermute | solution.py:30
  11.2 1.5 %shard_map.47 = (bf16[128,512]{1,0:T(8,128)(2,1)S(1)}, bf16[32,1024]{1,0:T(8,128)(2,1)S(1)}, s32[4,8,1024]{2,1,0:T(8,128)S(1)}) custom-call(s32[8]{0:T(128)S(1)} %copy-done, bf16[32,4096]{1,0:T(8,128)(2,1)} %q_ref.3, bf16[128,1024]{1,0:T(8,128)(2,1)} %k_ref.3, bf16[128,1024]{1,0:T(8,128)(2,1)} %v_ref.3, bf16[32,1024]{1,0:T(8,128)(2,1)S(1)} %collective-permute-done._.refs_1_), custom_call_target="tpu_custom_call" | custom-call | tf_op jit(solution)/shard_map/pallas_call | solution.py:119
  12.7 0.1 collective-permute-done.1.refs_2_
  12.8 1.7 %collective-permute-done.2.refs_3_ = bf16[32,1024]{1,0:T(8,128)(2,1)S(1)} collective-permute-done((bf16[32,1024]{1,0:T(8,128)(2,1)S(1)}, bf16[32,1024]{1,0:T(8,128)(2,1)S(1)}, u32[]{:S(2)}, u32[]{:S(2)}) %collective-permute-start.2) | collective-permute-done | bytes 65568 | tf_op jit(solution)/shard_map/ppermute | solution.py:30
  14.5 0.8 %collective-permute-start.8 = (bf16[128,256]{1,0:T(8,128)(2,1)S(1)}, bf16[128,256]{1,0:T(8,128)(2,1)S(1)}, u32[]{:S(2)}, u32[]{:S(2)}) collective-permute-start(bf16[128,256]{1,0:T(8,128)(2,1)S(1)} %get-tuple-element.32), channel_id=1, source_target_pairs={{0,8},{4,12},{8,0},{12,4},{16,24},{20,28},{24,16},{28,20},{1,9},{5... | collective-permute-start | bytes 196616 | tf_op jit(solution)/shard_map/ppermute | solution.py:30
  15.4 2.2 %collective-permute-start.10 = (bf16[128,256]{1,0:T(8,128)(2,1)S(1)}, bf16[128,256]{1,0:T(8,128)(2,1)S(1)}, u32[]{:S(2)}, u32[]{:S(2)}) collective-permute-start(bf16[128,256]{1,0:T(8,128)(2,1)S(1)} %get-tuple-element.37), channel_id=1, source_target_pairs={{0,16},{4,20},{8,24},{12,28},{16,0},{20,4},{24,8},{28,12},{1,17},{... | collective-permute-start | bytes 196616 | tf_op jit(solution)/shard_map/ppermute | solution.py:30
  17.6 0.0 collective-permute-done.3.refs_0_.rest_5_.rest_4_
  17.6 1.4 %collective-permute-start.12 = (bf16[128,256]{1,0:T(8,128)(2,1)S(1)}, bf16[128,256]{1,0:T(8,128)(2,1)S(1)}, u32[]{:S(2)}, u32[]{:S(2)}) collective-permute-start(bf16[128,256]{1,0:T(8,128)(2,1)S(1)} %get-tuple-element.38), channel_id=1, source_target_pairs={{0,24},{4,28},{8,16},{12,20},{16,8},{20,12},{24,0},{28,4},{1,25},{... | collective-permute-start | bytes 196616 | tf_op jit(solution)/shard_map/ppermute | solution.py:30
  19.0 0.0 collective-permute-done.4.refs_1_.rest_4_.rest_3_
  19.0 0.1 collective-permute-start.5
  19.1 0.4 %collective-permute-done.6.rest_3_.rest_2_ = bf16[128,512]{1,0:T(8,128)(2,1)S(1)} collective-permute-done((bf16[128,512]{1,0:T(8,128)(2,1)S(1)}, bf16[128,512]{1,0:T(8,128)(2,1)S(1)}, u32[]{:S(2)}, u32[]{:S(2)}) %collective-permute-start.6) | collective-permute-done | bytes 131104 | tf_op jit(solution)/shard_map/ppermute | solution.py:30
  19.5 0.1 collective-permute-start.7
  19.6 1.9 %collective-permute-done.8.rest_0_ = bf16[128,256]{1,0:T(8,128)(2,1)S(1)} collective-permute-done((bf16[128,256]{1,0:T(8,128)(2,1)S(1)}, bf16[128,256]{1,0:T(8,128)(2,1)S(1)}, u32[]{:S(2)}, u32[]{:S(2)}) %collective-permute-start.8) | collective-permute-done | bytes 65568 | tf_op jit(solution)/shard_map/ppermute | solution.py:30
  21.5 0.6 %shard_map.50 = (f32[128,256]{1,0:T(8,128)S(1)}, f32[128,512]{1,0:T(8,128)S(1)}, f32[128,256]{1,0:T(8,128)S(1)}, f32[128,512]{1,0:T(8,128)S(1)}) custom-call(s32[4,8,1024]{2,1,0:T(8,128)S(1)} %get-tuple-element.23.refs_4_.rel_ref, bf16[128,256]{1,0:T(8,128)(2,1)S(1)} %collective-permute-done.8.rest_0_, ...), custom_call_target="tpu_custom_call" | custom-call | flops 60000002048 | tf_op jit(solution)/shard_map/pallas_call | solution.py:215
  22.2 0.5 %shard_map.52.rest_7_ = bf16[128,256]{1,0:T(8,128)(2,1)S(1)} custom-call(s32[4,8,1024]{2,1,0:T(8,128)S(1)} %get-tuple-element.23.refs_4_.rel_ref, bf16[128,256]{1,0:T(8,128)(2,1)S(1)} %collective-permute-done.8.rest_0_, bf16[3,128,512]{2,1,0:T(8,128)(2,1)S(1)} %collective-permute-done.5.rest_1_.rest_5_, ...), custom_call_target="tpu_custom_call" | custom-call | tf_op jit(solution)/shard_map/pallas_call | solution.py:229
  22.7 0.7 %shard_map.53 = bf16[128,256]{1,0:T(8,128)(2,1)S(1)} custom-call(s32[4,8,1024]{2,1,0:T(8,128)S(1)} %get-tuple-element.23.refs_4_.rel_ref, bf16[128,256]{1,0:T(8,128)(2,1)S(1)} %collective-permute-done.10.rest_0_, bf16[128,512]{1,0:T(8,128)(2,1)S(1)} %get-tuple-element.30.refs_2_.rest_2_.rest_1_, bf16[128,512]{1,0:T(8,128)(2,1)S(1)} %collective-permute-done.6.rest_3_.rest_2_, ...), custom_call_target="tpu_custom_call" | custom-call | tf_op jit(solution)/shard_map/pallas_call | solution.py:229
  23.3 0.9 %collective-permute-start.11 = (bf16[128,256]{1,0:T(8,128)(2,1)S(1)}, bf16[128,256]{1,0:T(8,128)(2,1)S(1)}, u32[]{:S(2)}, u32[]{:S(2)}) collective-permute-start(bf16[128,256]{1,0:T(8,128)(2,1)S(1)} %shard_map.53), channel_id=1, source_target_pairs={{0,16},{4,20},{8,24},{12,28},{16,0},{20,4},{24,8},{28,12},{1,17},{... | collective-permute-start | bytes 196616 | tf_op jit(solution)/shard_map/ppermute | solution.py:30
  24.3 0.7 %shard_map.54 = bf16[128,256]{1,0:T(8,128)(2,1)S(1)} custom-call(s32[4,8,1024]{2,1,0:T(8,128)S(1)} %get-tuple-element.23.refs_4_.rel_ref, bf16[128,256]{1,0:T(8,128)(2,1)S(1)} %collective-permute-done.12.rest_0_, bf16[128,512]{1,0:T(8,128)(2,1)S(1)} %get-tuple-element.30.refs_2_.rest_2_.rest_1_, bf16[128,512]{1,0:T(8,128)(2,1)S(1)} %collective-permute-done.6.rest_3_.rest_2_, ...), custom_call_target="tpu_custom_call" | custom-call | tf_op jit(solution)/shard_map/pallas_call | solution.py:229
  24.9 1.5 %collective-permute-start.13 = (bf16[128,256]{1,0:T(8,128)(2,1)S(1)}, bf16[128,256]{1,0:T(8,128)(2,1)S(1)}, u32[]{:S(2)}, u32[]{:S(2)}) collective-permute-start(bf16[128,256]{1,0:T(8,128)(2,1)S(1)} %shard_map.54), channel_id=1, source_target_pairs={{0,24},{4,28},{8,16},{12,20},{16,8},{20,12},{24,0},{28,4},{1,25},{... | collective-permute-start | bytes 196616 | tf_op jit(solution)/shard_map/ppermute | solution.py:30
  26.4 1.2 %collective-permute-start.9 = (bf16[128,256]{1,0:T(8,128)(2,1)S(1)}, bf16[128,256]{1,0:T(8,128)(2,1)S(1)}, u32[]{:S(2)}, u32[]{:S(2)}) collective-permute-start(bf16[128,256]{1,0:T(8,128)(2,1)S(1)} %shard_map.52.rest_7_), channel_id=1, source_target_pairs={{0,8},{4,12},{8,0},{12,4},{16,24},{20,28},{24,16},{28,20},{1,9},{5... | collective-permute-start | bytes 196616 | tf_op jit(solution)/shard_map/ppermute | solution.py:30
  27.6 0.5 %shard_map.51.refs_0_ = bf16[128,256]{1,0:T(8,128)(2,1)S(1)} custom-call(s32[4,8,1024]{2,1,0:T(8,128)S(1)} %get-tuple-element.23.refs_4_.rel_ref, bf16[128,256]{1,0:T(8,128)(2,1)S(1)} %get-tuple-element.27.rest_1_.rest_0_, bf16[3,128,512]{2,1,0:T(8,128)(2,1)S(1)} %collective-permute-done.5.rest_1_.rest_5_, ...), custom_call_target="tpu_custom_call" | custom-call | tf_op jit(solution)/shard_map/pallas_call | solution.py:229
  28.1 2.0 %collective-permute-done.11.refs_2_ = bf16[128,256]{1,0:T(8,128)(2,1)S(1)} collective-permute-done((bf16[128,256]{1,0:T(8,128)(2,1)S(1)}, bf16[128,256]{1,0:T(8,128)(2,1)S(1)}, u32[]{:S(2)}, u32[]{:S(2)}) %collective-permute-start.11) | collective-permute-done | bytes 65568 | tf_op jit(solution)/shard_map/ppermute | solution.py:30
  30.1 1.3 %collective-permute-done.13.refs_3_ = bf16[128,256]{1,0:T(8,128)(2,1)S(1)} collective-permute-done((bf16[128,256]{1,0:T(8,128)(2,1)S(1)}, bf16[128,256]{1,0:T(8,128)(2,1)S(1)}, u32[]{:S(2)}, u32[]{:S(2)}) %collective-permute-start.13) | collective-permute-done | bytes 65568 | tf_op jit(solution)/shard_map/ppermute | solution.py:30
  31.4 0.1 collective-permute-done.9.refs_1_
  31.5 0.7 %shard_map.55 = bf16[128,1024]{1,0:T(8,128)(2,1)} custom-call(bf16[128,256]{1,0:T(8,128)(2,1)S(1)} %shard_map.51.refs_0_, bf16[128,256]{1,0:T(8,128)(2,1)S(1)} %collective-permute-done.9.refs_1_, bf16[128,256]{1,0:T(8,128)(2,1)S(1)} %collective-permute-done.11.refs_2_, bf16[128,256]{1,0:T(8,128)(2,1)S(1)} %collective-permute-done.13.refs_3_), custom_call_target="tpu_custom_call" | custom-call | tf_op jit(solution)/shard_map/pallas_call | solution.py:249
  (8 shorter events, 0.1 us)
Async XLA Ops:
  1.2 16.4 %collective-permute-start.3 = (bf16[128,512]{1,0:T(8,128)(2,1)S(1)}, bf16[128,512]{1,0:T(8,128)(2,1)S(1)}, u32[]{:S(2)}, u32[]{:S(2)}) collective-permute-start(bf16[128,512]{1,0:T(8,128)(2,1)S(1)} %get-tuple-element.28), channel_id=1, source_target_pairs={{0,24},{4,28},{8,16},{12,20},{16,8},{20,12},{24,0},{28,4},{1,25},{... | collective-permute-start | bytes 393224 | tf_op jit(solution)/shard_map/ppermute | solution.py:30
  6.3 12.7 %collective-permute-start.4 = (bf16[128,512]{1,0:T(8,128)(2,1)S(1)}, bf16[128,512]{1,0:T(8,128)(2,1)S(1)}, u32[]{:S(2)}, u32[]{:S(2)}) collective-permute-start(bf16[128,512]{1,0:T(8,128)(2,1)S(1)} %get-tuple-element.29), channel_id=1, source_target_pairs={{0,16},{4,20},{8,24},{12,28},{16,0},{20,4},{24,8},{28,12},{1,17},{... | collective-permute-start | bytes 393224 | tf_op jit(solution)/shard_map/ppermute | solution.py:30
  6.3 4.3 %collective-permute-start = (bf16[32,1024]{1,0:T(8,128)(2,1)S(1)}, bf16[32,1024]{1,0:T(8,128)(2,1)S(1)}, u32[]{:S(2)}, u32[]{:S(2)}) collective-permute-start(bf16[32,1024]{1,0:T(8,128)(2,1)S(1)} %get-tuple-element.22), channel_id=1, source_target_pairs={{0,1},{1,0},{2,3},{3,2},{4,5},{5,4},{6,7},{7,6},{8,9},{9,8},{10,11... | collective-permute-start | bytes 196616 | tf_op jit(solution)/shard_map/ppermute | solution.py:30
  7.8 5.0 %collective-permute-start.1 = (bf16[32,1024]{1,0:T(8,128)(2,1)S(1)}, bf16[32,1024]{1,0:T(8,128)(2,1)S(1)}, u32[]{:S(2)}, u32[]{:S(2)}) collective-permute-start(bf16[32,1024]{1,0:T(8,128)(2,1)S(1)} %get-tuple-element.25), channel_id=1, source_target_pairs={{0,2},{1,3},{2,0},{3,1},{4,6},{5,7},{6,4},{7,5},{8,10},{9,11},{10,... | collective-permute-start | bytes 196616 | tf_op jit(solution)/shard_map/ppermute | solution.py:30
  9.3 1.9 %copy-start = (s32[8]{0:T(128)S(1)}, s32[8]{0:T(128)}, u32[]{:S(2)}) copy-start(s32[8]{0:T(128)} %order_ref.1) | copy-start | bytes 100
  9.3 5.2 %collective-permute-start.2 = (bf16[32,1024]{1,0:T(8,128)(2,1)S(1)}, bf16[32,1024]{1,0:T(8,128)(2,1)S(1)}, u32[]{:S(2)}, u32[]{:S(2)}) collective-permute-start(bf16[32,1024]{1,0:T(8,128)(2,1)S(1)} %get-tuple-element.26), channel_id=1, source_target_pairs={{0,3},{1,2},{2,1},{3,0},{4,7},{5,6},{6,5},{7,4},{8,11},{9,10},{10,... | collective-permute-start | bytes 196616 | tf_op jit(solution)/shard_map/ppermute | solution.py:30
  10.6 8.9 %collective-permute-start.6 = (bf16[128,512]{1,0:T(8,128)(2,1)S(1)}, bf16[128,512]{1,0:T(8,128)(2,1)S(1)}, u32[]{:S(2)}, u32[]{:S(2)}) collective-permute-start(bf16[128,512]{1,0:T(8,128)(2,1)S(1)} %get-tuple-element.31), channel_id=1, source_target_pairs={{0,8},{4,12},{8,0},{12,4},{16,24},{20,28},{24,16},{28,20},{1,9},{5... | collective-permute-start | bytes 393224 | tf_op jit(solution)/shard_map/ppermute | solution.py:30
  14.5 7.0 %collective-permute-start.8 = (bf16[128,256]{1,0:T(8,128)(2,1)S(1)}, bf16[128,256]{1,0:T(8,128)(2,1)S(1)}, u32[]{:S(2)}, u32[]{:S(2)}) collective-permute-start(bf16[128,256]{1,0:T(8,128)(2,1)S(1)} %get-tuple-element.32), channel_id=1, source_target_pairs={{0,8},{4,12},{8,0},{12,4},{16,24},{20,28},{24,16},{28,20},{1,9},{5... | collective-permute-start | bytes 196616 | tf_op jit(solution)/shard_map/ppermute | solution.py:30
  15.4 7.3 %collective-permute-start.10 = (bf16[128,256]{1,0:T(8,128)(2,1)S(1)}, bf16[128,256]{1,0:T(8,128)(2,1)S(1)}, u32[]{:S(2)}, u32[]{:S(2)}) collective-permute-start(bf16[128,256]{1,0:T(8,128)(2,1)S(1)} %get-tuple-element.37), channel_id=1, source_target_pairs={{0,16},{4,20},{8,24},{12,28},{16,0},{20,4},{24,8},{28,12},{1,17},{... | collective-permute-start | bytes 196616 | tf_op jit(solution)/shard_map/ppermute | solution.py:30
  17.6 6.7 %collective-permute-start.12 = (bf16[128,256]{1,0:T(8,128)(2,1)S(1)}, bf16[128,256]{1,0:T(8,128)(2,1)S(1)}, u32[]{:S(2)}, u32[]{:S(2)}) collective-permute-start(bf16[128,256]{1,0:T(8,128)(2,1)S(1)} %get-tuple-element.38), channel_id=1, source_target_pairs={{0,24},{4,28},{8,16},{12,20},{16,8},{20,12},{24,0},{28,4},{1,25},{... | collective-permute-start | bytes 196616 | tf_op jit(solution)/shard_map/ppermute | solution.py:30
  19.0 3.1 %collective-permute-start.5 = (bf16[3,128,512]{2,1,0:T(8,128)(2,1)S(1)}, bf16[3,128,512]{2,1,0:T(8,128)(2,1)S(1)}, u32[]{:S(2)}, u32[]{:S(2)}) collective-permute-start(bf16[3,128,512]{2,1,0:T(8,128)(2,1)S(1)} %shard_map.49), channel_id=1, source_target_pairs={{0,4},{4,0},{8,12},{12,8},{16,20},{20,16},{24,28},{28,24},{1,5},{5... | collective-permute-start | bytes 1179656 | tf_op jit(solution)/shard_map/ppermute | solution.py:30
  19.5 2.7 %collective-permute-start.7 = (bf16[128,512]{1,0:T(8,128)(2,1)S(1)}, bf16[128,512]{1,0:T(8,128)(2,1)S(1)}, u32[]{:S(2)}, u32[]{:S(2)}) collective-permute-start(bf16[128,512]{1,0:T(8,128)(2,1)S(1)} %collective-permute-done.6.rest_3_.rest_2_), channel_id=1, source_target_pairs={{0,4},{4,0},{8,12},{12,8},{16,20},{20,16},{24,28},{28,24},{1,5},{5... | collective-permute-start | bytes 393224 | tf_op jit(solution)/shard_map/ppermute | solution.py:30
  23.3 6.8 %collective-permute-start.11 = (bf16[128,256]{1,0:T(8,128)(2,1)S(1)}, bf16[128,256]{1,0:T(8,128)(2,1)S(1)}, u32[]{:S(2)}, u32[]{:S(2)}) collective-permute-start(bf16[128,256]{1,0:T(8,128)(2,1)S(1)} %shard_map.53), channel_id=1, source_target_pairs={{0,16},{4,20},{8,24},{12,28},{16,0},{20,4},{24,8},{28,12},{1,17},{... | collective-permute-start | bytes 196616 | tf_op jit(solution)/shard_map/ppermute | solution.py:30
  24.9 6.5 %collective-permute-start.13 = (bf16[128,256]{1,0:T(8,128)(2,1)S(1)}, bf16[128,256]{1,0:T(8,128)(2,1)S(1)}, u32[]{:S(2)}, u32[]{:S(2)}) collective-permute-start(bf16[128,256]{1,0:T(8,128)(2,1)S(1)} %shard_map.54), channel_id=1, source_target_pairs={{0,24},{4,28},{8,16},{12,20},{16,8},{20,12},{24,0},{28,4},{1,25},{... | collective-permute-start | bytes 196616 | tf_op jit(solution)/shard_map/ppermute | solution.py:30
  26.4 5.1 %collective-permute-start.9 = (bf16[128,256]{1,0:T(8,128)(2,1)S(1)}, bf16[128,256]{1,0:T(8,128)(2,1)S(1)}, u32[]{:S(2)}, u32[]{:S(2)}) collective-permute-start(bf16[128,256]{1,0:T(8,128)(2,1)S(1)} %shard_map.52.rest_7_), channel_id=1, source_target_pairs={{0,8},{4,12},{8,0},{12,4},{16,24},{20,28},{24,16},{28,20},{1,9},{5... | collective-permute-start | bytes 196616 | tf_op jit(solution)/shard_map/ppermute | solution.py:30

commit v6 on v5

--- a/solution.py
+++ b/solution.py
@@ -184,29 +184,36 @@
 
     for index, (turn, q_ref) in enumerate(zip(turns, q_refs)):
         top_ref, sums_ref = states[2 * index : 2 * index + 2] or (None, None)
-        for column in range(0, width, HEAD_DIM):
-            tops, wide = pl.ds(column, HEAD_DIM), pl.ds(2 * column, 2 * HEAD_DIM)
-            top = None if first else top_ref[:, tops]
-            sums = None if first else sums_ref[:, wide]
-            for at in range(0, len(blocks), CORES):
+        columns = range(0, width, HEAD_DIM)
+        state = {column: None if first else (top_ref[:, pl.ds(column, HEAD_DIM)], sums_ref[:, pl.ds(2 * column, 2 * HEAD_DIM)]) for column in columns}
+        for at in range(0, len(blocks), CORES):
+            seen = rel_ref[turn, 0:1, pl.ds(start + at * rows, CORES * rows)] <= below
+            for column in columns:
                 s = lax.dot_general(
-                    q_ref[:, tops], both(at, column), (((1,), (1,)), ((), ())), preferred_element_type=jnp.float32
+                    q_ref[:, pl.ds(column, HEAD_DIM)],
+                    both(at, column),
+                    (((1,), (1,)), ((), ())),
+                    preferred_element_type=jnp.float32,
                 )
-                rel = rel_ref[turn, 0:1, pl.ds(start + at * rows, CORES * rows)]
-                s = jnp.where(rel <= below, s, jnp.float32(-1e30))
+                s = jnp.where(seen, s, jnp.float32(-1e30))
                 high = jnp.broadcast_to(jnp.max(s, axis=1, keepdims=True), (rows, HEAD_DIM))
-                high = high if top is None else jnp.maximum(top, high)
+                if state[column] is not None:
+                    top, sums = state[column]
+                    high = jnp.maximum(top, high)
                 weight = jnp.exp2((s - jnp.concatenate([high] * CORES, 1)) * scale).astype(jnp.bfloat16)
                 values = jnp.concatenate([both(at, width + column), ones], 1)
                 mixed = jnp.dot(weight, values, preferred_element_type=jnp.float32)
-                if top is not None:
+                if state[column] is not None:
                     shrink = jnp.exp2((top - high) * scale)
                     mixed += sums * jnp.concatenate([shrink, shrink], 1)
-                top, sums = high, mixed
+                state[column] = (high, mixed)
+        for column, (top, sums) in state.items():
             if last:
-                outs[index][:, tops] = (sums[:, :HEAD_DIM] / sums[:, HEAD_DIM:]).astype(outs[index].dtype)
+                mean = sums[:, :HEAD_DIM] / sums[:, HEAD_DIM:]
+                outs[index][:, pl.ds(column, HEAD_DIM)] = mean.astype(outs[index].dtype)
             else:
-                top_ref[:, tops], sums_ref[:, wide] = top, sums
+                top_ref[:, pl.ds(column, HEAD_DIM)] = top
+                sums_ref[:, pl.ds(2 * column, 2 * HEAD_DIM)] = sums
 
 
 def attend_near(turns, rel, q, near):
@@ -270,7 +277,7 @@
     stacked = [*across[::-1], 0]
     swap = swapped(stack([near[turn] for turn in stacked]), "seq", 1)
     far = (stacked, swap, {turn: swapped(near[turn], "seq", 1) for turn in within})
-    states = attend_near([*within, 0], rel, q, near)
+    states = attend_near([0, *within], rel, q, near)
     done = attend(within, rel, q, (), far, states) if within else {}
     out = {turn: over(part, turn) for turn, part in done.items()}
     for turn in across[::-1]:

time: 32.5 us -> 32.5 us (level)
  no operation moved by 1% of the time
where the time goes in v6:
time: 32.5 us; the launch traced here: 32.2 us
  starting transfers between devices  17.5 us (54%)
  waiting for transfers between devices  8.28 us (25%)
  Pallas kernels  6.37 us (20%)
    ppermute x14, starting transfers between devices, swapped(): return lax.ppermute(block, axis, route)  17.5 us
    ppermute x14, waiting for transfers between devices, swapped(): return lax.ppermute(block, axis, route)  8.28 us
    pallas_call x4, Pallas kernels, attend(): pl.pallas_call(functools.partial(attend_kernel, turns, len(q), bool(near)...  2.28 us
    pallas_call x1, Pallas kernels, measure(): pl.pallas_call(functools.partial(measure_kernel, turns, chips), out_shape...  1.48 us
    pallas_call x1, Pallas kernels, split(): pl.pallas_call(functools.partial(split_kernel, turns), out_shape=outs, in...  1.18 us
    pallas_call x1, Pallas kernels, join(): pl.pallas_call(functools.partial(join_kernel, chips), out_shape=jax.Shape...  0.74 us
  transfers between devices with their start and end apart: 14, of which 8 were waited for; matrix products, arithmetic and copies ran while one was open for 0% of the time, Pallas kernels for 14%

profile of v6, /device:TPU:0, one launch (start us, length us, event | category | flops | bytes accessed | tf_op | source)
XLA Modules:
  0.0 32.2 jit_solution(13920584260906998802)
XLA Ops:
  0.0 1.2 %shard_map.46 = (bf16[128,512]{1,0:T(8,128)(2,1)S(1)}, bf16[128,512]{1,0:T(8,128)(2,1)S(1)}, bf16[128,512]{1,0:T(8,128)(2,1)S(1)}, bf16[32,1024]{1,0:T(8,128)(2,...) custom-call(bf16[32,4096]{1,0:T(8,128)(2,1)} %q_ref.3, bf16[128,1024]{1,0:T(8,128)(2,1)} %k_ref.3, ...), custom_call_target="tpu_custom_call" | custom-call | tf_op jit(solution)/shard_map/pallas_call | solution.py:78
  1.2 5.1 %collective-permute-start.3 = (bf16[128,512]{1,0:T(8,128)(2,1)S(1)}, bf16[128,512]{1,0:T(8,128)(2,1)S(1)}, u32[]{:S(2)}, u32[]{:S(2)}) collective-permute-start(bf16[128,512]{1,0:T(8,128)(2,1)S(1)} %get-tuple-element.28), channel_id=1, source_target_pairs={{0,24},{4,28},{8,16},{12,20},{16,8},{20,12},{24,0},{28,4},{1,25},{... | collective-permute-start | bytes 393224 | tf_op jit(solution)/shard_map/ppermute | solution.py:30
  6.3 1.5 %collective-permute-start = (bf16[32,1024]{1,0:T(8,128)(2,1)S(1)}, bf16[32,1024]{1,0:T(8,128)(2,1)S(1)}, u32[]{:S(2)}, u32[]{:S(2)}) collective-permute-start(bf16[32,1024]{1,0:T(8,128)(2,1)S(1)} %get-tuple-element.22), channel_id=1, source_target_pairs={{0,1},{1,0},{2,3},{3,2},{4,5},{5,4},{6,7},{7,6},{8,9},{9,8},{10,11... | collective-permute-start | bytes 196616 | tf_op jit(solution)/shard_map/ppermute | solution.py:30
  7.8 1.5 %collective-permute-start.1 = (bf16[32,1024]{1,0:T(8,128)(2,1)S(1)}, bf16[32,1024]{1,0:T(8,128)(2,1)S(1)}, u32[]{:S(2)}, u32[]{:S(2)}) collective-permute-start(bf16[32,1024]{1,0:T(8,128)(2,1)S(1)} %get-tuple-element.25), channel_id=1, source_target_pairs={{0,2},{1,3},{2,0},{3,1},{4,6},{5,7},{6,4},{7,5},{8,10},{9,11},{10,... | collective-permute-start | bytes 196616 | tf_op jit(solution)/shard_map/ppermute | solution.py:30
  9.3 0.5 %collective-permute-start.2 = (bf16[32,1024]{1,0:T(8,128)(2,1)S(1)}, bf16[32,1024]{1,0:T(8,128)(2,1)S(1)}, u32[]{:S(2)}, u32[]{:S(2)}) collective-permute-start(bf16[32,1024]{1,0:T(8,128)(2,1)S(1)} %get-tuple-element.26), channel_id=1, source_target_pairs={{0,3},{1,2},{2,1},{3,0},{4,7},{5,6},{6,5},{7,4},{8,11},{9,10},{10,... | collective-permute-start | bytes 196616 | tf_op jit(solution)/shard_map/ppermute | solution.py:30
  9.8 0.8 %collective-permute-done._.refs_1_ = bf16[32,1024]{1,0:T(8,128)(2,1)S(1)} collective-permute-done((bf16[32,1024]{1,0:T(8,128)(2,1)S(1)}, bf16[32,1024]{1,0:T(8,128)(2,1)S(1)}, u32[]{:S(2)}, u32[]{:S(2)}) %collective-permute-start) | collective-permute-done | bytes 65568 | tf_op jit(solution)/shard_map/ppermute | solution.py:30
  10.6 0.6 %collective-permute-start.6 = (bf16[128,512]{1,0:T(8,128)(2,1)S(1)}, bf16[128,512]{1,0:T(8,128)(2,1)S(1)}, u32[]{:S(2)}, u32[]{:S(2)}) collective-permute-start(bf16[128,512]{1,0:T(8,128)(2,1)S(1)} %get-tuple-element.31), channel_id=1, source_target_pairs={{0,8},{4,12},{8,0},{12,4},{16,24},{20,28},{24,16},{28,20},{1,9},{5... | collective-permute-start | bytes 393224 | tf_op jit(solution)/shard_map/ppermute | solution.py:30
  11.2 1.5 %shard_map.47 = (bf16[128,512]{1,0:T(8,128)(2,1)S(1)}, bf16[32,1024]{1,0:T(8,128)(2,1)S(1)}, s32[4,8,1024]{2,1,0:T(8,128)S(1)}) custom-call(s32[8]{0:T(128)S(1)} %copy-done, bf16[32,4096]{1,0:T(8,128)(2,1)} %q_ref.3, bf16[128,1024]{1,0:T(8,128)(2,1)} %k_ref.3, bf16[128,1024]{1,0:T(8,128)(2,1)} %v_ref.3, bf16[32,1024]{1,0:T(8,128)(2,1)S(1)} %collective-permute-done._.refs_1_), custom_call_target="tpu_custom_call" | custom-call | tf_op jit(solution)/shard_map/pallas_call | solution.py:119
  12.7 0.1 collective-permute-done.1.refs_2_
  12.8 1.7 %collective-permute-done.2.refs_3_ = bf16[32,1024]{1,0:T(8,128)(2,1)S(1)} collective-permute-done((bf16[32,1024]{1,0:T(8,128)(2,1)S(1)}, bf16[32,1024]{1,0:T(8,128)(2,1)S(1)}, u32[]{:S(2)}, u32[]{:S(2)}) %collective-permute-start.2) | collective-permute-done | bytes 65568 | tf_op jit(solution)/shard_map/ppermute | solution.py:30
  14.5 0.8 %collective-permute-start.8 = (bf16[128,256]{1,0:T(8,128)(2,1)S(1)}, bf16[128,256]{1,0:T(8,128)(2,1)S(1)}, u32[]{:S(2)}, u32[]{:S(2)}) collective-permute-start(bf16[128,256]{1,0:T(8,128)(2,1)S(1)} %get-tuple-element.32), channel_id=1, source_target_pairs={{0,8},{4,12},{8,0},{12,4},{16,24},{20,28},{24,16},{28,20},{1,9},{5... | collective-permute-start | bytes 196616 | tf_op jit(solution)/shard_map/ppermute | solution.py:30
  15.4 2.2 %collective-permute-start.10 = (bf16[128,256]{1,0:T(8,128)(2,1)S(1)}, bf16[128,256]{1,0:T(8,128)(2,1)S(1)}, u32[]{:S(2)}, u32[]{:S(2)}) collective-permute-start(bf16[128,256]{1,0:T(8,128)(2,1)S(1)} %get-tuple-element.37), channel_id=1, source_target_pairs={{0,16},{4,20},{8,24},{12,28},{16,0},{20,4},{24,8},{28,12},{1,17},{... | collective-permute-start | bytes 196616 | tf_op jit(solution)/shard_map/ppermute | solution.py:30
  17.6 1.4 %collective-permute-start.12 = (bf16[128,256]{1,0:T(8,128)(2,1)S(1)}, bf16[128,256]{1,0:T(8,128)(2,1)S(1)}, u32[]{:S(2)}, u32[]{:S(2)}) collective-permute-start(bf16[128,256]{1,0:T(8,128)(2,1)S(1)} %get-tuple-element.38), channel_id=1, source_target_pairs={{0,24},{4,28},{8,16},{12,20},{16,8},{20,12},{24,0},{28,4},{1,25},{... | collective-permute-start | bytes 196616 | tf_op jit(solution)/shard_map/ppermute | solution.py:30
  19.0 0.1 collective-permute-start.5
  19.1 0.4 %collective-permute-done.6.rest_3_.rest_2_ = bf16[128,512]{1,0:T(8,128)(2,1)S(1)} collective-permute-done((bf16[128,512]{1,0:T(8,128)(2,1)S(1)}, bf16[128,512]{1,0:T(8,128)(2,1)S(1)}, u32[]{:S(2)}, u32[]{:S(2)}) %collective-permute-start.6) | collective-permute-done | bytes 131104 | tf_op jit(solution)/shard_map/ppermute | solution.py:30
  19.5 0.1 collective-permute-start.7
  19.6 1.9 %collective-permute-done.8.rest_1_.rest_0_ = bf16[128,256]{1,0:T(8,128)(2,1)S(1)} collective-permute-done((bf16[128,256]{1,0:T(8,128)(2,1)S(1)}, bf16[128,256]{1,0:T(8,128)(2,1)S(1)}, u32[]{:S(2)}, u32[]{:S(2)}) %collective-permute-start.8) | collective-permute-done | bytes 65568 | tf_op jit(solution)/shard_map/ppermute | solution.py:30
  21.5 0.6 %shard_map.50 = (f32[128,256]{1,0:T(8,128)S(1)}, f32[128,512]{1,0:T(8,128)S(1)}, f32[128,256]{1,0:T(8,128)S(1)}, f32[128,512]{1,0:T(8,128)S(1)}) custom-call(s32[4,8,1024]{2,1,0:T(8,128)S(1)} %get-tuple-element.23.refs_4_.rel_ref, bf16[128,256]{1,0:T(8,128)(2,1)S(1)} %get-tuple-element.27.rest_0_, ...), custom_call_target="tpu_custom_call" | custom-call | flops 60000002048 | tf_op jit(solution)/shard_map/pallas_call | solution.py:222
  22.1 0.0 collective-permute-done.7.rest_2_.rest_6_
  22.2 0.0 collective-permute-done.5.rest_1_.rest_5_
  22.2 0.5 %shard_map.52.rest_7_ = bf16[128,256]{1,0:T(8,128)(2,1)S(1)} custom-call(s32[4,8,1024]{2,1,0:T(8,128)S(1)} %get-tuple-element.23.refs_4_.rel_ref, bf16[128,256]{1,0:T(8,128)(2,1)S(1)} %collective-permute-done.8.rest_1_.rest_0_, bf16[3,128,512]{2,1,0:T(8,128)(2,1)S(1)} %collective-permute-done.5.rest_1_.rest_5_, ...), custom_call_target="tpu_custom_call" | custom-call | tf_op jit(solution)/shard_map/pallas_call | solution.py:236
  22.7 0.0 collective-permute-done.10.rest_0_
  22.7 0.6 %shard_map.53 = bf16[128,256]{1,0:T(8,128)(2,1)S(1)} custom-call(s32[4,8,1024]{2,1,0:T(8,128)S(1)} %get-tuple-element.23.refs_4_.rel_ref, bf16[128,256]{1,0:T(8,128)(2,1)S(1)} %collective-permute-done.10.rest_0_, bf16[128,512]{1,0:T(8,128)(2,1)S(1)} %get-tuple-element.30.refs_2_.rest_2_.rest_1_, bf16[128,512]{1,0:T(8,128)(2,1)S(1)} %collective-permute-done.6.rest_3_.rest_2_, ...), custom_call_target="tpu_custom_call" | custom-call | tf_op jit(solution)/shard_map/pallas_call | solution.py:236
  23.3 0.9 %collective-permute-start.11 = (bf16[128,256]{1,0:T(8,128)(2,1)S(1)}, bf16[128,256]{1,0:T(8,128)(2,1)S(1)}, u32[]{:S(2)}, u32[]{:S(2)}) collective-permute-start(bf16[128,256]{1,0:T(8,128)(2,1)S(1)} %shard_map.53), channel_id=1, source_target_pairs={{0,16},{4,20},{8,24},{12,28},{16,0},{20,4},{24,8},{28,12},{1,17},{... | collective-permute-start | bytes 196616 | tf_op jit(solution)/shard_map/ppermute | solution.py:30
  24.2 0.6 %shard_map.54 = bf16[128,256]{1,0:T(8,128)(2,1)S(1)} custom-call(s32[4,8,1024]{2,1,0:T(8,128)S(1)} %get-tuple-element.23.refs_4_.rel_ref, bf16[128,256]{1,0:T(8,128)(2,1)S(1)} %collective-permute-done.12.rest_0_, bf16[128,512]{1,0:T(8,128)(2,1)S(1)} %get-tuple-element.30.refs_2_.rest_2_.rest_1_, bf16[128,512]{1,0:T(8,128)(2,1)S(1)} %collective-permute-done.6.rest_3_.rest_2_, ...), custom_call_target="tpu_custom_call" | custom-call | tf_op jit(solution)/shard_map/pallas_call | solution.py:236
  24.9 1.5 %collective-permute-start.13 = (bf16[128,256]{1,0:T(8,128)(2,1)S(1)}, bf16[128,256]{1,0:T(8,128)(2,1)S(1)}, u32[]{:S(2)}, u32[]{:S(2)}) collective-permute-start(bf16[128,256]{1,0:T(8,128)(2,1)S(1)} %shard_map.54), channel_id=1, source_target_pairs={{0,24},{4,28},{8,16},{12,20},{16,8},{20,12},{24,0},{28,4},{1,25},{... | collective-permute-start | bytes 196616 | tf_op jit(solution)/shard_map/ppermute | solution.py:30
  26.4 1.2 %collective-permute-start.9 = (bf16[128,256]{1,0:T(8,128)(2,1)S(1)}, bf16[128,256]{1,0:T(8,128)(2,1)S(1)}, u32[]{:S(2)}, u32[]{:S(2)}) collective-permute-start(bf16[128,256]{1,0:T(8,128)(2,1)S(1)} %shard_map.52.rest_7_), channel_id=1, source_target_pairs={{0,8},{4,12},{8,0},{12,4},{16,24},{20,28},{24,16},{28,20},{1,9},{5... | collective-permute-start | bytes 196616 | tf_op jit(solution)/shard_map/ppermute | solution.py:30
  27.6 0.5 %shard_map.51.refs_0_ = bf16[128,256]{1,0:T(8,128)(2,1)S(1)} custom-call(s32[4,8,1024]{2,1,0:T(8,128)S(1)} %get-tuple-element.23.refs_4_.rel_ref, bf16[128,256]{1,0:T(8,128)(2,1)S(1)} %get-tuple-element.27.rest_0_, bf16[3,128,512]{2,1,0:T(8,128)(2,1)S(1)} %collective-permute-done.5.rest_1_.rest_5_, ...), custom_call_target="tpu_custom_call" | custom-call | tf_op jit(solution)/shard_map/pallas_call | solution.py:236
  28.1 2.0 %collective-permute-done.11.refs_2_ = bf16[128,256]{1,0:T(8,128)(2,1)S(1)} collective-permute-done((bf16[128,256]{1,0:T(8,128)(2,1)S(1)}, bf16[128,256]{1,0:T(8,128)(2,1)S(1)}, u32[]{:S(2)}, u32[]{:S(2)}) %collective-permute-start.11) | collective-permute-done | bytes 65568 | tf_op jit(solution)/shard_map/ppermute | solution.py:30
  30.1 1.3 %collective-permute-done.13.refs_3_ = bf16[128,256]{1,0:T(8,128)(2,1)S(1)} collective-permute-done((bf16[128,256]{1,0:T(8,128)(2,1)S(1)}, bf16[128,256]{1,0:T(8,128)(2,1)S(1)}, u32[]{:S(2)}, u32[]{:S(2)}) %collective-permute-start.13) | collective-permute-done | bytes 65568 | tf_op jit(solution)/shard_map/ppermute | solution.py:30
  31.4 0.1 collective-permute-done.9.refs_1_
  31.5 0.7 %shard_map.55 = bf16[128,1024]{1,0:T(8,128)(2,1)} custom-call(bf16[128,256]{1,0:T(8,128)(2,1)S(1)} %shard_map.51.refs_0_, bf16[128,256]{1,0:T(8,128)(2,1)S(1)} %collective-permute-done.9.refs_1_, bf16[128,256]{1,0:T(8,128)(2,1)S(1)} %collective-permute-done.11.refs_2_, bf16[128,256]{1,0:T(8,128)(2,1)S(1)} %collective-permute-done.13.refs_3_), custom_call_target="tpu_custom_call" | custom-call | tf_op jit(solution)/shard_map/pallas_call | solution.py:256
  (8 shorter events, 0.1 us)
Async XLA Ops:
  1.2 16.4 %collective-permute-start.3 = (bf16[128,512]{1,0:T(8,128)(2,1)S(1)}, bf16[128,512]{1,0:T(8,128)(2,1)S(1)}, u32[]{:S(2)}, u32[]{:S(2)}) collective-permute-start(bf16[128,512]{1,0:T(8,128)(2,1)S(1)} %get-tuple-element.28), channel_id=1, source_target_pairs={{0,24},{4,28},{8,16},{12,20},{16,8},{20,12},{24,0},{28,4},{1,25},{... | collective-permute-start | bytes 393224 | tf_op jit(solution)/shard_map/ppermute | solution.py:30
  6.3 12.7 %collective-permute-start.4 = (bf16[128,512]{1,0:T(8,128)(2,1)S(1)}, bf16[128,512]{1,0:T(8,128)(2,1)S(1)}, u32[]{:S(2)}, u32[]{:S(2)}) collective-permute-start(bf16[128,512]{1,0:T(8,128)(2,1)S(1)} %get-tuple-element.29), channel_id=1, source_target_pairs={{0,16},{4,20},{8,24},{12,28},{16,0},{20,4},{24,8},{28,12},{1,17},{... | collective-permute-start | bytes 393224 | tf_op jit(solution)/shard_map/ppermute | solution.py:30
  6.3 4.3 %collective-permute-start = (bf16[32,1024]{1,0:T(8,128)(2,1)S(1)}, bf16[32,1024]{1,0:T(8,128)(2,1)S(1)}, u32[]{:S(2)}, u32[]{:S(2)}) collective-permute-start(bf16[32,1024]{1,0:T(8,128)(2,1)S(1)} %get-tuple-element.22), channel_id=1, source_target_pairs={{0,1},{1,0},{2,3},{3,2},{4,5},{5,4},{6,7},{7,6},{8,9},{9,8},{10,11... | collective-permute-start | bytes 196616 | tf_op jit(solution)/shard_map/ppermute | solution.py:30
  7.8 5.0 %collective-permute-start.1 = (bf16[32,1024]{1,0:T(8,128)(2,1)S(1)}, bf16[32,1024]{1,0:T(8,128)(2,1)S(1)}, u32[]{:S(2)}, u32[]{:S(2)}) collective-permute-start(bf16[32,1024]{1,0:T(8,128)(2,1)S(1)} %get-tuple-element.25), channel_id=1, source_target_pairs={{0,2},{1,3},{2,0},{3,1},{4,6},{5,7},{6,4},{7,5},{8,10},{9,11},{10,... | collective-permute-start | bytes 196616 | tf_op jit(solution)/shard_map/ppermute | solution.py:30
  9.3 1.9 %copy-start = (s32[8]{0:T(128)S(1)}, s32[8]{0:T(128)}, u32[]{:S(2)}) copy-start(s32[8]{0:T(128)} %order_ref.1) | copy-start | bytes 100
  9.3 5.2 %collective-permute-start.2 = (bf16[32,1024]{1,0:T(8,128)(2,1)S(1)}, bf16[32,1024]{1,0:T(8,128)(2,1)S(1)}, u32[]{:S(2)}, u32[]{:S(2)}) collective-permute-start(bf16[32,1024]{1,0:T(8,128)(2,1)S(1)} %get-tuple-element.26), channel_id=1, source_target_pairs={{0,3},{1,2},{2,1},{3,0},{4,7},{5,6},{6,5},{7,4},{8,11},{9,10},{10,... | collective-permute-start | bytes 196616 | tf_op jit(solution)/shard_map/ppermute | solution.py:30
  10.6 8.9 %collective-permute-start.6 = (bf16[128,512]{1,0:T(8,128)(2,1)S(1)}, bf16[128,512]{1,0:T(8,128)(2,1)S(1)}, u32[]{:S(2)}, u32[]{:S(2)}) collective-permute-start(bf16[128,512]{1,0:T(8,128)(2,1)S(1)} %get-tuple-element.31), channel_id=1, source_target_pairs={{0,8},{4,12},{8,0},{12,4},{16,24},{20,28},{24,16},{28,20},{1,9},{5... | collective-permute-start | bytes 393224 | tf_op jit(solution)/shard_map/ppermute | solution.py:30
  14.5 7.0 %collective-permute-start.8 = (bf16[128,256]{1,0:T(8,128)(2,1)S(1)}, bf16[128,256]{1,0:T(8,128)(2,1)S(1)}, u32[]{:S(2)}, u32[]{:S(2)}) collective-permute-start(bf16[128,256]{1,0:T(8,128)(2,1)S(1)} %get-tuple-element.32), channel_id=1, source_target_pairs={{0,8},{4,12},{8,0},{12,4},{16,24},{20,28},{24,16},{28,20},{1,9},{5... | collective-permute-start | bytes 196616 | tf_op jit(solution)/shard_map/ppermute | solution.py:30
  15.4 7.3 %collective-permute-start.10 = (bf16[128,256]{1,0:T(8,128)(2,1)S(1)}, bf16[128,256]{1,0:T(8,128)(2,1)S(1)}, u32[]{:S(2)}, u32[]{:S(2)}) collective-permute-start(bf16[128,256]{1,0:T(8,128)(2,1)S(1)} %get-tuple-element.37), channel_id=1, source_target_pairs={{0,16},{4,20},{8,24},{12,28},{16,0},{20,4},{24,8},{28,12},{1,17},{... | collective-permute-start | bytes 196616 | tf_op jit(solution)/shard_map/ppermute | solution.py:30
  17.6 6.7 %collective-permute-start.12 = (bf16[128,256]{1,0:T(8,128)(2,1)S(1)}, bf16[128,256]{1,0:T(8,128)(2,1)S(1)}, u32[]{:S(2)}, u32[]{:S(2)}) collective-permute-start(bf16[128,256]{1,0:T(8,128)(2,1)S(1)} %get-tuple-element.38), channel_id=1, source_target_pairs={{0,24},{4,28},{8,16},{12,20},{16,8},{20,12},{24,0},{28,4},{1,25},{... | collective-permute-start | bytes 196616 | tf_op jit(solution)/shard_map/ppermute | solution.py:30
  19.0 3.1 %collective-permute-start.5 = (bf16[3,128,512]{2,1,0:T(8,128)(2,1)S(1)}, bf16[3,128,512]{2,1,0:T(8,128)(2,1)S(1)}, u32[]{:S(2)}, u32[]{:S(2)}) collective-permute-start(bf16[3,128,512]{2,1,0:T(8,128)(2,1)S(1)} %shard_map.49), channel_id=1, source_target_pairs={{0,4},{4,0},{8,12},{12,8},{16,20},{20,16},{24,28},{28,24},{1,5},{5... | collective-permute-start | bytes 1179656 | tf_op jit(solution)/shard_map/ppermute | solution.py:30
  19.5 2.7 %collective-permute-start.7 = (bf16[128,512]{1,0:T(8,128)(2,1)S(1)}, bf16[128,512]{1,0:T(8,128)(2,1)S(1)}, u32[]{:S(2)}, u32[]{:S(2)}) collective-permute-start(bf16[128,512]{1,0:T(8,128)(2,1)S(1)} %collective-permute-done.6.rest_3_.rest_2_), channel_id=1, source_target_pairs={{0,4},{4,0},{8,12},{12,8},{16,20},{20,16},{24,28},{28,24},{1,5},{5... | collective-permute-start | bytes 393224 | tf_op jit(solution)/shard_map/ppermute | solution.py:30
  23.3 6.8 %collective-permute-start.11 = (bf16[128,256]{1,0:T(8,128)(2,1)S(1)}, bf16[128,256]{1,0:T(8,128)(2,1)S(1)}, u32[]{:S(2)}, u32[]{:S(2)}) collective-permute-start(bf16[128,256]{1,0:T(8,128)(2,1)S(1)} %shard_map.53), channel_id=1, source_target_pairs={{0,16},{4,20},{8,24},{12,28},{16,0},{20,4},{24,8},{28,12},{1,17},{... | collective-permute-start | bytes 196616 | tf_op jit(solution)/shard_map/ppermute | solution.py:30
  24.9 6.5 %collective-permute-start.13 = (bf16[128,256]{1,0:T(8,128)(2,1)S(1)}, bf16[128,256]{1,0:T(8,128)(2,1)S(1)}, u32[]{:S(2)}, u32[]{:S(2)}) collective-permute-start(bf16[128,256]{1,0:T(8,128)(2,1)S(1)} %shard_map.54), channel_id=1, source_target_pairs={{0,24},{4,28},{8,16},{12,20},{16,8},{20,12},{24,0},{28,4},{1,25},{... | collective-permute-start | bytes 196616 | tf_op jit(solution)/shard_map/ppermute | solution.py:30
  26.4 5.1 %collective-permute-start.9 = (bf16[128,256]{1,0:T(8,128)(2,1)S(1)}, bf16[128,256]{1,0:T(8,128)(2,1)S(1)}, u32[]{:S(2)}, u32[]{:S(2)}) collective-permute-start(bf16[128,256]{1,0:T(8,128)(2,1)S(1)} %shard_map.52.rest_7_), channel_id=1, source_target_pairs={{0,8},{4,12},{8,0},{12,4},{16,24},{20,28},{24,16},{28,20},{1,9},{5... | collective-permute-start | bytes 196616 | tf_op jit(solution)/shard_map/ppermute | solution.py:30

commit v7 on v6

--- a/solution.py
+++ b/solution.py
@@ -45,8 +45,8 @@
 
 def copy_all(pairs, sem):
     copies = [pltpu.make_async_copy(one, other, sem.at[i]) for i, (one, other) in enumerate(pairs)]
-    for one in copies:
-        one.start()
+    for at, one in enumerate(copies):
+        one.start(priority=at % 2)
     return copies
 
 

time: 32.5 us -> 32.5 us (level)
  no operation moved by 1% of the time
where the time goes in v7:
time: 32.5 us; the launch traced here: 32.2 us
  starting transfers between devices  17.5 us (54%)
  waiting for transfers between devices  8.28 us (25%)
  Pallas kernels  6.36 us (20%)
    ppermute x14, starting transfers between devices, swapped(): return lax.ppermute(block, axis, route)  17.5 us
    ppermute x14, waiting for transfers between devices, swapped(): return lax.ppermute(block, axis, route)  8.28 us
    pallas_call x4, Pallas kernels, attend(): pl.pallas_call(functools.partial(attend_kernel, turns, len(q), bool(near)...  2.27 us
    pallas_call x1, Pallas kernels, measure(): pl.pallas_call(functools.partial(measure_kernel, turns, chips), out_shape...  1.48 us
    pallas_call x1, Pallas kernels, split(): pl.pallas_call(functools.partial(split_kernel, turns), out_shape=outs, in...  1.18 us
    pallas_call x1, Pallas kernels, join(): pl.pallas_call(functools.partial(join_kernel, chips), out_shape=jax.Shape...  0.74 us
  transfers between devices with their start and end apart: 14, of which 8 were waited for; matrix products, arithmetic and copies ran while one was open for 0% of the time, Pallas kernels for 14%

profile of v7, /device:TPU:0, one launch (start us, length us, event | category | flops | bytes accessed | tf_op | source)
XLA Modules:
  0.0 32.2 jit_solution(413570490582964403)
XLA Ops:
  0.0 1.2 %shard_map.46 = (bf16[128,512]{1,0:T(8,128)(2,1)S(1)}, bf16[128,512]{1,0:T(8,128)(2,1)S(1)}, bf16[128,512]{1,0:T(8,128)(2,1)S(1)}, bf16[32,1024]{1,0:T(8,128)(2,...) custom-call(bf16[32,4096]{1,0:T(8,128)(2,1)} %q_ref.3, bf16[128,1024]{1,0:T(8,128)(2,1)} %k_ref.3, ...), custom_call_target="tpu_custom_call" | custom-call | tf_op jit(solution)/shard_map/pallas_call | solution.py:78
  1.2 5.1 %collective-permute-start.3 = (bf16[128,512]{1,0:T(8,128)(2,1)S(1)}, bf16[128,512]{1,0:T(8,128)(2,1)S(1)}, u32[]{:S(2)}, u32[]{:S(2)}) collective-permute-start(bf16[128,512]{1,0:T(8,128)(2,1)S(1)} %get-tuple-element.28), channel_id=1, source_target_pairs={{0,24},{4,28},{8,16},{12,20},{16,8},{20,12},{24,0},{28,4},{1,25},{... | collective-permute-start | bytes 393224 | tf_op jit(solution)/shard_map/ppermute | solution.py:30
  6.3 1.5 %collective-permute-start = (bf16[32,1024]{1,0:T(8,128)(2,1)S(1)}, bf16[32,1024]{1,0:T(8,128)(2,1)S(1)}, u32[]{:S(2)}, u32[]{:S(2)}) collective-permute-start(bf16[32,1024]{1,0:T(8,128)(2,1)S(1)} %get-tuple-element.22), channel_id=1, source_target_pairs={{0,1},{1,0},{2,3},{3,2},{4,5},{5,4},{6,7},{7,6},{8,9},{9,8},{10,11... | collective-permute-start | bytes 196616 | tf_op jit(solution)/shard_map/ppermute | solution.py:30
  7.8 1.5 %collective-permute-start.1 = (bf16[32,1024]{1,0:T(8,128)(2,1)S(1)}, bf16[32,1024]{1,0:T(8,128)(2,1)S(1)}, u32[]{:S(2)}, u32[]{:S(2)}) collective-permute-start(bf16[32,1024]{1,0:T(8,128)(2,1)S(1)} %get-tuple-element.25), channel_id=1, source_target_pairs={{0,2},{1,3},{2,0},{3,1},{4,6},{5,7},{6,4},{7,5},{8,10},{9,11},{10,... | collective-permute-start | bytes 196616 | tf_op jit(solution)/shard_map/ppermute | solution.py:30
  9.3 0.5 %collective-permute-start.2 = (bf16[32,1024]{1,0:T(8,128)(2,1)S(1)}, bf16[32,1024]{1,0:T(8,128)(2,1)S(1)}, u32[]{:S(2)}, u32[]{:S(2)}) collective-permute-start(bf16[32,1024]{1,0:T(8,128)(2,1)S(1)} %get-tuple-element.26), channel_id=1, source_target_pairs={{0,3},{1,2},{2,1},{3,0},{4,7},{5,6},{6,5},{7,4},{8,11},{9,10},{10,... | collective-permute-start | bytes 196616 | tf_op jit(solution)/shard_map/ppermute | solution.py:30
  9.8 0.8 %collective-permute-done._.refs_1_ = bf16[32,1024]{1,0:T(8,128)(2,1)S(1)} collective-permute-done((bf16[32,1024]{1,0:T(8,128)(2,1)S(1)}, bf16[32,1024]{1,0:T(8,128)(2,1)S(1)}, u32[]{:S(2)}, u32[]{:S(2)}) %collective-permute-start) | collective-permute-done | bytes 65568 | tf_op jit(solution)/shard_map/ppermute | solution.py:30
  10.6 0.6 %collective-permute-start.6 = (bf16[128,512]{1,0:T(8,128)(2,1)S(1)}, bf16[128,512]{1,0:T(8,128)(2,1)S(1)}, u32[]{:S(2)}, u32[]{:S(2)}) collective-permute-start(bf16[128,512]{1,0:T(8,128)(2,1)S(1)} %get-tuple-element.31), channel_id=1, source_target_pairs={{0,8},{4,12},{8,0},{12,4},{16,24},{20,28},{24,16},{28,20},{1,9},{5... | collective-permute-start | bytes 393224 | tf_op jit(solution)/shard_map/ppermute | solution.py:30
  11.2 1.5 %shard_map.47 = (bf16[128,512]{1,0:T(8,128)(2,1)S(1)}, bf16[32,1024]{1,0:T(8,128)(2,1)S(1)}, s32[4,8,1024]{2,1,0:T(8,128)S(1)}) custom-call(s32[8]{0:T(128)S(1)} %copy-done, bf16[32,4096]{1,0:T(8,128)(2,1)} %q_ref.3, bf16[128,1024]{1,0:T(8,128)(2,1)} %k_ref.3, bf16[128,1024]{1,0:T(8,128)(2,1)} %v_ref.3, bf16[32,1024]{1,0:T(8,128)(2,1)S(1)} %collective-permute-done._.refs_1_), custom_call_target="tpu_custom_call" | custom-call | tf_op jit(solution)/shard_map/pallas_call | solution.py:119
  12.7 0.1 collective-permute-done.1.refs_2_
  12.8 1.7 %collective-permute-done.2.refs_3_ = bf16[32,1024]{1,0:T(8,128)(2,1)S(1)} collective-permute-done((bf16[32,1024]{1,0:T(8,128)(2,1)S(1)}, bf16[32,1024]{1,0:T(8,128)(2,1)S(1)}, u32[]{:S(2)}, u32[]{:S(2)}) %collective-permute-start.2) | collective-permute-done | bytes 65568 | tf_op jit(solution)/shard_map/ppermute | solution.py:30
  14.5 0.8 %collective-permute-start.8 = (bf16[128,256]{1,0:T(8,128)(2,1)S(1)}, bf16[128,256]{1,0:T(8,128)(2,1)S(1)}, u32[]{:S(2)}, u32[]{:S(2)}) collective-permute-start(bf16[128,256]{1,0:T(8,128)(2,1)S(1)} %get-tuple-element.32), channel_id=1, source_target_pairs={{0,8},{4,12},{8,0},{12,4},{16,24},{20,28},{24,16},{28,20},{1,9},{5... | collective-permute-start | bytes 196616 | tf_op jit(solution)/shard_map/ppermute | solution.py:30
  15.4 2.2 %collective-permute-start.10 = (bf16[128,256]{1,0:T(8,128)(2,1)S(1)}, bf16[128,256]{1,0:T(8,128)(2,1)S(1)}, u32[]{:S(2)}, u32[]{:S(2)}) collective-permute-start(bf16[128,256]{1,0:T(8,128)(2,1)S(1)} %get-tuple-element.37), channel_id=1, source_target_pairs={{0,16},{4,20},{8,24},{12,28},{16,0},{20,4},{24,8},{28,12},{1,17},{... | collective-permute-start | bytes 196616 | tf_op jit(solution)/shard_map/ppermute | solution.py:30
  17.6 1.4 %collective-permute-start.12 = (bf16[128,256]{1,0:T(8,128)(2,1)S(1)}, bf16[128,256]{1,0:T(8,128)(2,1)S(1)}, u32[]{:S(2)}, u32[]{:S(2)}) collective-permute-start(bf16[128,256]{1,0:T(8,128)(2,1)S(1)} %get-tuple-element.38), channel_id=1, source_target_pairs={{0,24},{4,28},{8,16},{12,20},{16,8},{20,12},{24,0},{28,4},{1,25},{... | collective-permute-start | bytes 196616 | tf_op jit(solution)/shard_map/ppermute | solution.py:30
  19.0 0.0 collective-permute-done.4.refs_1_.rest_4_.rest_3_
  19.0 0.1 collective-permute-start.5
  19.1 0.4 %collective-permute-done.6.rest_3_.rest_2_ = bf16[128,512]{1,0:T(8,128)(2,1)S(1)} collective-permute-done((bf16[128,512]{1,0:T(8,128)(2,1)S(1)}, bf16[128,512]{1,0:T(8,128)(2,1)S(1)}, u32[]{:S(2)}, u32[]{:S(2)}) %collective-permute-start.6) | collective-permute-done | bytes 131104 | tf_op jit(solution)/shard_map/ppermute | solution.py:30
  19.5 0.1 collective-permute-start.7
  19.6 1.9 %collective-permute-done.8.rest_1_.rest_0_ = bf16[128,256]{1,0:T(8,128)(2,1)S(1)} collective-permute-done((bf16[128,256]{1,0:T(8,128)(2,1)S(1)}, bf16[128,256]{1,0:T(8,128)(2,1)S(1)}, u32[]{:S(2)}, u32[]{:S(2)}) %collective-permute-start.8) | collective-permute-done | bytes 65568 | tf_op jit(solution)/shard_map/ppermute | solution.py:30
  21.5 0.6 %shard_map.50 = (f32[128,256]{1,0:T(8,128)S(1)}, f32[128,512]{1,0:T(8,128)S(1)}, f32[128,256]{1,0:T(8,128)S(1)}, f32[128,512]{1,0:T(8,128)S(1)}) custom-call(s32[4,8,1024]{2,1,0:T(8,128)S(1)} %get-tuple-element.23.refs_4_.rel_ref, bf16[128,256]{1,0:T(8,128)(2,1)S(1)} %get-tuple-element.27.rest_0_, ...), custom_call_target="tpu_custom_call" | custom-call | flops 60000002048 | tf_op jit(solution)/shard_map/pallas_call | solution.py:222
  22.2 0.0 collective-permute-done.5.rest_1_.rest_5_
  22.2 0.5 %shard_map.52.rest_7_ = bf16[128,256]{1,0:T(8,128)(2,1)S(1)} custom-call(s32[4,8,1024]{2,1,0:T(8,128)S(1)} %get-tuple-element.23.refs_4_.rel_ref, bf16[128,256]{1,0:T(8,128)(2,1)S(1)} %collective-permute-done.8.rest_1_.rest_0_, bf16[3,128,512]{2,1,0:T(8,128)(2,1)S(1)} %collective-permute-done.5.rest_1_.rest_5_, ...), custom_call_target="tpu_custom_call" | custom-call | tf_op jit(solution)/shard_map/pallas_call | solution.py:236
  22.7 0.0 collective-permute-done.10.rest_0_
  22.7 0.6 %shard_map.53 = bf16[128,256]{1,0:T(8,128)(2,1)S(1)} custom-call(s32[4,8,1024]{2,1,0:T(8,128)S(1)} %get-tuple-element.23.refs_4_.rel_ref, bf16[128,256]{1,0:T(8,128)(2,1)S(1)} %collective-permute-done.10.rest_0_, bf16[128,512]{1,0:T(8,128)(2,1)S(1)} %get-tuple-element.30.refs_2_.rest_2_.rest_1_, bf16[128,512]{1,0:T(8,128)(2,1)S(1)} %collective-permute-done.6.rest_3_.rest_2_, ...), custom_call_target="tpu_custom_call" | custom-call | tf_op jit(solution)/shard_map/pallas_call | solution.py:236
  23.3 0.9 %collective-permute-start.11 = (bf16[128,256]{1,0:T(8,128)(2,1)S(1)}, bf16[128,256]{1,0:T(8,128)(2,1)S(1)}, u32[]{:S(2)}, u32[]{:S(2)}) collective-permute-start(bf16[128,256]{1,0:T(8,128)(2,1)S(1)} %shard_map.53), channel_id=1, source_target_pairs={{0,16},{4,20},{8,24},{12,28},{16,0},{20,4},{24,8},{28,12},{1,17},{... | collective-permute-start | bytes 196616 | tf_op jit(solution)/shard_map/ppermute | solution.py:30
  24.2 0.6 %shard_map.54 = bf16[128,256]{1,0:T(8,128)(2,1)S(1)} custom-call(s32[4,8,1024]{2,1,0:T(8,128)S(1)} %get-tuple-element.23.refs_4_.rel_ref, bf16[128,256]{1,0:T(8,128)(2,1)S(1)} %collective-permute-done.12.rest_0_, bf16[128,512]{1,0:T(8,128)(2,1)S(1)} %get-tuple-element.30.refs_2_.rest_2_.rest_1_, bf16[128,512]{1,0:T(8,128)(2,1)S(1)} %collective-permute-done.6.rest_3_.rest_2_, ...), custom_call_target="tpu_custom_call" | custom-call | tf_op jit(solution)/shard_map/pallas_call | solution.py:236
  24.9 1.5 %collective-permute-start.13 = (bf16[128,256]{1,0:T(8,128)(2,1)S(1)}, bf16[128,256]{1,0:T(8,128)(2,1)S(1)}, u32[]{:S(2)}, u32[]{:S(2)}) collective-permute-start(bf16[128,256]{1,0:T(8,128)(2,1)S(1)} %shard_map.54), channel_id=1, source_target_pairs={{0,24},{4,28},{8,16},{12,20},{16,8},{20,12},{24,0},{28,4},{1,25},{... | collective-permute-start | bytes 196616 | tf_op jit(solution)/shard_map/ppermute | solution.py:30
  26.4 1.2 %collective-permute-start.9 = (bf16[128,256]{1,0:T(8,128)(2,1)S(1)}, bf16[128,256]{1,0:T(8,128)(2,1)S(1)}, u32[]{:S(2)}, u32[]{:S(2)}) collective-permute-start(bf16[128,256]{1,0:T(8,128)(2,1)S(1)} %shard_map.52.rest_7_), channel_id=1, source_target_pairs={{0,8},{4,12},{8,0},{12,4},{16,24},{20,28},{24,16},{28,20},{1,9},{5... | collective-permute-start | bytes 196616 | tf_op jit(solution)/shard_map/ppermute | solution.py:30
  27.6 0.5 %shard_map.51.refs_0_ = bf16[128,256]{1,0:T(8,128)(2,1)S(1)} custom-call(s32[4,8,1024]{2,1,0:T(8,128)S(1)} %get-tuple-element.23.refs_4_.rel_ref, bf16[128,256]{1,0:T(8,128)(2,1)S(1)} %get-tuple-element.27.rest_0_, bf16[3,128,512]{2,1,0:T(8,128)(2,1)S(1)} %collective-permute-done.5.rest_1_.rest_5_, ...), custom_call_target="tpu_custom_call" | custom-call | tf_op jit(solution)/shard_map/pallas_call | solution.py:236
  28.1 2.0 %collective-permute-done.11.refs_2_ = bf16[128,256]{1,0:T(8,128)(2,1)S(1)} collective-permute-done((bf16[128,256]{1,0:T(8,128)(2,1)S(1)}, bf16[128,256]{1,0:T(8,128)(2,1)S(1)}, u32[]{:S(2)}, u32[]{:S(2)}) %collective-permute-start.11) | collective-permute-done | bytes 65568 | tf_op jit(solution)/shard_map/ppermute | solution.py:30
  30.1 1.3 %collective-permute-done.13.refs_3_ = bf16[128,256]{1,0:T(8,128)(2,1)S(1)} collective-permute-done((bf16[128,256]{1,0:T(8,128)(2,1)S(1)}, bf16[128,256]{1,0:T(8,128)(2,1)S(1)}, u32[]{:S(2)}, u32[]{:S(2)}) %collective-permute-start.13) | collective-permute-done | bytes 65568 | tf_op jit(solution)/shard_map/ppermute | solution.py:30
  31.4 0.1 collective-permute-done.9.refs_1_
  31.5 0.7 %shard_map.55 = bf16[128,1024]{1,0:T(8,128)(2,1)} custom-call(bf16[128,256]{1,0:T(8,128)(2,1)S(1)} %shard_map.51.refs_0_, bf16[128,256]{1,0:T(8,128)(2,1)S(1)} %collective-permute-done.9.refs_1_, bf16[128,256]{1,0:T(8,128)(2,1)S(1)} %collective-permute-done.11.refs_2_, bf16[128,256]{1,0:T(8,128)(2,1)S(1)} %collective-permute-done.13.refs_3_), custom_call_target="tpu_custom_call" | custom-call | tf_op jit(solution)/shard_map/pallas_call | solution.py:256
  (8 shorter events, 0.1 us)
Async XLA Ops:
  1.2 16.4 %collective-permute-start.3 = (bf16[128,512]{1,0:T(8,128)(2,1)S(1)}, bf16[128,512]{1,0:T(8,128)(2,1)S(1)}, u32[]{:S(2)}, u32[]{:S(2)}) collective-permute-start(bf16[128,512]{1,0:T(8,128)(2,1)S(1)} %get-tuple-element.28), channel_id=1, source_target_pairs={{0,24},{4,28},{8,16},{12,20},{16,8},{20,12},{24,0},{28,4},{1,25},{... | collective-permute-start | bytes 393224 | tf_op jit(solution)/shard_map/ppermute | solution.py:30
  6.3 12.7 %collective-permute-start.4 = (bf16[128,512]{1,0:T(8,128)(2,1)S(1)}, bf16[128,512]{1,0:T(8,128)(2,1)S(1)}, u32[]{:S(2)}, u32[]{:S(2)}) collective-permute-start(bf16[128,512]{1,0:T(8,128)(2,1)S(1)} %get-tuple-element.29), channel_id=1, source_target_pairs={{0,16},{4,20},{8,24},{12,28},{16,0},{20,4},{24,8},{28,12},{1,17},{... | collective-permute-start | bytes 393224 | tf_op jit(solution)/shard_map/ppermute | solution.py:30
  6.3 4.3 %collective-permute-start = (bf16[32,1024]{1,0:T(8,128)(2,1)S(1)}, bf16[32,1024]{1,0:T(8,128)(2,1)S(1)}, u32[]{:S(2)}, u32[]{:S(2)}) collective-permute-start(bf16[32,1024]{1,0:T(8,128)(2,1)S(1)} %get-tuple-element.22), channel_id=1, source_target_pairs={{0,1},{1,0},{2,3},{3,2},{4,5},{5,4},{6,7},{7,6},{8,9},{9,8},{10,11... | collective-permute-start | bytes 196616 | tf_op jit(solution)/shard_map/ppermute | solution.py:30
  7.8 5.0 %collective-permute-start.1 = (bf16[32,1024]{1,0:T(8,128)(2,1)S(1)}, bf16[32,1024]{1,0:T(8,128)(2,1)S(1)}, u32[]{:S(2)}, u32[]{:S(2)}) collective-permute-start(bf16[32,1024]{1,0:T(8,128)(2,1)S(1)} %get-tuple-element.25), channel_id=1, source_target_pairs={{0,2},{1,3},{2,0},{3,1},{4,6},{5,7},{6,4},{7,5},{8,10},{9,11},{10,... | collective-permute-start | bytes 196616 | tf_op jit(solution)/shard_map/ppermute | solution.py:30
  9.3 1.9 %copy-start = (s32[8]{0:T(128)S(1)}, s32[8]{0:T(128)}, u32[]{:S(2)}) copy-start(s32[8]{0:T(128)} %order_ref.1) | copy-start | bytes 100
  9.3 5.2 %collective-permute-start.2 = (bf16[32,1024]{1,0:T(8,128)(2,1)S(1)}, bf16[32,1024]{1,0:T(8,128)(2,1)S(1)}, u32[]{:S(2)}, u32[]{:S(2)}) collective-permute-start(bf16[32,1024]{1,0:T(8,128)(2,1)S(1)} %get-tuple-element.26), channel_id=1, source_target_pairs={{0,3},{1,2},{2,1},{3,0},{4,7},{5,6},{6,5},{7,4},{8,11},{9,10},{10,... | collective-permute-start | bytes 196616 | tf_op jit(solution)/shard_map/ppermute | solution.py:30
  10.6 8.9 %collective-permute-start.6 = (bf16[128,512]{1,0:T(8,128)(2,1)S(1)}, bf16[128,512]{1,0:T(8,128)(2,1)S(1)}, u32[]{:S(2)}, u32[]{:S(2)}) collective-permute-start(bf16[128,512]{1,0:T(8,128)(2,1)S(1)} %get-tuple-element.31), channel_id=1, source_target_pairs={{0,8},{4,12},{8,0},{12,4},{16,24},{20,28},{24,16},{28,20},{1,9},{5... | collective-permute-start | bytes 393224 | tf_op jit(solution)/shard_map/ppermute | solution.py:30
  14.5 7.0 %collective-permute-start.8 = (bf16[128,256]{1,0:T(8,128)(2,1)S(1)}, bf16[128,256]{1,0:T(8,128)(2,1)S(1)}, u32[]{:S(2)}, u32[]{:S(2)}) collective-permute-start(bf16[128,256]{1,0:T(8,128)(2,1)S(1)} %get-tuple-element.32), channel_id=1, source_target_pairs={{0,8},{4,12},{8,0},{12,4},{16,24},{20,28},{24,16},{28,20},{1,9},{5... | collective-permute-start | bytes 196616 | tf_op jit(solution)/shard_map/ppermute | solution.py:30
  15.4 7.3 %collective-permute-start.10 = (bf16[128,256]{1,0:T(8,128)(2,1)S(1)}, bf16[128,256]{1,0:T(8,128)(2,1)S(1)}, u32[]{:S(2)}, u32[]{:S(2)}) collective-permute-start(bf16[128,256]{1,0:T(8,128)(2,1)S(1)} %get-tuple-element.37), channel_id=1, source_target_pairs={{0,16},{4,20},{8,24},{12,28},{16,0},{20,4},{24,8},{28,12},{1,17},{... | collective-permute-start | bytes 196616 | tf_op jit(solution)/shard_map/ppermute | solution.py:30
  17.6 6.7 %collective-permute-start.12 = (bf16[128,256]{1,0:T(8,128)(2,1)S(1)}, bf16[128,256]{1,0:T(8,128)(2,1)S(1)}, u32[]{:S(2)}, u32[]{:S(2)}) collective-permute-start(bf16[128,256]{1,0:T(8,128)(2,1)S(1)} %get-tuple-element.38), channel_id=1, source_target_pairs={{0,24},{4,28},{8,16},{12,20},{16,8},{20,12},{24,0},{28,4},{1,25},{... | collective-permute-start | bytes 196616 | tf_op jit(solution)/shard_map/ppermute | solution.py:30
  19.0 3.1 %collective-permute-start.5 = (bf16[3,128,512]{2,1,0:T(8,128)(2,1)S(1)}, bf16[3,128,512]{2,1,0:T(8,128)(2,1)S(1)}, u32[]{:S(2)}, u32[]{:S(2)}) collective-permute-start(bf16[3,128,512]{2,1,0:T(8,128)(2,1)S(1)} %shard_map.49), channel_id=1, source_target_pairs={{0,4},{4,0},{8,12},{12,8},{16,20},{20,16},{24,28},{28,24},{1,5},{5... | collective-permute-start | bytes 1179656 | tf_op jit(solution)/shard_map/ppermute | solution.py:30
  19.5 2.7 %collective-permute-start.7 = (bf16[128,512]{1,0:T(8,128)(2,1)S(1)}, bf16[128,512]{1,0:T(8,128)(2,1)S(1)}, u32[]{:S(2)}, u32[]{:S(2)}) collective-permute-start(bf16[128,512]{1,0:T(8,128)(2,1)S(1)} %collective-permute-done.6.rest_3_.rest_2_), channel_id=1, source_target_pairs={{0,4},{4,0},{8,12},{12,8},{16,20},{20,16},{24,28},{28,24},{1,5},{5... | collective-permute-start | bytes 393224 | tf_op jit(solution)/shard_map/ppermute | solution.py:30
  23.3 6.8 %collective-permute-start.11 = (bf16[128,256]{1,0:T(8,128)(2,1)S(1)}, bf16[128,256]{1,0:T(8,128)(2,1)S(1)}, u32[]{:S(2)}, u32[]{:S(2)}) collective-permute-start(bf16[128,256]{1,0:T(8,128)(2,1)S(1)} %shard_map.53), channel_id=1, source_target_pairs={{0,16},{4,20},{8,24},{12,28},{16,0},{20,4},{24,8},{28,12},{1,17},{... | collective-permute-start | bytes 196616 | tf_op jit(solution)/shard_map/ppermute | solution.py:30
  24.9 6.5 %collective-permute-start.13 = (bf16[128,256]{1,0:T(8,128)(2,1)S(1)}, bf16[128,256]{1,0:T(8,128)(2,1)S(1)}, u32[]{:S(2)}, u32[]{:S(2)}) collective-permute-start(bf16[128,256]{1,0:T(8,128)(2,1)S(1)} %shard_map.54), channel_id=1, source_target_pairs={{0,24},{4,28},{8,16},{12,20},{16,8},{20,12},{24,0},{28,4},{1,25},{... | collective-permute-start | bytes 196616 | tf_op jit(solution)/shard_map/ppermute | solution.py:30
  26.4 5.1 %collective-permute-start.9 = (bf16[128,256]{1,0:T(8,128)(2,1)S(1)}, bf16[128,256]{1,0:T(8,128)(2,1)S(1)}, u32[]{:S(2)}, u32[]{:S(2)}) collective-permute-start(bf16[128,256]{1,0:T(8,128)(2,1)S(1)} %shard_map.52.rest_7_), channel_id=1, source_target_pairs={{0,8},{4,12},{8,0},{12,4},{16,24},{20,28},{24,16},{28,20},{1,9},{5... | collective-permute-start | bytes 196616 | tf_op jit(solution)/shard_map/ppermute | solution.py:30
